TPU v7x, 32 devices: a whole 2x2x4 slice. The times are simulated.
32 devices in a mesh: ctx: 4 (over y, x), seq: 8 (over z, core).
Axes of the slice: x: 2, y: 2, z: 4, core: 2. Of those that a mesh axis runs over, the one named last changes fastest.
Arguments:
- hidden_in: bfloat16 [8192, 1024], P(('ctx', 'seq')), may hold values from -6 to 6
- cotangent: bfloat16 [8192, 1024], P(('ctx', 'seq')), may hold values from -6 to 6
- norm_gain: bfloat16 [2, 1024], P(None, ('ctx', 'seq')), may hold values from 0.5 to 1.5
- in_weight: bfloat16 [2, 1024, 4096], P(None, None, ('ctx', 'seq')), may hold values from -0.1875 to 0.1875
- conv_weight: bfloat16 [2, 4, 2048], P(None, None, ('ctx', 'seq')), may hold values from -3 to 3
- conv_bias: bfloat16 [2, 2048], P(None, ('ctx', 'seq')), may hold values from -3 to 3
- x_weight: bfloat16 [2, 2048, 96], P(None, ('ctx', 'seq')), may hold values from -0.125 to 0.125
- dt_weight: bfloat16 [2, 64, 2048], P(None, None, ('ctx', 'seq')), may hold values from -0.75 to 0.75
- dt_bias: bfloat16 [2, 2048], P(None, ('ctx', 'seq')), may hold values from -4.5 to -1
- a_log: bfloat16 [2, 2048, 16], P(None, ('ctx', 'seq')), may hold values from -8 to 1
- skip_gain: bfloat16 [2, 2048], P(None, ('ctx', 'seq')), may hold values from 0.5 to 1.5
- out_weight: bfloat16 [2, 2048, 1024], P(None, None, ('ctx', 'seq')), may hold values from -0.125 to 0.125
Outputs:
- out_stream: bfloat16 [8192, 1024], P(('ctx', 'seq'))
- hidden_grad: float32 [8192, 1024], P(('ctx', 'seq'))
- norm_gain_grad: float32 [2, 1024], P(None, ('ctx', 'seq'))
- in_weight_grad: float32 [2, 1024, 4096], P(None, None, ('ctx', 'seq'))
- conv_weight_grad: float32 [2, 4, 2048], P(None, None, ('ctx', 'seq'))
- conv_bias_grad: float32 [2, 2048], P(None, ('ctx', 'seq'))
- x_weight_grad: float32 [2, 2048, 96], P(None, ('ctx', 'seq'))
- dt_weight_grad: float32 [2, 64, 2048], P(None, None, ('ctx', 'seq'))
- dt_bias_grad: float32 [2, 2048], P(None, ('ctx', 'seq'))
- a_log_grad: float32 [2, 2048, 16], P(None, ('ctx', 'seq'))
- skip_gain_grad: float32 [2, 2048], P(None, ('ctx', 'seq'))
- out_weight_grad: float32 [2, 2048, 1024], P(None, None, ('ctx', 'seq'))
All inputs are finite; a program needn't handle non-finite values.
Results may differ from a plain program's by a relative error of at most 0.015.
Values may be sent and summed in bfloat16 or wider, within the bound.
A program may use at most 640 MiB of HBM per device.

v0:
```python
import math

import jax
import jax.numpy as jnp
from jax import lax
from jax.sharding import PartitionSpec as P

EPS = 1e-05
HIGH = lax.Precision.HIGHEST


def from_behind(value, axis, steps):
    count = lax.axis_size(axis)
    initial, last = (max(0, -steps), min(count, count - steps))
    return lax.ppermute(value, axis, [(source, source + steps) for source in range(initial, last)])


def entering(part, axis, combine, identity):
    place = lax.axis_index(axis)
    gathered = jax.tree.map(lambda a: lax.all_gather(a, axis), part)
    state = jax.tree.map(lambda a, e: jnp.zeros_like(a) + jnp.asarray(e, a.dtype), part, identity)

    def one(turn, state):
        return combine(
            state, jax.tree.map(lambda a: lax.dynamic_index_in_dim(a, turn, 0, False), gathered)
        )

    return lax.fori_loop(0, place, one, state)


def carried_in(array, axis, combine, identity):
    size, position = (lax.axis_size(axis), lax.axis_index(axis))
    everything = jax.tree.map(
        lambda part, kind: lax.all_gather(part.astype(kind), axis),
        array,
        (jnp.bfloat16, jnp.bfloat16),
    )
    start = jax.tree.map(
        lambda part, zero: jnp.broadcast_to(jnp.asarray(zero, part.dtype), part.shape),
        array,
        identity,
    )

    def turn(k, before):
        at = size - 1 - k
        reached = at > position
        new = combine(
            before, jax.tree.map(lambda part, own: part[at].astype(own.dtype), everything, array)
        )
        return jax.tree.map(lambda a, b: jnp.where(reached, a, b), new, before)

    return lax.fori_loop(0, size, turn, start)


def combine(earlier, later):
    return (earlier[0] * later[0], later[0] * earlier[1] + later[1])


def rms_norm(stream, gain_vec):
    return stream * lax.rsqrt(jnp.mean(stream * stream, axis=1, keepdims=True) + EPS) * gain_vec


def causal_conv(padded, conv_w, conv_b):
    length = padded.shape[0] - conv_w.shape[0] + 1
    summed = conv_b[None, :] + conv_w[0][None, :] * padded[0:length]
    for offset in range(1, conv_w.shape[0]):
        summed = summed + conv_w[offset][None, :] * padded[offset : offset + length]
    return jax.nn.silu(summed)


def scan_states(conv_act, step_size, in_coeff, out_coeff, a_log_turned, start):
    decay_rate = -jnp.exp(a_log_turned)

    def row_step(state, pieces):
        act_row, step_row, in_row, out_row = pieces
        state = (
            jnp.exp(step_row[None, :] * decay_rate) * state
            + in_row[:, None] * (step_row * act_row)[None, :]
        )
        return (state, jnp.sum(out_row[:, None] * state, axis=0))

    final_state, outputs = lax.scan(
        row_step, start, (conv_act, step_size, in_coeff, out_coeff), unroll=16
    )
    return (outputs, final_state)


def decayed_sum(offsets, left_side, right_side, decay_rate):
    length = offsets.shape[0]
    blk_rows = math.gcd(length, 128)

    def block_step(summed, pieces):
        off_rows, left_rows, right_rows = pieces
        weights = jnp.exp(off_rows[:, None, :] * decay_rate[None])
        return (
            summed + jnp.einsum("tni,ti,tn->ni", weights, left_rows, right_rows, precision=HIGH),
            None,
        )

    shaped = tuple(
        (
            member.reshape(length // blk_rows, blk_rows, member.shape[1])
            for member in (offsets, left_side, right_side)
        )
    )
    summed, _ = lax.scan(block_step, jnp.zeros(decay_rate.shape, jnp.float32), shaped)
    return summed


def outer_sum(left_side, right_side):
    return lax.dot_general(
        left_side, right_side, (((0,), (0,)), ((), ())), preferred_element_type=jnp.float32
    )


def back_dot(grad_rows, weight):
    return lax.dot_general(
        grad_rows, weight, (((1,), (1,)), ((), ())), preferred_element_type=jnp.float32
    )


def forward_layer(stream, params):
    gain_vec, w_in, conv_w, conv_b, w_x, w_dt, b_dt, a_lg, skip_vec, w_out = params
    inner_width = w_dt.shape[1]
    rank_width = w_dt.shape[0]
    state_width = a_lg.shape[1]
    rim_width = conv_w.shape[0] - 1
    normed = rms_norm(stream, gain_vec.astype(jnp.float32))
    normed_low = normed.astype(jnp.bfloat16)
    projected = jnp.dot(normed_low, w_in, preferred_element_type=jnp.float32)
    conv_input = projected[:, :inner_width].astype(jnp.bfloat16)
    gate_branch = projected[:, inner_width:]
    edge_rows = from_behind(conv_input[-rim_width:], "seq", 1)
    padded = jnp.concatenate([edge_rows, conv_input], 0).astype(jnp.float32)
    conv_low = causal_conv(padded, conv_w.astype(jnp.float32), conv_b.astype(jnp.float32)).astype(
        jnp.bfloat16
    )
    conv_act = conv_low.astype(jnp.float32)
    small_proj = jnp.dot(conv_low, w_x, preferred_element_type=jnp.float32)
    step_low = small_proj[:, :rank_width].astype(jnp.bfloat16)
    in_coeff = small_proj[:, rank_width : rank_width + state_width]
    out_coeff = small_proj[:, rank_width + state_width :]
    step_pre = jnp.dot(step_low, w_dt, preferred_element_type=jnp.float32) + b_dt.astype(
        jnp.float32
    )
    step_size = jax.nn.softplus(step_pre)
    a_log_turned = a_lg.astype(jnp.float32).T
    decay_rate = -jnp.exp(a_log_turned)
    running = jnp.cumsum(step_size, axis=0)
    group_ends = decayed_sum(
        running[-1][None, :] - running, step_size * conv_act, in_coeff, decay_rate
    )
    through = jnp.exp(running[-1][None, :] * decay_rate)
    start = entering(
        (through, group_ends), "seq", combine, (jnp.ones_like(through), jnp.zeros_like(group_ends))
    )[1]
    scan_out, _ = scan_states(conv_act, step_size, in_coeff, out_coeff, a_log_turned, start)
    y_value = scan_out + skip_vec.astype(jnp.float32) * conv_act
    mixed = (y_value * jax.nn.silu(gate_branch)).astype(jnp.bfloat16)
    new_stream = stream + jnp.dot(mixed, w_out, preferred_element_type=jnp.float32)
    record = (
        stream,
        normed_low,
        gate_branch,
        padded,
        conv_low,
        conv_act,
        step_low,
        step_pre,
        step_size,
        in_coeff,
        out_coeff,
        running,
        through,
        start,
        y_value,
        mixed,
    )
    return (new_stream, record)


def backward_layer(stream_grad, params, record):
    gain_vec, w_in, conv_w, conv_b, w_x, w_dt, b_dt, a_lg, skip_vec, w_out = params
    (
        stream,
        normed_low,
        gate_branch,
        padded,
        conv_low,
        conv_act,
        step_low,
        step_pre,
        step_size,
        in_coeff,
        out_coeff,
        running,
        through,
        start,
        y_value,
        mixed,
    ) = record
    inner_width = w_dt.shape[1]
    rim_width = conv_w.shape[0] - 1
    a_log_turned = a_lg.astype(jnp.float32).T
    decay_rate = -jnp.exp(a_log_turned)
    skip32 = skip_vec.astype(jnp.float32)
    proj_grad = stream_grad.astype(jnp.bfloat16)
    g_out = outer_sum(mixed, proj_grad)
    mixed_grad = back_dot(proj_grad, w_out)
    gate_sigm = jax.nn.sigmoid(gate_branch)
    scan_grad = mixed_grad * gate_branch * gate_sigm
    gate_grad = mixed_grad * y_value * gate_sigm * (1.0 + gate_branch * (1.0 - gate_sigm))
    g_skip = jnp.sum(scan_grad * conv_act, axis=0)
    own_adjoint = decayed_sum(running, scan_grad, out_coeff, decay_rate)
    later_adjoint = carried_in(
        (through, own_adjoint),
        "seq",
        combine,
        (jnp.ones_like(through), jnp.zeros_like(own_adjoint)),
    )[1]
    _, pullback = jax.vjp(
        scan_states, conv_act, step_size, in_coeff, out_coeff, a_log_turned, start
    )
    act_grad, step_grad, in_grad, out_grad, g_alog_turned, _ = pullback((scan_grad, later_adjoint))
    g_alog = g_alog_turned.T
    act_grad = act_grad + skip32 * scan_grad
    pre_grad = step_grad * jax.nn.sigmoid(step_pre)
    g_bdt = jnp.sum(pre_grad, axis=0)
    pre_low = pre_grad.astype(jnp.bfloat16)
    g_dt = outer_sum(step_low, pre_low)
    small_grad = jnp.concatenate([back_dot(pre_low, w_dt), in_grad, out_grad], 1).astype(
        jnp.bfloat16
    )
    g_x = outer_sum(conv_low, small_grad)
    act_grad = act_grad + back_dot(small_grad, w_x)
    _, conv_pull = jax.vjp(
        causal_conv, padded, conv_w.astype(jnp.float32), conv_b.astype(jnp.float32)
    )
    pad_grad, g_conv, g_convb = conv_pull(act_grad)
    rim_grad = from_behind(pad_grad[:rim_width], "seq", -1)
    filler = jnp.zeros((pad_grad.shape[0] - 2 * rim_width, inner_width), jnp.float32)
    input_grad = pad_grad[rim_width:] + jnp.concatenate([filler, rim_grad], 0)
    proj_back = jnp.concatenate([input_grad, gate_grad], 1).astype(jnp.bfloat16)
    g_in = outer_sum(normed_low, proj_back)
    normed_grad = back_dot(proj_back, w_in)
    _, norm_pull = jax.vjp(rms_norm, stream, gain_vec.astype(jnp.float32))
    norm_back, g_gain = norm_pull(normed_grad)
    return (
        stream_grad + norm_back,
        (g_gain, g_in, g_conv, g_convb, g_x, g_dt, g_bdt, g_alog, g_skip, g_out),
    )


def on_device(
    hidden_in,
    cotangent,
    norm_gain,
    in_weight,
    conv_weight,
    conv_bias,
    x_weight,
    dt_weight,
    dt_bias,
    a_log,
    skip_gain,
    out_weight,
):
    layers = norm_gain.shape[0]
    stream = hidden_in.astype(jnp.float32)
    saved = []
    kept_params = []
    for layer_idx in range(layers):
        params = (
            lax.all_gather(norm_gain[layer_idx], ("ctx", "seq"), axis=0, tiled=True),
            lax.all_gather(in_weight[layer_idx], ("ctx", "seq"), axis=1, tiled=True),
            lax.all_gather(conv_weight[layer_idx], ("ctx", "seq"), axis=1, tiled=True),
            lax.all_gather(conv_bias[layer_idx], ("ctx", "seq"), axis=0, tiled=True),
            lax.all_gather(x_weight[layer_idx], ("ctx", "seq"), axis=0, tiled=True),
            lax.all_gather(dt_weight[layer_idx], ("ctx", "seq"), axis=1, tiled=True),
            lax.all_gather(dt_bias[layer_idx], ("ctx", "seq"), axis=0, tiled=True),
            lax.all_gather(a_log[layer_idx], ("ctx", "seq"), axis=0, tiled=True),
            lax.all_gather(skip_gain[layer_idx], ("ctx", "seq"), axis=0, tiled=True),
            lax.all_gather(out_weight[layer_idx], ("ctx", "seq"), axis=1, tiled=True),
        )
        stream, record = forward_layer(stream, params)
        saved.append(record)
        kept_params.append(None)
    stream_grad = cotangent.astype(jnp.float32)
    gradients = []
    for layer_idx in reversed(range(layers)):
        params = (
            lax.all_gather(norm_gain[layer_idx], ("ctx", "seq"), axis=0, tiled=True),
            lax.all_gather(in_weight[layer_idx], ("ctx", "seq"), axis=1, tiled=True),
            lax.all_gather(conv_weight[layer_idx], ("ctx", "seq"), axis=1, tiled=True),
            lax.all_gather(conv_bias[layer_idx], ("ctx", "seq"), axis=0, tiled=True),
            lax.all_gather(x_weight[layer_idx], ("ctx", "seq"), axis=0, tiled=True),
            lax.all_gather(dt_weight[layer_idx], ("ctx", "seq"), axis=1, tiled=True),
            lax.all_gather(dt_bias[layer_idx], ("ctx", "seq"), axis=0, tiled=True),
            lax.all_gather(a_log[layer_idx], ("ctx", "seq"), axis=0, tiled=True),
            lax.all_gather(skip_gain[layer_idx], ("ctx", "seq"), axis=0, tiled=True),
            lax.all_gather(out_weight[layer_idx], ("ctx", "seq"), axis=1, tiled=True),
        )
        stream_grad, layer_grads = backward_layer(stream_grad, params, saved[layer_idx])
        g_gain, g_in, g_conv, g_convb, g_x, g_dt, g_bdt, g_alog, g_skip, g_out = layer_grads
        reduced = (
            lax.psum_scatter(g_gain, ("ctx", "seq"), scatter_dimension=0, tiled=True),
            lax.psum_scatter(g_in, ("ctx", "seq"), scatter_dimension=1, tiled=True),
            lax.psum_scatter(g_conv, ("ctx", "seq"), scatter_dimension=1, tiled=True),
            lax.psum_scatter(g_convb, ("ctx", "seq"), scatter_dimension=0, tiled=True),
            lax.psum_scatter(g_x, ("ctx", "seq"), scatter_dimension=0, tiled=True),
            lax.psum_scatter(g_dt, ("ctx", "seq"), scatter_dimension=1, tiled=True),
            lax.psum_scatter(g_bdt, ("ctx", "seq"), scatter_dimension=0, tiled=True),
            lax.psum_scatter(g_alog, ("ctx", "seq"), scatter_dimension=0, tiled=True),
            lax.psum_scatter(g_skip, ("ctx", "seq"), scatter_dimension=0, tiled=True),
            lax.psum_scatter(g_out, ("ctx", "seq"), scatter_dimension=1, tiled=True),
        )
        gradients.insert(0, reduced)
    stacked = tuple(
        (
            jnp.stack([gradients[layer_idx][member] for layer_idx in range(layers)], 0)
            for member in range(10)
        )
    )
    return (stream.astype(jnp.bfloat16), stream_grad) + stacked


def solution(mesh):
    return jax.shard_map(
        on_device,
        mesh=mesh,
        in_specs=(
            P(("ctx", "seq"), None),
            P(("ctx", "seq"), None),
            P(None, ("ctx", "seq")),
            P(None, None, ("ctx", "seq")),
            P(None, None, ("ctx", "seq")),
            P(None, ("ctx", "seq")),
            P(None, ("ctx", "seq"), None),
            P(None, None, ("ctx", "seq")),
            P(None, ("ctx", "seq")),
            P(None, ("ctx", "seq"), None),
            P(None, ("ctx", "seq")),
            P(None, None, ("ctx", "seq")),
        ),
        out_specs=(
            P(("ctx", "seq"), None),
            P(("ctx", "seq"), None),
            P(None, ("ctx", "seq")),
            P(None, None, ("ctx", "seq")),
            P(None, None, ("ctx", "seq")),
            P(None, ("ctx", "seq")),
            P(None, ("ctx", "seq"), None),
            P(None, None, ("ctx", "seq")),
            P(None, ("ctx", "seq")),
            P(None, ("ctx", "seq"), None),
            P(None, ("ctx", "seq")),
            P(None, None, ("ctx", "seq")),
        ),
        check_vma=False,
    )
```

profile of v0, /device:TPU:0, one launch (start us, length us, event | category | flops | bytes accessed | tf_op | source)
XLA Modules:
  0.0 5482.1 jit_solution(14176136399591888786)
XLA Ops:
  13.9 43.1 all-reduce.35
  58.4 57.8 %all-gather.1 = bf16[1,4,2048]{1,0,2:T(2,128)(2,1)S(1)} all-gather(bf16[1,4,64]{1,0,2:T(2,128)(2,1)S(1)} %copy.188), channel_id=3, replica_groups=mesh['ctx'=4,'seq'=8] {'ctx','seq'}, dimensions={2}, use_global_device_ids=true | all-gather | bytes 16896 | tf_op jit(solution)/shard_map/all_gather | solution.py:276
  201.9 42.5 slice_reduce_fusion.7
  362.7 46.7 all-gather.13
  410.6 43.4 slice_reduce_fusion.3
  497.0 47.0 all-gather.17
  545.8 53.1 all-gather.19
  622.8 80.5 %while.223 = (s32[]{:T(128)}, f32[16,2048]{1,0:T(8,128)S(1)}, f32[16,16,2048]{2,1,0:T(8,128)}, f32[16,16,2048]{2,1,0:T(8,128)}, f32[16,2048]{1,0:T(8,128)S(1)}, ...) while((s32[]{:T(128)}, f32[16,2048]{1,0:T(8,128)S(1)}, ...), condition=%wide.region_24.25_spmd, body=%wide.region_7.24_spmd.sunk | while | flops 4718609 | bytes 3874577 | solution.py:82
  764.4 713.3 %while.227 = (s32[]{:T(128)}, f32[16,2048]{1,0:T(8,128)S(1)}, f32[16,16,1,2048]{3,2,1,0:T(1,128)}, f32[16,16,16,2048]{3,2,1,0:T(8,128)}, f32[16,16,16,2048]{3,2,...) while((s32[]{:T(128)}, f32[16,2048]{1,0:T(8,128)S(1)}, ...), condition=%wide.region_128.129_spmd, body=%wide.region_127.128_spmd.sunk | while | flops 3735566 | bytes 27579756 | solution.py:82
  1682.0 348.6 %while.226 = (s32[]{:T(128)}, f32[16,2048]{1,0:T(8,128)S(1)}, f32[16,16,1,2048]{3,2,1,0:T(1,128)}, f32[16,16,16,2048]{3,2,1,0:T(8,128)}, f32[16,16,16,2048]{3,2,...) while((s32[]{:T(128)}, f32[16,2048]{1,0:T(8,128)S(1)}, ...), condition=%wide.region_55.56_spmd, body=%wide.region_54.55_spmd.sunk | while | flops 3735566 | bytes 27606516 | solution.py:82
  2035.8 846.1 %while.232 = (s32[]{:T(128)}, f32[16,2048]{1,0:T(8,128)}, f32[16,2048]{1,0:T(8,128)S(1)}, f32[16,16,2048]{2,1,0:T(8,128)}, f32[16,16,2048]{2,1,0:T(8,128)}, /*in...) while((s32[]{:T(128)}, f32[16,2048]{1,0:T(8,128)}, ...), condition=%wide.region_121.122_spmd.clone, body=%wide.region_56.121_spmd.clone.sunk | while | flops 7994899 | bytes 19434076 | solution.py:82
  2889.0 161.2 %while.225 = (s32[]{:T(128)}, f32[16,2048]{1,0:T(8,128)S(1)}, f32[16,16,2048]{2,1,0:T(8,128)}, f32[16,16,2048]{2,1,0:T(8,128)}, f32[16,2048]{1,0:T(8,128)S(1)}, ...) while((s32[]{:T(128)}, f32[16,2048]{1,0:T(8,128)S(1)}, ...), condition=%wide.region_49.50_spmd, body=%wide.region_32.49_spmd.sunk | while | flops 4718609 | bytes 3874577 | solution.py:82
  3156.4 690.1 %while.235 = (s32[]{:T(128)}, f32[16,2048]{1,0:T(8,128)}, f32[16,2048]{1,0:T(8,128)S(1)}, f32[16,16,2048]{2,1,0:T(8,128)}, f32[16,16,2048]{2,1,0:T(8,128)}, /*in...) while((s32[]{:T(128)}, f32[16,2048]{1,0:T(8,128)}, ...), condition=%wide.region_194.195_spmd.clone, body=%wide.region_129.194_spmd.clone.sunk | while | flops 7994899 | bytes 27492428 | solution.py:82
  3918.1 42.3 all-reduce.34
  3998.5 132.0 %reduce-scatter.47.cloned.1.call-done = f32[64,16]{1,0:T(8,128)} async-done(((f32[2048,16]{1,0:T(8,128)}), f32[64,16]{1,0:T(8,128)}) %reduce-scatter.47.cloned.1.call-update) | async-done | bytes 4112
  4131.3 132.5 %reduce-scatter.45.cloned.1.call-done = f32[64,16]{1,0:T(8,128)} async-done(((f32[2048,16]{1,0:T(8,128)}), f32[64,16]{1,0:T(8,128)}) %reduce-scatter.45.cloned.1.call-update) | async-done | bytes 4112
  4265.2 132.0 %reduce-scatter.43.cloned.1.call-done = f32[64,64]{1,0:T(8,128)} async-done(((f32[2048,64]{1,0:T(8,128)}), f32[64,64]{1,0:T(8,128)}) %reduce-scatter.43.cloned.1.call-update) | async-done | bytes 16400
  4398.1 132.5 %reduce-scatter.41.cloned.1.call-done = f32[64,64]{1,0:T(8,128)} async-done(((f32[2048,64]{1,0:T(8,128)}), f32[64,64]{1,0:T(8,128)}) %reduce-scatter.41.cloned.1.call-update) | async-done | bytes 16400
  4532.0 131.8 %reduce-scatter.31.cloned.1.call-done = f32[64,96]{1,0:T(8,128)} async-done(((f32[2048,96]{1,0:T(8,128)}), f32[64,96]{1,0:T(8,128)}) %reduce-scatter.31.cloned.1.call-update) | async-done | bytes 24592 | tf_op jit(solution)/shard_map/reduce_scatter | solution.py:310
  4663.8 133.4 %reduce-scatter.29.cloned.1.call-done = f32[64,96]{1,0:T(8,128)} async-done(((f32[2048,96]{1,0:T(8,128)}), f32[64,96]{1,0:T(8,128)}) %reduce-scatter.29.cloned.1.call-update) | async-done | bytes 24592 | tf_op jit(solution)/shard_map/reduce_scatter | solution.py:310
  4798.7 149.1 %reduce-scatter.35.cloned.1.call-done = f32[2048,32]{0,1:T(8,128)} async-done(((f32[2048,1024]{0,1:T(8,128)}), f32[2048,32]{0,1:T(8,128)}) %reduce-scatter.35.cloned.1.call-update) | async-done | bytes 262160 | tf_op jit(solution)/shard_map/reduce_scatter | solution.py:315
  4947.7 151.4 %reduce-scatter.33.cloned.1.call-done = f32[2048,32]{0,1:T(8,128)} async-done(((f32[2048,1024]{0,1:T(8,128)}), f32[2048,32]{0,1:T(8,128)}) %reduce-scatter.33.cloned.1.call-update) | async-done | bytes 262160 | tf_op jit(solution)/shard_map/reduce_scatter | solution.py:315
  5101.0 185.3 %reduce-scatter.27.cloned.1.call-done = f32[1024,128]{1,0:T(8,128)} async-done(((f32[1024,4096]{1,0:T(8,128)}), f32[1024,128]{1,0:T(8,128)}) %reduce-scatter.27.cloned.1.call-update) | async-done | bytes 524304 | tf_op jit(solution)/shard_map/reduce_scatter | solution.py:307
  5286.3 186.5 %reduce-scatter.25.cloned.1.call-done = f32[1024,128]{1,0:T(8,128)} async-done(((f32[1024,4096]{1,0:T(8,128)}), f32[1024,128]{1,0:T(8,128)}) %reduce-scatter.25.cloned.1.call-update) | async-done | bytes 524304 | tf_op jit(solution)/shard_map/reduce_scatter | solution.py:307
  (8227 shorter events, 3762.6 us)
Async XLA Ops:
  7.2 237.3 %all-gather.37.cloned.1.call-start = ((), (), s32[]{:S(2)}) async-start(), calls=%async_computation.18 | async-start | bytes 8650752 | tf_op jit(solution)/shard_map/all_gather | solution.py:275
  9.1 612.0 %all-gather.41.cloned.1.call-start = ((), (), s32[]{:S(2)}) async-start(), calls=%async_computation.20 | async-start | bytes 1179648 | tf_op jit(solution)/shard_map/all_gather | solution.py:20
  252.3 47.5 collective-permute-start
  355.5 265.6 %all-gather.39.cloned.1.call-start = ((), (), s32[]{:S(2)}) async-start(), calls=%async_computation.19 | async-start | bytes 1179648 | tf_op jit(solution)/shard_map/all_gather | solution.py:20
  356.3 350.7 %all-gather.43.cloned.1.call-start = ((), (), s32[]{:S(2)}) async-start(), calls=%async_computation.21 | async-start | bytes 4325376 | tf_op jit(solution)/shard_map/all_gather | solution.py:283
  358.0 352.9 %all-gather.45.cloned.1.call-start = ((), (), s32[]{:S(2)}) async-start(), calls=%async_computation.22 | async-start | bytes 8650752 | tf_op jit(solution)/shard_map/all_gather | solution.py:275
  358.6 1120.9 %all-gather.51.cloned.1.call-start = ((), (), s32[]{:S(2)}) async-start(), calls=%async_computation.25 | async-start | bytes 4325376 | tf_op jit(solution)/shard_map/all_gather | solution.py:283
  359.2 1261.8 %all-gather.49.cloned.1.call-start = ((), (), s32[]{:S(2)}) async-start(), calls=%async_computation.24 | async-start | bytes 1179648 | tf_op jit(solution)/shard_map/all_gather | solution.py:20
  719.7 758.2 %collective-permute-start.1 = (bf16[3,2048]{1,0:T(4,128)(2,1)}, bf16[3,2048]{1,0:T(4,128)(2,1)S(1)}, u32[]{:S(2)}, u32[]{:S(2)}) collective-permute-start(bf16[3,2048]{1,0:T(4,128)(2,1)} %slice.4844), channel_id=1, source_target_pairs={{0,1},{1,2},{2,3},{3,4},{4,5},{5,6},{6,7},{8,9},{9,10},{10,11},{11... | collective-permute-start | bytes 36872 | tf_op jit(solution)/shard_map/ppermute | solution.py:15
  1543.7 98.2 %all-gather.47.cloned.1.call-start = ((), (), s32[]{:S(2)}) async-start(), calls=%async_computation.23 | async-start | bytes 1179648 | tf_op jit(solution)/shard_map/all_gather | solution.py:20
  1620.1 2344.2 %reduce-scatter.39.cloned.1.call-start = ((), (), s32[]{:S(2)}) async-start(), calls=%async_computation.27 | async-start | bytes 1081344
  3062.5 3.9 collective-permute-start.2
  3065.3 931.8 %reduce-scatter.37.cloned.1.call-start = ((), (), s32[]{:S(2)}) async-start(), calls=%async_computation.26 | async-start | bytes 1081344
  3860.3 270.2 %reduce-scatter.47.cloned.1.call-start = ((), (), s32[]{:S(2)}) async-start(), calls=%async_computation.31 | async-start | bytes 1081344
  3861.8 401.9 %reduce-scatter.45.cloned.1.call-start = ((), (), s32[]{:S(2)}) async-start(), calls=%async_computation.30 | async-start | bytes 1081344
  3863.3 533.9 %reduce-scatter.43.cloned.1.call-start = ((), (), s32[]{:S(2)}) async-start(), calls=%async_computation.29 | async-start | bytes 1081344
  3864.9 665.6 %reduce-scatter.41.cloned.1.call-start = ((), (), s32[]{:S(2)}) async-start(), calls=%async_computation.28 | async-start | bytes 1081344
  3866.6 797.2 %reduce-scatter.31.cloned.1.call-start = ((), (), s32[]{:S(2)}) async-start(), calls=%async_computation.15 | async-start | bytes 1081344 | tf_op jit(solution)/shard_map/reduce_scatter | solution.py:310
  3868.2 929.0 %reduce-scatter.29.cloned.1.call-start = ((), (), s32[]{:S(2)}) async-start(), calls=%async_computation.14 | async-start | bytes 1081344 | tf_op jit(solution)/shard_map/reduce_scatter | solution.py:310
  3869.8 1078.0 %reduce-scatter.35.cloned.1.call-start = ((), (), s32[]{:S(2)}) async-start(), calls=%async_computation.17 | async-start | bytes 8650752 | tf_op jit(solution)/shard_map/reduce_scatter | solution.py:315
  3874.5 1224.6 %reduce-scatter.33.cloned.1.call-start = ((), (), s32[]{:S(2)}) async-start(), calls=%async_computation.16 | async-start | bytes 8650752 | tf_op jit(solution)/shard_map/reduce_scatter | solution.py:315
  3880.6 1405.7 %reduce-scatter.27.cloned.1.call-start = ((), (), s32[]{:S(2)}) async-start(), calls=%async_computation.13 | async-start | bytes 17301504 | tf_op jit(solution)/shard_map/reduce_scatter | solution.py:307
  3891.5 1581.3 %reduce-scatter.25.cloned.1.call-start = ((), (), s32[]{:S(2)}) async-start(), calls=%async_computation.12 | async-start | bytes 17301504 | tf_op jit(solution)/shard_map/reduce_scatter | solution.py:307
  3892.7 3.6 collective-permute-start.3
  (1233 other events, 16790.3 us)
Sparse Core Ops, SparseCore 0:
  11.5 101.7 all-gather.36
  355.7 21.7 all-gather.40
  379.6 24.6 all-gather.38
  407.1 61.8 all-gather.42
  472.4 103.7 all-gather.44
  579.0 62.0 all-gather.50
  1543.8 24.3 all-gather.48
  1620.2 21.6 all-gather.46
  3065.4 141.8 reduce-scatter.38
  3860.4 136.5 reduce-scatter.36
  3999.3 131.1 reduce-scatter.46
  4132.7 131.0 reduce-scatter.44
  4266.0 131.1 reduce-scatter.42
  4399.4 131.1 reduce-scatter.40
  4532.7 131.1 reduce-scatter.30
  4666.0 131.1 reduce-scatter.28
  4799.4 148.2 reduce-scatter.34
  4949.9 149.1 reduce-scatter.32
  5101.4 184.8 reduce-scatter.26
  5288.4 184.3 reduce-scatter.24
where the time goes:
time: 5560 us; the launch traced here: 5480 us
  other arithmetic  1640 us (29%)
  waiting for transfers between devices  1520 us (27%)
  local copies, waits for them, and re-layouts  1510 us (27%)
  blocking collectives  528 us (9%)
  matrix products  223 us (4%)
    unnamed x26, waiting for transfers between devices  563 us
    while x928, other arithmetic  477 us
    reduce_scatter x2, waiting for transfers between devices, on_device(): lax.psum_scatter(g_in, ('ctx', 'seq'), scatter_dimension=1, tiled=True)  372 us
    concatenate x224, local copies, waits for them, and re-layouts, scan_states(): lax.scan(row_step, start, (conv_act, step_size, in_coeff, out_coeff), unr...  364 us
    while x3872, local copies, waits for them, and re-layouts  350 us
    reduce_scatter x2, waiting for transfers between devices, on_device(): lax.psum_scatter(g_out, ('ctx', 'seq'), scatter_dimension=1, tiled=True)  300 us
    reduce_sum x512, other arithmetic, row_step(): in_row[:, None] * (step_row * act_row)[None, :]  281 us
    dynamic_update_slice x256, local copies, waits for them, and re-layouts, scan_states(): lax.scan(row_step, start, (conv_act, step_size, in_coeff, out_coeff), unr...  277 us

commit v1 on v0

v1 whole, which is shorter than its diff:
```python
import functools

import jax
import jax.numpy as jnp
from jax import lax
from jax.experimental import pallas as pl
from jax.experimental.pallas import tpu as pltpu
from jax.sharding import PartitionSpec as P

EPS = 1e-05
LOG2E = 1.4426950408889634
MESH = pl.DeviceIdType.MESH
F32, BF16 = jnp.float32, jnp.bfloat16
NT = (((1,), (1,)), ((), ()))
TN = (((0,), (0,)), ((), ()))
VMEM_BYTES = 63 * 2**20
CHUNK = 16
GROUP = 512
HALO = 16


def dot(a, b, dims=None):
    if dims is None:
        dims = (((1,), (0,)), ((), ()))
    return lax.dot_general(a, b, dims, preferred_element_type=F32)


def lanes(index, width):
    return pl.ds(pl.multiple_of(index * width, width), width)


def widen(tile, width):
    times = width // tile.shape[1]
    return jnp.concatenate([tile] * times, axis=1) if times > 1 else tile


def softplus(v):
    return jnp.maximum(v, 0.0) + jnp.log1p(jnp.exp(-jnp.abs(v)))


def sigmoid(v):
    return 1.0 / (1.0 + jnp.exp(-v))


def keep_sum(own_sum, i, step):
    total = jnp.sum(step, axis=0, keepdims=True)
    fold = own_sum.shape[1]
    for part in range(GROUP // fold):
        row = i * (GROUP // fold) + part
        own_sum[pl.ds(row, 1), :] = total[:, part * fold : (part + 1) * fold]


def sum_of(sum_s, j, g):
    fold = sum_s.shape[2]
    each = GROUP // fold
    return jnp.concatenate(
        [sum_s[j, pl.ds(g * each + part, 1), :] for part in range(each)], 1
    )


def chunk_mask(rows, states):
    wide = CHUNK * states
    token = lax.rem(lax.broadcasted_iota(jnp.int32, (rows, wide), 0), CHUNK)
    owner = lax.broadcasted_iota(jnp.int32, (rows, wide), 1) // states
    return token == owner


def spread(small_low, first, states):
    wide = CHUNK * states
    row = lax.broadcasted_iota(jnp.int32, (small_low.shape[1], wide), 0)
    col = lax.broadcasted_iota(jnp.int32, (small_low.shape[1], wide), 1)
    pick = (row == first + lax.rem(col, states)).astype(F32).astype(BF16)
    tiled = dot(small_low, pick)
    return jnp.where(chunk_mask(small_low.shape[0], states), tiled, 0.0).astype(BF16)


def gather_back(partial, first, states, width):
    wide = CHUNK * states
    row = lax.broadcasted_iota(jnp.int32, (wide, width), 0)
    col = lax.broadcasted_iota(jnp.int32, (wide, width), 1)
    pick = (col == first + lax.rem(row, states)).astype(F32).astype(BF16)
    kept = jnp.where(chunk_mask(partial.shape[0], states), partial, 0.0)
    return dot(kept.astype(BF16), pick)


class Names:
    def __init__(self, states, taps):
        self.conv = states
        self.conv_b = states + taps
        self.dt_b = states + taps + 1
        self.skip = states + taps + 2
        self.count = states + taps + 3
        self.padded = -(-self.count // 8) * 8


def forward_kernel(
    cfg,
    stream_ref,
    gain_ref,
    win_ref,
    xw_ref,
    dtw_ref,
    vec_ref,
    wout_ref,
    new_ref,
    pad_ref,
    gate_ref,
    act_ref,
    sp_ref,
    pre_ref,
    h_hbm,
    y_ref,
    mixed_ref,
    normed_s,
    padf_s,
    halo_s,
    dt_s,
    dx_s,
    bb_s,
    cd_s,
    hs,
    own_sum,
    sum_s,
    own_end,
    end_s,
    halo_sem,
    sum_send,
    sum_recv,
    end_send,
    end_recv,
    h_sem,
):
    rows, inner, states, taps, rank, count = cfg
    at = Names(states, taps)
    ctx, me = lax.axis_index("ctx"), lax.axis_index("seq")
    groups, steps = inner // GROUP, rows // CHUNK
    barrier = pltpu.get_barrier_semaphore()

    def greet(j, _):
        pl.semaphore_signal(barrier, inc=1, device_id=(ctx, j), device_id_type=MESH)
        return 0

    lax.fori_loop(0, me, greet, 0)
    stream = stream_ref[...]
    scale = lax.rsqrt(jnp.mean(stream * stream, axis=1, keepdims=True) + EPS)
    normed_s[...] = (stream * scale * gain_ref[...]).astype(BF16)

    @pl.loop(0, inner // GROUP)
    def _(i):
        low = dot(normed_s[...], win_ref[lanes(i, GROUP), :], NT).astype(BF16)
        pad_ref[pl.ds(HALO, rows), lanes(i, GROUP)] = low
        padf_s[pl.ds(HALO, rows), lanes(i, GROUP)] = low.astype(F32)

    @pl.when(me < count - 1)
    def _():
        pl.semaphore_wait(barrier, count - 1 - me)

    def edge():
        return pltpu.make_async_remote_copy(
            pad_ref.at[pl.ds(rows, HALO)],
            halo_s,
            halo_sem.at[0],
            halo_sem.at[1],
            device_id=(ctx, jnp.minimum(me + 1, count - 1)),
            device_id_type=MESH,
        )

    @pl.when(me < count - 1)
    def _():
        edge().start()

    @pl.loop(0, inner // GROUP)
    def _(i):
        gate_ref[:, lanes(i, GROUP)] = dot(
            normed_s[...], win_ref[lanes(i + inner // GROUP, GROUP), :], NT
        )

    @pl.when(me > 0)
    def _():
        edge().wait_recv()

    @pl.when(me == 0)
    def _():
        halo_s[...] = jnp.zeros_like(halo_s)

    pad_ref[pl.ds(0, HALO), :] = halo_s[...]
    padf_s[pl.ds(0, HALO), :] = halo_s[...].astype(F32)

    @pl.loop(0, inner // GROUP)
    def _(i):
        here = lanes(i, GROUP)
        total = vec_ref[pl.ds(at.conv_b, 1), here]
        for k in range(taps):
            total = (
                total
                + vec_ref[pl.ds(at.conv + k, 1), here]
                * padf_s[pl.ds(HALO - taps + 1 + k, rows), here]
            )
        act_ref[:, here] = (total * sigmoid(total)).astype(BF16)

    small = dot(act_ref[...], xw_ref[...], NT)
    sp_ref[...] = small
    small_low = small.astype(BF16)

    @pl.loop(0, inner // GROUP)
    def _(i):
        here = lanes(i, GROUP)
        before = dot(small_low, dtw_ref[:, here]) + vec_ref[pl.ds(at.dt_b, 1), here]
        step = softplus(before)
        pre_ref[:, here] = before
        dt_s[:, here] = step
        dx_s[:, here] = step * act_ref[:, here].astype(F32)
        keep_sum(own_sum, i, step)

    def sums(j):
        return pltpu.make_async_remote_copy(
            own_sum,
            sum_s.at[me],
            sum_send.at[j],
            sum_recv.at[me],
            device_id=(ctx, j),
            device_id_type=MESH,
        )

    def sums_from(j):
        return pltpu.make_async_remote_copy(
            own_sum,
            sum_s.at[j],
            sum_send.at[j],
            sum_recv.at[j],
            device_id=(ctx, j),
            device_id_type=MESH,
        )

    def ends(g, j, slot):
        return pltpu.make_async_remote_copy(
            own_end.at[:, pl.ds(g * GROUP, GROUP)],
            end_s.at[slot, :, pl.ds(g * GROUP, GROUP)],
            end_send.at[g, j],
            end_recv.at[g, slot],
            device_id=(ctx, j),
            device_id_type=MESH,
        )

    def each(first, last, act):
        def body(j, _):
            act(j)
            return 0

        lax.fori_loop(first, last, body, 0)

    each(me + 1, count, lambda j: sums(j).start())
    for n in range(states):
        bb_s[:, n, :] = jnp.broadcast_to(
            small[:, rank + n : rank + n + 1], (rows, 128)
        )
    cd_s[...] = spread(small_low, rank + states, states)

    def advance(t, state, rate2, here):
        return (
            jnp.exp2(dt_s[pl.ds(t, 1), here] * rate2) * state
            + dx_s[pl.ds(t, 1), here] * widen(bb_s[t], GROUP)
        )

    for g in range(groups):
        here = pl.ds(g * GROUP, GROUP)
        rate2 = vec_ref[pl.ds(0, states), here] * LOG2E

        def first_pass(step, state):
            for i in range(CHUNK):
                state = advance(step * CHUNK + i, state, rate2, here)
            return state

        own_end[:, here] = lax.fori_loop(
            0, steps, first_pass, jnp.zeros((states, GROUP), F32)
        ).astype(BF16)
        each(me + 1, count, lambda j: ends(g, j, me).start())

    for g in range(groups):
        here = pl.ds(g * GROUP, GROUP)
        rate2 = vec_ref[pl.ds(0, states), here] * LOG2E

        def carry(j, state):
            if g == 0:
                sums_from(j).wait_recv()
            ends(g, j, j).wait_recv()
            return (
                jnp.exp2(rate2 * sum_of(sum_s, j, g)) * state
                + end_s[j, :, here].astype(F32)
            )

        start = lax.fori_loop(0, me, carry, jnp.zeros((states, GROUP), F32))
        hs[pl.ds(0, states), here] = start.astype(BF16)

        def second_pass(step, state):
            base = pl.multiple_of(step * CHUNK * states + states, states)
            for i in range(CHUNK):
                state = advance(step * CHUNK + i, state, rate2, here)
                hs[pl.ds(base + i * states, states), here] = state.astype(BF16)
            tokens = pl.ds(pl.multiple_of(step * CHUNK, CHUNK), CHUNK)
            y_ref[tokens, here] = dot(
                cd_s[tokens, :], hs[pl.ds(base, CHUNK * states), here]
            )
            return state

        lax.fori_loop(0, steps, second_pass, start)
        pltpu.make_async_copy(hs.at[:, here], h_hbm.at[:, here], h_sem.at[g]).start()
        y_value = (
            y_ref[:, here]
            + vec_ref[pl.ds(at.skip, 1), here] * act_ref[:, here].astype(F32)
        )
        gate = gate_ref[:, here]
        y_ref[:, here] = y_value
        mixed_ref[:, here] = (y_value * gate * sigmoid(gate)).astype(BF16)

    width = stream_ref.shape[1]
    for i in range(width // 256):
        here = pl.ds(i * 256, 256)
        new_ref[:, here] = stream_ref[:, here] + dot(
            mixed_ref[...], wout_ref[here, :], NT
        )

    @pl.when(me < count - 1)
    def _():
        edge().wait_send()

    each(me + 1, count, lambda j: sums(j).wait_send())
    for g in range(groups):
        here = pl.ds(g * GROUP, GROUP)
        each(me + 1, count, lambda j: ends(g, j, me).wait_send())
        pltpu.make_async_copy(hs.at[:, here], h_hbm.at[:, here], h_sem.at[g]).wait()


def backward_kernel(
    cfg,
    sgrad_ref,
    stream_ref,
    gain_ref,
    win_ref,
    xw_ref,
    dtw_ref,
    vec_ref,
    wout_ref,
    pad_ref,
    gate_ref,
    act_ref,
    sp_ref,
    pre_ref,
    h_hbm,
    y_ref,
    mixed_ref,
    nsg_ref,
    gin_hbm,
    gout_hbm,
    gx_ref,
    gdt_ref,
    gvec_ref,
    ggain_ref,
    hb,
    normed_s,
    low_s,
    sg_s,
    dt_s,
    dx_s,
    stepg_s,
    pb_s,
    cb_s,
    bd_s,
    ab_s,
    rb_s,
    pin_s,
    pout_s,
    prelow_s,
    stage_in,
    stage_out,
    halo_s,
    own_sum,
    sum_s,
    own_end,
    end_s,
    halo_sem,
    sum_send,
    sum_recv,
    end_send,
    end_recv,
    h_sem,
    in_sem,
    out_sem,
):
    rows, inner, states, taps, rank, count = cfg
    at = Names(states, taps)
    ctx, me = lax.axis_index("ctx"), lax.axis_index("seq")
    groups, steps = inner // GROUP, rows // CHUNK
    width = stream_ref.shape[1]
    barrier = pltpu.get_barrier_semaphore()

    def each(first, last, act):
        def body(j, _):
            act(j)
            return 0

        lax.fori_loop(first, last, body, 0)

    each(
        me + 1,
        count,
        lambda j: pl.semaphore_signal(
            barrier, inc=1, device_id=(ctx, j), device_id_type=MESH
        ),
    )

    def states_in(g):
        return pltpu.make_async_copy(
            h_hbm.at[:, pl.ds(g * GROUP, GROUP)], hb.at[g % 2], h_sem.at[g % 2]
        )

    states_in(0).start()
    low_s[...] = sgrad_ref[...].astype(BF16)
    stream = stream_ref[...]
    scale = lax.rsqrt(jnp.mean(stream * stream, axis=1, keepdims=True) + EPS)
    normed_s[...] = (stream * scale * gain_ref[...]).astype(BF16)
    small_low = sp_ref[...].astype(BF16)

    @pl.loop(0, inner // GROUP)
    def _(i):
        here = lanes(i, GROUP)
        mixed_grad = dot(low_s[...], wout_ref[:, here])
        gate = gate_ref[:, here]
        sig = sigmoid(gate)
        act = act_ref[:, here].astype(F32)
        scan_grad = mixed_grad * gate * sig
        sg_s[:, here] = scan_grad
        pb_s[:, lanes(i + inner // GROUP, GROUP)] = (
            mixed_grad * y_ref[:, here] * sig * (1.0 + gate * (1.0 - sig))
        ).astype(BF16)
        gvec_ref[pl.ds(at.skip, 1), here] = jnp.sum(
            scan_grad * act, axis=0, keepdims=True
        )
        step = softplus(pre_ref[:, here])
        dt_s[:, here] = step
        dx_s[pl.ds(0, rows), here] = step * act
        keep_sum(own_sum, i, step)

    def sums(j, slot):
        return pltpu.make_async_remote_copy(
            own_sum,
            sum_s.at[slot],
            sum_send.at[j],
            sum_recv.at[slot],
            device_id=(ctx, j),
            device_id_type=MESH,
        )

    def ends(g, j, slot):
        return pltpu.make_async_remote_copy(
            own_end.at[:, pl.ds(g * GROUP, GROUP)],
            end_s.at[slot, :, pl.ds(g * GROUP, GROUP)],
            end_send.at[g, j],
            end_recv.at[g, slot],
            device_id=(ctx, j),
            device_id_type=MESH,
        )

    @pl.when(me > 0)
    def _():
        pl.semaphore_wait(barrier, me)

    each(0, me, lambda j: sums(j, me).start())
    for n in range(states):
        first = rank + states + n
        cb_s[:, n, :] = jnp.broadcast_to(
            sp_ref[:, first : first + 1], (rows, 128)
        )
    bd_s[...] = spread(small_low, rank, states)
    ones = jnp.where(chunk_mask(CHUNK, states), 1.0, 0.0).astype(BF16)

    for g in range(groups):
        here = pl.ds(g * GROUP, GROUP)
        rate2 = vec_ref[pl.ds(0, states), here] * LOG2E

        def first_pass(k, state):
            step = steps - 1 - k
            for i in reversed(range(CHUNK)):
                t = step * CHUNK + i
                state = jnp.exp2(dt_s[pl.ds(t, 1), here] * rate2) * (
                    state + sg_s[pl.ds(t, 1), here] * widen(cb_s[t], GROUP)
                )
            return state

        own_end[:, here] = lax.fori_loop(
            0, steps, first_pass, jnp.zeros((states, GROUP), F32)
        ).astype(BF16)
        each(0, me, lambda j: ends(g, j, me).start())

    for g in range(groups):
        here = pl.ds(g * GROUP, GROUP)
        rate = vec_ref[pl.ds(0, states), here]
        rate2 = rate * LOG2E
        if g + 1 < groups:
            states_in(g + 1).start()

        def carry(k, state):
            j = count - 1 - k
            if g == 0:
                sums(j, j).wait_recv()
            ends(g, j, j).wait_recv()
            return (
                jnp.exp2(rate2 * sum_of(sum_s, j, g)) * state
                + end_s[j, :, here].astype(F32)
            )

        begin = lax.fori_loop(
            0, count - 1 - me, carry, jnp.zeros((states, GROUP), F32)
        )
        states_in(g).wait()

        def second_pass(k, both):
            state, total = both
            step = steps - 1 - k
            base = pl.multiple_of(step * CHUNK * states, states)
            for i in reversed(range(CHUNK)):
                t = step * CHUNK + i
                dt = dt_s[pl.ds(t, 1), here]
                adjoint = state + sg_s[pl.ds(t, 1), here] * widen(cb_s[t], GROUP)
                state = jnp.exp2(dt * rate2) * adjoint
                held = hb[g % 2, pl.ds(base + i * states, states), :].astype(F32)
                rated = state * held * rate
                total = total + dt * rated
                ab_s[pl.ds(i * states, states), :] = adjoint.astype(BF16)
                rb_s[pl.ds(i * states, states), :] = rated.astype(BF16)
            tokens = pl.ds(pl.multiple_of(step * CHUNK, CHUNK), CHUNK)
            from_in = dot(bd_s[tokens, :], ab_s[...])
            from_rate = dot(ones, rb_s[...])
            scan_grad = sg_s[tokens, here]
            into_in = dot(dx_s[tokens, here].astype(BF16), ab_s[...], NT)
            into_out = dot(
                scan_grad.astype(BF16),
                hb[g % 2, pl.ds(base + states, CHUNK * states), :],
                NT,
            )
            if g == 0:
                pin_s[tokens, :] = into_in
                pout_s[tokens, :] = into_out
            else:
                pin_s[tokens, :] += into_in
                pout_s[tokens, :] += into_out
            stepg_s[tokens, here] = (
                act_ref[tokens, here].astype(F32) * from_in + from_rate
            )
            sg_s[tokens, here] = (
                dt_s[tokens, here] * from_in
                + vec_ref[pl.ds(at.skip, 1), here] * scan_grad
            )
            return state, total

        _, total = lax.fori_loop(
            0, steps, second_pass, (begin, jnp.zeros((states, GROUP), F32))
        )
        gvec_ref[pl.ds(0, states), here] = total

    @pl.loop(0, inner // GROUP)
    def _(i):
        here = lanes(i, GROUP)
        pre_grad = stepg_s[pl.ds(0, rows), here] * sigmoid(pre_ref[:, here])
        gvec_ref[pl.ds(at.dt_b, 1), here] = jnp.sum(pre_grad, axis=0, keepdims=True)
        prelow_s[:, here] = pre_grad.astype(BF16)
        dx_s[:, here] = pad_ref[:, here].astype(F32)

    small_grad = (
        dot(prelow_s[...], dtw_ref[...], NT)
        + gather_back(pin_s[...], rank, states, sp_ref.shape[1])
        + gather_back(pout_s[...], rank + states, states, sp_ref.shape[1])
    ).astype(BF16)

    @pl.loop(0, inner // GROUP)
    def _(i):
        here = lanes(i, GROUP)
        gdt_ref[:, here] = dot(small_low, prelow_s[:, here], TN)
        gx_ref[:, here] = dot(small_grad, act_ref[:, here], TN)
        act_grad = sg_s[:, here] + dot(small_grad, xw_ref[:, here])
        total = vec_ref[pl.ds(at.conv_b, 1), here]
        for k in range(taps):
            total = (
                total
                + vec_ref[pl.ds(at.conv + k, 1), here]
                * dx_s[pl.ds(HALO - taps + 1 + k, rows), here]
            )
        sig = sigmoid(total)
        conv_grad = act_grad * sig * (1.0 + total * (1.0 - sig))
        stepg_s[pl.ds(0, rows), here] = conv_grad
        gvec_ref[pl.ds(at.conv_b, 1), here] = jnp.sum(conv_grad, axis=0, keepdims=True)
        for k in range(taps):
            gvec_ref[pl.ds(at.conv + k, 1), here] = jnp.sum(
                conv_grad * dx_s[pl.ds(HALO - taps + 1 + k, rows), here],
                axis=0,
                keepdims=True,
            )

    def edge():
        return pltpu.make_async_remote_copy(
            stepg_s.at[pl.ds(0, 8)],
            halo_s,
            halo_sem.at[0],
            halo_sem.at[1],
            device_id=(ctx, jnp.maximum(me - 1, 0)),
            device_id_type=MESH,
        )

    @pl.when(me > 0)
    def _():
        edge().start()

    tiles = inner // GROUP

    def project(i, first):
        here = lanes(i, GROUP)
        slot = lax.rem(i, 2)
        copy = pltpu.make_async_copy(
            stage_in.at[slot], gin_hbm.at[here], in_sem.at[slot]
        )

        @pl.when(first >= 2)
        def _():
            copy.wait()

        stage_in[slot] = dot(pb_s[:, here], normed_s[...], TN).astype(BF16)
        copy.start()
        part = dot(pb_s[:, here], win_ref[here, :])

        @pl.when(first == 0)
        def _():
            nsg_ref[...] = part

        @pl.when(first > 0)
        def _():
            nsg_ref[...] += part

    @pl.loop(0, tiles)
    def _(i):
        project(i + tiles, i)

    out_rows = stage_out.shape[1]
    for r in range(width // out_rows):
        slot = r % 2
        copy = pltpu.make_async_copy(
            stage_out.at[slot],
            gout_hbm.at[pl.ds(r * out_rows, out_rows)],
            out_sem.at[slot],
        )
        if r >= 2:
            copy.wait()

        @pl.loop(0, tiles)
        def _(i):
            here = lanes(i, GROUP)
            stage_out[slot, :, here] = dot(
                low_s[:, pl.ds(r * out_rows, out_rows)], mixed_ref[:, here], TN
            ).astype(BF16)

        copy.start()

    @pl.when(me < count - 1)
    def _():
        edge().wait_recv()

    @pl.when(me == count - 1)
    def _():
        halo_s[...] = jnp.zeros_like(halo_s)

    @pl.when(me > 0)
    def _():
        edge().wait_send()

    stepg_s[pl.ds(rows, 8), :] = halo_s[...]

    @pl.loop(0, tiles)
    def _(i):
        here = lanes(i, GROUP)
        total = jnp.zeros((rows, GROUP), F32)
        for k in range(taps):
            total = (
                total
                + vec_ref[pl.ds(at.conv + k, 1), here]
                * stepg_s[pl.ds(taps - 1 - k, rows), here]
            )
        pb_s[:, here] = total.astype(BF16)
        project(i, i + tiles)

    stream = stream_ref[...]
    scale = lax.rsqrt(jnp.mean(stream * stream, axis=1, keepdims=True) + EPS)
    normed_grad = nsg_ref[...]
    ggain_ref[...] = jnp.broadcast_to(
        jnp.sum(normed_grad * stream * scale, axis=0, keepdims=True), (8, width)
    )
    scaled = normed_grad * gain_ref[...]
    inner_sum = jnp.mean(scaled * stream, axis=1, keepdims=True)
    nsg_ref[...] = (
        sgrad_ref[...] + scale * scaled - stream * (scale * scale * scale) * inner_sum
    )
    for slot in range(2):
        pltpu.make_async_copy(
            stage_in.at[slot], gin_hbm.at[pl.ds(0, GROUP)], in_sem.at[slot]
        ).wait()
        pltpu.make_async_copy(
            stage_out.at[slot], gout_hbm.at[pl.ds(0, out_rows)], out_sem.at[slot]
        ).wait()
    each(0, me, lambda j: sums(j, me).wait_send())
    for g in range(groups):
        each(0, me, lambda j: ends(g, j, me).wait_send())


def in_vmem(count):
    return [pl.BlockSpec(memory_space=pltpu.VMEM)] * count


def in_any(count):
    return [pl.BlockSpec(memory_space=pl.ANY)] * count


def forward_call(cfg, stream, gain, win, xw, dtw, vec, wout):
    rows, inner, states, taps, rank, count = cfg
    small = rank + 2 * states
    groups = inner // GROUP
    shape = jax.ShapeDtypeStruct
    dma = pltpu.SemaphoreType.DMA
    return pl.pallas_call(
        functools.partial(forward_kernel, cfg),
        out_shape=(
            shape(stream.shape, F32),
            shape((rows + HALO, inner), BF16),
            shape((rows, inner), F32),
            shape((rows, inner), BF16),
            shape((rows, small), F32),
            shape((rows, inner), F32),
            shape(((rows + 1) * states, inner), BF16),
            shape((rows, inner), F32),
            shape((rows, inner), BF16),
        ),
        in_specs=in_vmem(7),
        out_specs=tuple(in_vmem(6) + in_any(1) + in_vmem(2)),
        scratch_shapes=[
            pltpu.VMEM(stream.shape, BF16),
            pltpu.VMEM((rows + HALO, inner), F32),
            pltpu.VMEM((HALO, inner), BF16),
            pltpu.VMEM((rows, inner), F32),
            pltpu.VMEM((rows, inner), F32),
            pltpu.VMEM((rows, states, 128), F32),
            pltpu.VMEM((rows, CHUNK * states), BF16),
            pltpu.VMEM(((rows + 1) * states, inner), BF16),
            pltpu.VMEM((8, inner // 8), F32),
            pltpu.VMEM((count, 8, inner // 8), F32),
            pltpu.VMEM((states, inner), BF16),
            pltpu.VMEM((count, states, inner), BF16),
            dma((2,)),
            dma((count,)),
            dma((count,)),
            dma((groups, count)),
            dma((groups, count)),
            dma((groups,)),
        ],
        compiler_params=pltpu.CompilerParams(
            collective_id=0, has_side_effects=True, vmem_limit_bytes=VMEM_BYTES
        ),
        name="forward_layer",
    )(stream, gain, win, xw, dtw, vec, wout)


def backward_call(cfg, sgrad, stream, gain, win, xw, dtw, vec, wout, saved):
    rows, inner, states, taps, rank, count = cfg
    width = stream.shape[1]
    small = rank + 2 * states
    groups = inner // GROUP
    wide = CHUNK * states
    shape = jax.ShapeDtypeStruct
    dma = pltpu.SemaphoreType.DMA
    return pl.pallas_call(
        functools.partial(backward_kernel, cfg),
        out_shape=(
            shape((rows, width), F32),
            shape((2 * inner, width), BF16),
            shape((width, inner), BF16),
            shape((small, inner), F32),
            shape((small, inner), F32),
            shape((Names(states, taps).padded, inner), F32),
            shape((8, width), F32),
        ),
        in_specs=in_vmem(13) + in_any(1) + in_vmem(2),
        out_specs=tuple(in_vmem(1) + in_any(2) + in_vmem(4)),
        scratch_shapes=[
            pltpu.VMEM((2, (rows + 1) * states, GROUP), BF16),
            pltpu.VMEM((rows, width), BF16),
            pltpu.VMEM((rows, width), BF16),
            pltpu.VMEM((rows, inner), F32),
            pltpu.VMEM((rows, inner), F32),
            pltpu.VMEM((rows + HALO, inner), F32),
            pltpu.VMEM((rows + 8, inner), F32),
            pltpu.VMEM((rows, 2 * inner), BF16),
            pltpu.VMEM((rows, states, 128), F32),
            pltpu.VMEM((rows, wide), BF16),
            pltpu.VMEM((wide, GROUP), BF16),
            pltpu.VMEM((wide, GROUP), BF16),
            pltpu.VMEM((rows, wide), F32),
            pltpu.VMEM((rows, wide), F32),
            pltpu.VMEM((rows, inner), BF16),
            pltpu.VMEM((2, GROUP, width), BF16),
            pltpu.VMEM((2, width // 4, inner), BF16),
            pltpu.VMEM((8, inner), F32),
            pltpu.VMEM((8, inner // 8), F32),
            pltpu.VMEM((count, 8, inner // 8), F32),
            pltpu.VMEM((states, inner), BF16),
            pltpu.VMEM((count, states, inner), BF16),
            dma((2,)),
            dma((count,)),
            dma((count,)),
            dma((groups, count)),
            dma((groups, count)),
            dma((2,)),
            dma((2,)),
            dma((2,)),
        ],
        compiler_params=pltpu.CompilerParams(
            collective_id=1, has_side_effects=True, vmem_limit_bytes=VMEM_BYTES
        ),
        name="backward_layer",
    )(sgrad, stream, gain, win, xw, dtw, vec, wout, *saved)


def parts_of(in_rows, out_rows, small_rows):
    cut = in_rows * 3 // 4 // 16 * 16
    return (
        (0, 0, cut, 1),
        (2, 0, small_rows, 1),
        (0, cut, in_rows - cut, 0),
        (1, 0, out_rows, 0),
    )


def places():
    ctx, seq = lax.axis_index("ctx"), lax.axis_index("seq")
    return lax.div(ctx, 2), lax.rem(ctx, 2), lax.div(seq, 2), lax.rem(seq, 2)


def device(y, x, z, core):
    return (2 * y + x, 2 * z + core)


def greet_square(depth):
    y, x, z, core = places()
    barrier = pltpu.get_barrier_semaphore()
    partners = [device(y, x, z, 1 - core), device(y, 1 - x, z, core)]
    partners.append(device(1 - y, x, z, core))
    for step in range(1, depth):
        partners.append(device(y, x, lax.rem(z + step, depth), core))
    for partner in partners:
        pl.semaphore_signal(barrier, inc=1, device_id=partner, device_id_type=MESH)
    pl.semaphore_wait(barrier, len(partners))


def gather_kernel(layers, depth, parts, *refs):
    local, whole = refs[: 3 * layers], refs[3 * layers : 6 * layers]
    own_sem, send_sem, recv_sem = refs[6 * layers :]
    y, x, z, core = places()
    greet_square(depth)
    own_copies = []
    for layer in range(layers):
        for array in range(3):
            copy = pltpu.make_async_copy(
                local[3 * layer + array],
                whole[3 * layer + array].at[y, x, z, core],
                own_sem.at[layer, array],
            )
            copy.start()
            own_copies.append(copy)
    sent = []
    used = [0] * layers

    def span(layer, part, block):
        array, first, rows, _ = parts[part]
        return whole[3 * layer + array].at[(*block, pl.ds(first, rows))]

    def send(layer, part, block, to, own=False):
        array, first, rows, _ = parts[part]
        source = (
            local[3 * layer + array].at[pl.ds(first, rows)]
            if own
            else span(layer, part, block)
        )
        copy = pltpu.make_async_remote_copy(
            source,
            span(layer, part, block),
            send_sem.at[layer, used[layer]],
            recv_sem.at[(layer, *block[:2], block[2], block[3], part)],
            device_id=to,
            device_id_type=MESH,
        )
        used[layer] += 1
        copy.start()
        sent.append(copy)

    def arrive(layer, part, block):
        pltpu.make_async_remote_copy(
            span(layer, part, block),
            span(layer, part, block),
            send_sem.at[layer, 0],
            recv_sem.at[(layer, *block[:2], block[2], block[3], part)],
            device_id=device(y, x, z, 1 - core),
            device_id_type=MESH,
        ).wait_recv()

    x_side, y_side = device(y, 1 - x, z, core), device(1 - y, x, z, core)
    sibling = device(y, x, z, 1 - core)
    everything = range(len(parts))
    line = [lax.rem(z + step, depth) for step in range(depth)]

    def begin(layer):
        block = (y, x, z, core)
        for part in everything:
            for to in (x_side, y_side):
                send(layer, part, block, to, own=True)
            for step in range(1, depth):
                to = device(y, x, line[step], core)
                send(layer, part, block, to, own=True)
            send(layer, part, block, sibling, own=True)

    def along(layer):
        for step in range(depth):
            for part in everything:
                block = (y, x, line[step], core)
                if step > 0:
                    arrive(layer, part, block)
                    for to in (x_side, y_side, sibling):
                        send(layer, part, block, to)
                if parts[part][3] == 1:
                    block, to = (y, 1 - x, line[step], core), y_side
                else:
                    block, to = (1 - y, x, line[step], core), x_side
                arrive(layer, part, block)
                send(layer, part, block, to)
                send(layer, part, block, sibling)

    def rest(layer):
        for step in range(depth):
            for part in everything:
                for other in (0, 1):
                    if parts[part][3] == 1:
                        block = (1 - y, x if other == 0 else 1 - x, line[step], core)
                    else:
                        block = (y if other == 0 else 1 - y, 1 - x, line[step], core)
                    arrive(layer, part, block)
                    send(layer, part, block, sibling)

    def finish(layer):
        for step in range(depth):
            for part in everything:
                for far_y in (y, 1 - y):
                    for far_x in (x, 1 - x):
                        arrive(layer, part, (far_y, far_x, line[step], 1 - core))

    for layer in range(layers):
        begin(layer)
        along(layer)
        rest(layer)
    for layer in range(layers):
        finish(layer)
    for copy in own_copies:
        copy.wait()
    for copy in sent:
        copy.wait_send()


def gather_call(depth, local):
    layers = len(local)
    flat = [array for layer in local for array in layer]
    parts = parts_of(*(array.shape[0] for array in local[0]))
    outs = [
        jax.ShapeDtypeStruct((2, 2, depth, 2) + array.shape, array.dtype)
        for array in flat
    ]
    sends = len(parts) * (2 + depth + 3 * (depth - 1) + 2 * depth + 2 * depth)
    dma = pltpu.SemaphoreType.DMA
    gathered = pl.pallas_call(
        functools.partial(gather_kernel, layers, depth, parts),
        out_shape=tuple(outs),
        in_specs=in_any(len(flat)),
        out_specs=tuple(in_any(len(flat))),
        scratch_shapes=[
            dma((layers, 3)),
            dma((layers, sends)),
            dma((layers, 2, 2, depth, 2, len(parts))),
        ],
        compiler_params=pltpu.CompilerParams(collective_id=2, has_side_effects=True),
        name="gather_weights",
    )(*flat)
    joined = [
        array.reshape((-1,) + piece.shape[1:]) for array, piece in zip(gathered, flat)
    ]
    return [joined[3 * layer : 3 * layer + 3] for layer in range(layers)]


def reduce_kernel(depth, parts, *refs):
    whole, outs = refs[:3], refs[3:6]
    pieces = len(parts)
    own = refs[6 : 6 + pieces]
    core_in = refs[6 + pieces : 6 + 2 * pieces]
    first_in = refs[6 + 2 * pieces : 6 + 3 * pieces]
    second_in = refs[6 + 3 * pieces : 6 + 4 * pieces]
    line_in = refs[6 + 4 * pieces : 6 + 5 * pieces]
    own_sem, send_sem, recv_sem = refs[6 + 5 * pieces :]
    y, x, z, core = places()
    greet_square(depth)
    line = [lax.rem(z + step + 1, depth) for step in range(depth)]
    x_side, y_side = device(y, 1 - x, z, core), device(1 - y, x, z, core)
    sibling = device(y, x, z, 1 - core)

    def part_of(part, step, side):
        array, first, rows, _ = parts[part]
        return whole[array].at[:, :, line[step], side, pl.ds(first, rows)]

    def local(part, step):
        return pltpu.make_async_copy(
            part_of(part, step, core), own[part].at[step], own_sem.at[step, part]
        )

    def remote(stage, part, step, source, target, to):
        return pltpu.make_async_remote_copy(
            source,
            target,
            send_sem.at[stage, step, part],
            recv_sem.at[stage, step, part],
            device_id=to,
            device_id_type=MESH,
        )

    def hop(stage, part, step):
        crosses_y = parts[part][3] == 1
        if stage == 0:
            return remote(
                0,
                part,
                step,
                part_of(part, step, 1 - core),
                core_in[part].at[step],
                sibling,
            )
        if stage == 1:
            source = (
                core_in[part].at[step, 1 - y]
                if crosses_y
                else core_in[part].at[step, :, 1 - x]
            )
            to = y_side if crosses_y else x_side
            return remote(1, part, step, source, first_in[part].at[step], to)
        if stage == 2:
            source = first_in[part].at[step, 1 - x if crosses_y else 1 - y]
            to = x_side if crosses_y else y_side
            return remote(2, part, step, source, second_in[part].at[step], to)
        to = device(y, x, line[step], core)
        return remote(
            3, part, step, second_in[part].at[step], line_in[part].at[step], to
        )

    def add(target, other, rows):
        @pl.loop(0, rows // 16)
        def _(r):
            here = pl.ds(pl.multiple_of(r * 16, 16), 16)
            target[here] = (
                target[here].astype(F32) + other[here].astype(F32)
            ).astype(BF16)

    def settle(stage, part, step):
        rows = parts[part][2]
        crosses_y = parts[part][3] == 1
        hop(stage, part, step).wait_recv()
        if stage == 0:
            local(part, step).wait()
            for far_y in (0, 1):
                for far_x in (0, 1):
                    add(
                        core_in[part].at[step, far_y, far_x],
                        own[part].at[step, far_y, far_x],
                        rows,
                    )
        elif stage == 1:
            for far in (0, 1):
                kept = (
                    core_in[part].at[step, y, far]
                    if crosses_y
                    else core_in[part].at[step, far, x]
                )
                add(first_in[part].at[step, far], kept, rows)
        elif stage == 2:
            add(
                second_in[part].at[step],
                first_in[part].at[step, x if crosses_y else y],
                rows,
            )

    everything = range(pieces)
    for step in range(depth):
        for part in everything:
            hop(0, part, step).start()
            local(part, step).start()
    for turn in range(depth + 2):
        for stage in range(3):
            step = turn - stage
            if 0 <= step < depth:
                for part in everything:
                    settle(stage, part, step)
                    if stage < 2 or step < depth - 1:
                        hop(stage + 1, part, step).start()
    for step in range(depth - 1):
        for part in everything:
            hop(3, part, step).wait_recv()
    for part in everything:
        array, first, rows, _ = parts[part]

        @pl.loop(0, rows // 16)
        def _(r):
            here = pl.ds(pl.multiple_of(r * 16, 16), 16)
            total = second_in[part][depth - 1, here].astype(F32)
            for step in range(depth - 1):
                total = total + line_in[part][step, here].astype(F32)
            there = pl.ds(pl.multiple_of(first + r * 16, 16), 16)
            outs[array][there] = total

    for step in range(depth):
        for part in everything:
            for stage in range(4):
                if stage < 3 or step < depth - 1:
                    hop(stage, part, step).wait_send()


def reduce_call(depth, whole):
    count = 8 * depth
    sizes = [array.shape[0] // count for array in whole]
    widths = [array.shape[1] for array in whole]
    parts = parts_of(*sizes)
    shaped = [
        array.reshape(2, 2, depth, 2, size, wide)
        for array, size, wide in zip(whole, sizes, widths)
    ]

    def buffers(lead):
        return [
            pltpu.VMEM(lead + (rows, widths[array]), BF16)
            for array, _, rows, _ in parts
        ]

    dma = pltpu.SemaphoreType.DMA
    return pl.pallas_call(
        functools.partial(reduce_kernel, depth, parts),
        out_shape=tuple(
            jax.ShapeDtypeStruct((size, wide), F32) for size, wide in zip(sizes, widths)
        ),
        in_specs=in_any(3),
        out_specs=tuple(in_vmem(3)),
        scratch_shapes=buffers((depth, 2, 2))
        + buffers((depth, 2, 2))
        + buffers((depth, 2))
        + buffers((depth,))
        + buffers((depth,))
        + [
            dma((depth, len(parts))),
            dma((4, depth, len(parts))),
            dma((4, depth, len(parts))),
        ],
        compiler_params=pltpu.CompilerParams(
            collective_id=3, has_side_effects=True, vmem_limit_bytes=VMEM_BYTES
        ),
        name="reduce_gradients",
    )(*shaped)


def round_up(value, step):
    return -(-value // step) * step


def on_device(
    mesh,
    hidden_in,
    cotangent,
    norm_gain,
    in_weight,
    conv_weight,
    conv_bias,
    x_weight,
    dt_weight,
    dt_bias,
    a_log,
    skip_gain,
    out_weight,
):
    layers = norm_gain.shape[0]
    rows, width = hidden_in.shape
    taps, channels = conv_weight.shape[1:]
    states = a_log.shape[2]
    rank = dt_weight.shape[1]
    small = rank + 2 * states
    devices, count = mesh.shape["ctx"] * mesh.shape["seq"], mesh.shape["seq"]
    inner = channels * devices
    gains = norm_gain.shape[1]
    at = Names(states, taps)
    cfg = (rows, inner, states, taps, rank, count)
    per_channel = small + rank + at.count
    packed = per_channel * channels + gains
    small_rows = round_up(packed, 16 * 1024) // 1024
    depth = count // 2
    by_kernel = (
        mesh.shape["ctx"] == 4
        and count % 2 == 0
        and in_weight.shape[2] % 64 == 0
        and out_weight.shape[2] % 16 == 0
    )

    def pack(layer):
        by_row = jnp.concatenate(
            [
                x_weight[layer].T,
                dt_weight[layer],
                a_log[layer].T,
                conv_weight[layer],
                conv_bias[layer][None],
                dt_bias[layer][None],
                skip_gain[layer][None],
            ],
            0,
        )
        flat = jnp.concatenate([by_row.reshape(-1), norm_gain[layer]])
        flat = jnp.pad(flat, (0, small_rows * 1024 - packed))
        return flat.reshape(small_rows, 1024)

    local = [
        (in_weight[layer].T, out_weight[layer].T, pack(layer))
        for layer in range(layers)
    ]
    if by_kernel:
        gathered = gather_call(depth, local)
    else:
        gathered = [
            [lax.all_gather(array, ("ctx", "seq"), axis=0, tiled=True) for array in layer]
            for layer in local
        ]

    weights = []
    for win, wout, pack_all in gathered:
        flat = pack_all.reshape(devices, small_rows * 1024)
        by_row = flat[:, : per_channel * channels].reshape(
            devices, per_channel, channels
        )
        by_row = by_row.transpose(1, 0, 2).reshape(per_channel, inner)
        gain = flat[:, per_channel * channels : packed].reshape(1, width).astype(F32)
        xw = by_row[:small]
        dtw = jnp.pad(by_row[small : small + rank], ((0, small - rank), (0, 0)))
        vec = by_row[small + rank :].astype(F32)
        vec = jnp.concatenate([-jnp.exp(vec[:states]), vec[states:]], 0)
        vec = jnp.pad(vec, ((0, at.padded - at.count), (0, 0)))
        weights.append((gain, win, xw, dtw, vec, wout))

    stream = hidden_in.astype(F32)
    streams, saved = [], []
    for layer in range(layers):
        streams.append(stream)
        stream, *kept = forward_call(cfg, stream, *weights[layer])
        saved.append(kept)
    stream_grad = cotangent.astype(F32)
    grads = [None] * layers
    for layer in reversed(range(layers)):
        stream_grad, g_in, g_out, g_x, g_dt, g_vec, g_gain = backward_call(
            cfg, stream_grad, streams[layer], *weights[layer], saved[layer]
        )
        by_row = jnp.concatenate([g_x, g_dt[:rank], g_vec[: at.count]], 0)
        by_row = by_row.reshape(per_channel, devices, channels).transpose(1, 0, 2)
        flat = jnp.concatenate(
            [
                by_row.reshape(devices, per_channel * channels),
                g_gain[0].reshape(devices, gains),
            ],
            1,
        )
        flat = jnp.pad(flat, ((0, 0), (0, small_rows * 1024 - packed)))
        g_small = flat.astype(BF16).reshape(devices * small_rows, 1024)
        if by_kernel:
            summed = reduce_call(depth, (g_in, g_out, g_small))
        else:
            summed = [
                lax.psum_scatter(
                    array.astype(F32), ("ctx", "seq"), scatter_dimension=0, tiled=True
                )
                for array in (g_in, g_out, g_small)
            ]
        s_in, s_out, s_small = summed
        flat = s_small.reshape(-1)
        by_row = flat[: per_channel * channels].reshape(per_channel, channels)
        s_x, s_dt, s_vec = (
            by_row[:small],
            by_row[small : small + rank],
            by_row[small + rank :],
        )
        grads[layer] = (
            flat[per_channel * channels : packed],
            s_in.T,
            s_vec[at.conv : at.conv + taps],
            s_vec[at.conv_b],
            s_x.T,
            s_dt,
            s_vec[at.dt_b],
            s_vec[:states].T,
            s_vec[at.skip],
            s_out.T,
        )
    stacked = tuple(
        jnp.stack([grads[layer][member] for layer in range(layers)], 0)
        for member in range(10)
    )
    return (stream.astype(BF16), stream_grad) + stacked


def solution(mesh):
    split = ("ctx", "seq")
    tokens, last = P(split, None), P(None, split)
    middle, third = P(None, split, None), P(None, None, split)
    weights = (last, third, third, last, middle, third, last, middle, last, third)
    return jax.shard_map(
        functools.partial(on_device, mesh),
        mesh=mesh,
        in_specs=(tokens, tokens) + weights,
        out_specs=(tokens, tokens) + weights,
        check_vma=False,
    )
```

time: 5560 us -> 630 us (0.11); the launches traced: 5480 us -> 621 us
  other arithmetic: 1640 us -> 13.6 us
  waiting for transfers between devices: 1520 us -> 0 us
  local copies, waits for them, and re-layouts: 1510 us -> 38.9 us
  Pallas kernels: 0 us -> 567 us
  blocking collectives: 528 us -> 0 us
  matrix products: 223 us -> 0 us
    reduce_scatter x6 -> x0, waiting for transfers between devices: 937 us -> none  [the longest x2 372 us: on_device(): lax.psum_scatter(g_in, ('ctx', 'seq'), scatter_dimension=1, tiled=True)]
    reduce_sum x771 -> x0, other arithmetic: 674 us -> none  [the longest x512 281 us: row_step(): in_row[:, None] * (step_row * act_row)[None, :]]
    pallas_call x0 -> x7, Pallas kernels: none -> 567 us  [the longest x1 179 us: gather_call(): pl.pallas_call(functools.partial(gather_kernel, layers, depth, parts), ou...]
    unnamed x26 -> x0, waiting for transfers between devices: 563 us -> none
    while x928 -> x0, other arithmetic: 477 us -> none
    all_gather x12 -> x0, blocking collectives: 443 us -> none  [the longest x2 105 us: on_device(): lax.all_gather(conv_weight[layer_idx], ('ctx', 'seq'), axis=1, tiled=True)]
    concatenate x224 -> x6, local copies, waits for them, and re-layouts: 364 us -> 1.47 us  [the longest x2 1.02 us: on_device(): by_row = jnp.concatenate([g_x, g_dt[:rank], g_vec[:at.count]], 0)]
    while x3876 -> x0, local copies, waits for them, and re-layouts: 352 us -> none
where the time goes in v1:
time: 630 us; the launch traced here: 621 us
  Pallas kernels  567 us (90%)
  local copies, waits for them, and re-layouts  38.9 us (6%)
  other arithmetic  13.6 us (2%)
    pallas_call x1, Pallas kernels, gather_call(): pl.pallas_call(functools.partial(gather_kernel, layers, depth, parts), ou...  179 us
    pallas_call x2, Pallas kernels, backward_call(): pl.pallas_call(functools.partial(backward_kernel, cfg), out_shape=(shape(...  147 us
    pallas_call x2, Pallas kernels, reduce_call(): pl.pallas_call(functools.partial(reduce_kernel, depth, parts), out_shape=...  146 us
    pallas_call x2, Pallas kernels, forward_call(): pl.pallas_call(functools.partial(forward_kernel, cfg), out_shape=(shape(s...  93.7 us
    unnamed x51, local copies, waits for them, and re-layouts  13.4 us

profile of v1, /device:TPU:0, one launch (start us, length us, event | category | flops | bytes accessed | tf_op | source)
XLA Modules:
  0.0 620.8 jit_solution(10930696870562455864)
XLA Ops:
  0.7 2.2 convert_element_type.41.stream_ref
  3.0 1.1 fusion.16
  9.9 179.2 %gather_weights.1 = (bf16[2,2,4,2,128,1024]{5,4,3,2,1,0:T(8,128)(2,1)}, bf16[2,2,4,2,32,2048]{5,4,3,2,1,0:T(8,128)(2,1)}, bf16[2,2,4,2,16,1024]{5,4,3,2,1,0:T(8,...) custom-call(bf16[128,1024]{1,0:T(8,128)(2,1)} %bitcast.146, ...), custom_call_target="tpu_custom_call" | custom-call | tf_op jit(solution)/shard_map/gather_weights/pallas_call | solution.py:981
  189.2 1.8 copy.81
  191.8 1.1 reshape.187
  193.3 1.0 copy.63.xw_ref
  197.0 45.5 %forward_layer.2 = (f32[256,1024]{1,0:T(8,128)}, bf16[272,2048]{1,0:T(8,128)(2,1)}, f32[256,2048]{1,0:T(8,128)}, bf16[256,2048]{1,0:T(8,128)(2,1)}, f32[256,96]{...) custom-call(f32[256,1024]{1,0:T(8,128)} %convert_element_type.41.str, ...), custom_call_target="tpu_custom_call" | custom-call | tf_op jit(solution)/shard_map/forward_layer/pallas_call | solution.py:726
  242.5 1.8 copy.82
  245.2 1.1 reshape.190
  246.7 1.0 copy.68.xw_ref
  250.4 48.1 %forward_layer.3 = (f32[256,1024]{1,0:T(8,128)}, bf16[272,2048]{1,0:T(8,128)(2,1)}, f32[256,2048]{1,0:T(8,128)}, bf16[256,2048]{1,0:T(8,128)(2,1)}, f32[256,96]{...) custom-call(f32[256,1024]{1,0:T(8,128)} %get-tuple-element.59.stream, ...), custom_call_target="tpu_custom_call" | custom-call | tf_op jit(solution)/shard_map/forward_layer/pallas_call | solution.py:726
  298.5 2.1 convert_element_type.48
  300.6 1.1 convert_element_type.49.sgrad_ref
  301.7 74.1 %backward_layer.2 = (f32[256,1024]{1,0:T(8,128)}, bf16[4096,1024]{1,0:T(8,128)(2,1)}, bf16[1024,2048]{1,0:T(8,128)(2,1)}, f32[96,2048]{1,0:T(8,128)}, f32[96,204...) custom-call(f32[256,1024]{1,0:T(8,128)} %convert_element_type.49.sgrad_ref, ...), custom_call_target="tpu_custom_call" | custom-call | tf_op jit(solution)/shard_map/backward_layer/pallas_call | solution.py:776
  375.9 73.2 %backward_layer.3 = (f32[256,1024]{1,0:T(8,128)}, bf16[4096,1024]{1,0:T(8,128)(2,1)}, bf16[1024,2048]{1,0:T(8,128)(2,1)}, f32[96,2048]{1,0:T(8,128)}, f32[96,204...) custom-call(f32[256,1024]{1,0:T(8,128)} %get-tuple-element.72.sgrad_ref, ...), custom_call_target="tpu_custom_call" | custom-call | tf_op jit(solution)/shard_map/backward_layer/pallas_call | solution.py:776
  450.0 1.1 slice.416
  453.6 1.6 copy.85
  455.2 72.8 %reduce_gradients.3 = (f32[128,1024]{1,0:T(8,128)}, f32[32,2048]{1,0:T(8,128)}, f32[16,1024]{1,0:T(8,128)}) custom-call(bf16[2,2,4,2,128,1024]{5,4,3,2,1,0:T(8,128)(2,1)} %bitcast.123, bf16[2,2,4,2,32,2048]{5,4,3,2,1,0:T(8,128)(2,1)} %bitcast.135, bf16[2,2,4,2,16,1024]{5,4,3,2,1,0:T(8,128)(2,1)} %bitcast.136), custom_call_target="tpu_custom_call" | custom-call | tf_op jit(solution)/shard_map/reduce_gradients/pallas_call | solution.py:1150
  530.7 1.1 slice.417
  534.3 1.6 copy.83
  535.9 73.4 %reduce_gradients.2 = (f32[128,1024]{1,0:T(8,128)}, f32[32,2048]{1,0:T(8,128)}, f32[16,1024]{1,0:T(8,128)}) custom-call(bf16[2,2,4,2,128,1024]{5,4,3,2,1,0:T(8,128)(2,1)} %bitcast.122, bf16[2,2,4,2,32,2048]{5,4,3,2,1,0:T(8,128)(2,1)} %bitcast.134, bf16[2,2,4,2,16,1024]{5,4,3,2,1,0:T(8,128)(2,1)} %bitcast.137), custom_call_target="tpu_custom_call" | custom-call | tf_op jit(solution)/shard_map/reduce_gradients/pallas_call | solution.py:1150
  610.8 1.1 pad_maximum_fusion
  612.0 1.3 copy.75
  619.4 1.0 copy.88
  (154 shorter events, 29.7 us)
Async XLA Ops:
  0.6 4.3 copy-start.7
  0.7 5.0 copy-start.15
  0.7 5.0 copy-start.11
  0.7 5.0 copy-start.12
  0.7 5.1 copy-start.13
  0.7 5.2 copy-start.14
  0.7 5.3 copy-start.16
  0.7 5.4 copy-start.17
  0.7 5.5 copy-start.18
  250.4 50.3 %copy-start.3 = (bf16[256,1024]{1,0:T(8,128)(2,1)S(1)}, bf16[256,1024]{1,0:T(8,128)(2,1)}, u32[]{:S(2)}) copy-start(bf16[256,1024]{1,0:T(8,128)(2,1)} %param.13) | copy-start | bytes 1572868
  375.9 74.1 %copy-start.10 = (f32[24,2048]{1,0:T(8,128)S(1)}, f32[24,2048]{1,0:T(8,128)}, u32[]{:S(2)}) copy-start(f32[24,2048]{1,0:T(8,128)} %get-tuple-element.93) | copy-start | bytes 589828
  375.9 75.2 %copy-start.2 = (f32[96,2048]{1,0:T(8,128)S(1)}, f32[96,2048]{1,0:T(8,128)}, u32[]{:S(2)}) copy-start(f32[96,2048]{1,0:T(8,128)} %get-tuple-element.91) | copy-start | bytes 2359300
  455.2 76.7 %copy-start.1 = (f32[96,2048]{1,0:T(8,128)S(1)}, f32[96,2048]{1,0:T(8,128)}, u32[]{:S(2)}) copy-start(f32[96,2048]{1,0:T(8,128)} %get-tuple-element.84) | copy-start | bytes 2359300
  535.9 74.9 %copy-start.4 = (f32[128,1024]{1,0:T(8,128)S(1)}, f32[128,1024]{1,0:T(8,128)}, u32[]{:S(2)}) copy-start(f32[128,1024]{1,0:T(8,128)} %get-tuple-element.97) | copy-start | bytes 1572868
  610.8 2.5 copy-start.5
  610.8 2.6 copy-start.6
  612.0 6.6 %copy-start.8 = (f32[32,2048]{1,0:T(8,128)S(1)}, f32[32,2048]{1,0:T(8,128)}, u32[]{:S(2)}) copy-start(f32[32,2048]{1,0:T(8,128)} %get-tuple-element.99) | copy-start | bytes 786436
  612.0 6.6 %copy-start.9 = (f32[32,2048]{1,0:T(8,128)S(1)}, f32[32,2048]{1,0:T(8,128)}, u32[]{:S(2)}) copy-start(f32[32,2048]{1,0:T(8,128)} %get-tuple-element.98) | copy-start | bytes 786436
  612.0 7.4 %copy-start = (f32[256,1024]{1,0:T(8,128)S(1)}, f32[256,1024]{1,0:T(8,128)}, u32[]{:S(2)}) copy-start(f32[256,1024]{1,0:T(8,128)} %get-tuple-element.165) | copy-start | bytes 3145732

commit v2 on v1

--- a/solution.py
+++ b/solution.py
@@ -1,4 +1,6 @@
+import collections
 import functools
+import types
 
 import jax
 import jax.numpy as jnp
@@ -84,150 +86,242 @@
 
 
 class Names:
-    def __init__(self, states, taps):
+    def __init__(self, states, taps, rank):
+        self.small = rank + 2 * states
+        self.dt = self.small
+        self.vec = self.small + rank
+        self.count = self.vec + states + taps + 4
+        self.rows = -(-self.count // 16) * 16
         self.conv = states
         self.conv_b = states + taps
         self.dt_b = states + taps + 1
         self.skip = states + taps + 2
-        self.count = states + taps + 3
-        self.padded = -(-self.count // 8) * 8
-
-
-def forward_kernel(
-    cfg,
-    stream_ref,
-    gain_ref,
-    win_ref,
-    xw_ref,
-    dtw_ref,
-    vec_ref,
-    wout_ref,
-    new_ref,
-    pad_ref,
-    gate_ref,
-    act_ref,
-    sp_ref,
-    pre_ref,
-    h_hbm,
-    y_ref,
-    mixed_ref,
-    normed_s,
-    padf_s,
-    halo_s,
-    dt_s,
-    dx_s,
-    bb_s,
-    cd_s,
-    hs,
-    own_sum,
-    sum_s,
-    own_end,
-    end_s,
-    halo_sem,
-    sum_send,
-    sum_recv,
-    end_send,
-    end_recv,
-    h_sem,
-):
-    rows, inner, states, taps, rank, count = cfg
-    at = Names(states, taps)
-    ctx, me = lax.axis_index("ctx"), lax.axis_index("seq")
-    groups, steps = inner // GROUP, rows // CHUNK
+        self.gain = states + taps + 3
+
+
+def load_small(at, sw_ref, vec_s, dtw_s):
+    states, rank = at.conv, at.vec - at.dt
+    vec_s[...] = sw_ref[pl.ds(at.vec, at.rows - at.vec), :].astype(F32)
+    vec_s[pl.ds(0, states), :] = -jnp.exp(vec_s[pl.ds(0, states), :])
+    dtw_s[pl.ds(0, rank), :] = sw_ref[pl.ds(at.dt, rank), :]
+    dtw_s[pl.ds(rank, at.small - rank), :] = jnp.zeros(
+        (at.small - rank, dtw_s.shape[1]), BF16
+    )
+
+
+def gain_pick(channels):
+    gains = channels // 2
+    row = lax.broadcasted_iota(jnp.int32, (256, 128), 0)
+    col = lax.broadcasted_iota(jnp.int32, (256, 128), 1)
+    place = lax.div(col, gains) * channels + lax.rem(col, gains)
+    return (row == place).astype(F32).astype(BF16)
+
+
+def gain_row(at, channels, vec_s):
+    pick = gain_pick(channels)
+    row = vec_s[pl.ds(at.gain // 8 * 8, 8), :].astype(BF16)
+    tiles = [
+        dot(row[:, 256 * i : 256 * i + 256], pick) for i in range(row.shape[1] // 256)
+    ]
+    gain = jnp.concatenate(tiles, 1)
+    return gain[at.gain % 8 : at.gain % 8 + 1]
+
+
+def merge_small(channels, blocks, sw_ref):
+    each = 128 // channels
+    rows = blocks.shape[1]
+    owner = lax.div(lax.broadcasted_iota(jnp.int32, (rows, 128), 1), channels)
+
+    @pl.loop(0, sw_ref.shape[1] // 128)
+    def _(j):
+        held = [blocks[j * each + part].astype(F32) for part in range(each)]
+        for fold in range(each):
+            tile = None
+            for part in range(each):
+                shift = (part - fold) * channels % 128
+                moved = pltpu.roll(held[part], shift, 1) if shift else held[part]
+                tile = moved if tile is None else jnp.where(owner == part, moved, tile)
+            sw_ref[pl.ds(fold * rows, rows), lanes(j, 128)] = tile.astype(BF16)
+
+
+def split_small(channels, full_ref, blocks):
+    each = 128 // channels
+    rows = blocks.shape[1]
+    owner = lax.div(lax.broadcasted_iota(jnp.int32, (rows, 128), 1), channels)
+
+    @pl.loop(0, full_ref.shape[1] // 128)
+    def _(j):
+        held = [
+            full_ref[pl.ds(fold * rows, rows), lanes(j, 128)] for fold in range(each)
+        ]
+        for part in range(each):
+            tile = None
+            for fold in range(each):
+                shift = (fold - part) * channels % 128
+                moved = pltpu.roll(held[fold], shift, 1) if shift else held[fold]
+                tile = moved if tile is None else jnp.where(owner == fold, moved, tile)
+            blocks[j * each + part] = tile.astype(BF16)
+
+
+def places():
+    ctx, seq = lax.axis_index("ctx"), lax.axis_index("seq")
+    return lax.div(ctx, 2), lax.rem(ctx, 2), lax.div(seq, 2), lax.rem(seq, 2)
+
+
+def device(y, x, z, core):
+    return (2 * y + x, 2 * z + core)
+
+
+def square_partners(depth):
+    y, x, z, core = places()
+    partners = [device(y, x, z, 1 - core), device(y, 1 - x, z, core)]
+    partners.append(device(1 - y, x, z, core))
+    for step in range(1, depth):
+        partners.append(device(y, x, lax.rem(z + step, depth), core))
+    return partners
+
+
+def greet_square(depth):
     barrier = pltpu.get_barrier_semaphore()
-
-    def greet(j, _):
-        pl.semaphore_signal(barrier, inc=1, device_id=(ctx, j), device_id_type=MESH)
-        return 0
-
-    lax.fori_loop(0, me, greet, 0)
-    stream = stream_ref[...]
-    scale = lax.rsqrt(jnp.mean(stream * stream, axis=1, keepdims=True) + EPS)
-    normed_s[...] = (stream * scale * gain_ref[...]).astype(BF16)
-
-    @pl.loop(0, inner // GROUP)
-    def _(i):
-        low = dot(normed_s[...], win_ref[lanes(i, GROUP), :], NT).astype(BF16)
-        pad_ref[pl.ds(HALO, rows), lanes(i, GROUP)] = low
-        padf_s[pl.ds(HALO, rows), lanes(i, GROUP)] = low.astype(F32)
-
-    @pl.when(me < count - 1)
-    def _():
-        pl.semaphore_wait(barrier, count - 1 - me)
-
-    def edge():
-        return pltpu.make_async_remote_copy(
-            pad_ref.at[pl.ds(rows, HALO)],
-            halo_s,
-            halo_sem.at[0],
-            halo_sem.at[1],
-            device_id=(ctx, jnp.minimum(me + 1, count - 1)),
+    partners = square_partners(depth)
+    for partner in partners:
+        pl.semaphore_signal(barrier, inc=1, device_id=partner, device_id_type=MESH)
+    pl.semaphore_wait(barrier, len(partners))
+
+
+class Gather:
+    def __init__(self, depth, pieces, own_sem, send_sem, recv_sem):
+        self.depth, self.pieces = depth, pieces
+        self.own_sem, self.send_sem, self.recv_sem = own_sem, send_sem, recv_sem
+        self.y, self.x, self.z, self.core = places()
+        self.used = [0] * len(pieces)
+        self.sent = []
+        turn = 1 - 2 * lax.div(self.z, max(depth // 2, 1))
+        self.line = [
+            lax.rem(self.z + turn * step + depth, depth) for step in range(depth)
+        ]
+        y, x, z, core = self.y, self.x, self.z, self.core
+        self.x_side, self.y_side = device(y, 1 - x, z, core), device(1 - y, x, z, core)
+        self.sibling = device(y, x, z, 1 - core)
+
+    @staticmethod
+    def sends(depth):
+        return 3 + depth - 1 + 3 * (depth - 1) + 2 * depth + 2 * depth
+
+    def slot(self, y, x, z, core):
+        return ((2 * y + x) * self.depth + z) * 2 + core
+
+    def span(self, item, slot):
+        _, whole, first, rows, _ = self.pieces[item]
+        return whole.at[slot, pl.ds(first, rows)]
+
+    def send(self, item, slot, to, own=False):
+        local, _, first, rows, _ = self.pieces[item]
+        copy = pltpu.make_async_remote_copy(
+            local.at[pl.ds(first, rows)] if own else self.span(item, slot),
+            self.span(item, slot),
+            self.send_sem.at[item, self.used[item]],
+            self.recv_sem.at[item, slot],
+            device_id=to,
             device_id_type=MESH,
         )
-
-    @pl.when(me < count - 1)
-    def _():
-        edge().start()
-
-    @pl.loop(0, inner // GROUP)
-    def _(i):
-        gate_ref[:, lanes(i, GROUP)] = dot(
-            normed_s[...], win_ref[lanes(i + inner // GROUP, GROUP), :], NT
-        )
-
-    @pl.when(me > 0)
-    def _():
-        edge().wait_recv()
-
-    @pl.when(me == 0)
-    def _():
-        halo_s[...] = jnp.zeros_like(halo_s)
-
-    pad_ref[pl.ds(0, HALO), :] = halo_s[...]
-    padf_s[pl.ds(0, HALO), :] = halo_s[...].astype(F32)
-
-    @pl.loop(0, inner // GROUP)
-    def _(i):
-        here = lanes(i, GROUP)
-        total = vec_ref[pl.ds(at.conv_b, 1), here]
-        for k in range(taps):
-            total = (
-                total
-                + vec_ref[pl.ds(at.conv + k, 1), here]
-                * padf_s[pl.ds(HALO - taps + 1 + k, rows), here]
-            )
-        act_ref[:, here] = (total * sigmoid(total)).astype(BF16)
-
-    small = dot(act_ref[...], xw_ref[...], NT)
-    sp_ref[...] = small
-    small_low = small.astype(BF16)
-
-    @pl.loop(0, inner // GROUP)
-    def _(i):
-        here = lanes(i, GROUP)
-        before = dot(small_low, dtw_ref[:, here]) + vec_ref[pl.ds(at.dt_b, 1), here]
-        step = softplus(before)
-        pre_ref[:, here] = before
-        dt_s[:, here] = step
-        dx_s[:, here] = step * act_ref[:, here].astype(F32)
-        keep_sum(own_sum, i, step)
-
-    def sums(j):
+        self.used[item] += 1
+        copy.start()
+        self.sent.append(copy)
+
+    def arrive(self, item, slot):
+        pltpu.make_async_remote_copy(
+            self.span(item, slot),
+            self.span(item, slot),
+            self.send_sem.at[item, 0],
+            self.recv_sem.at[item, slot],
+            device_id=self.sibling,
+            device_id_type=MESH,
+        ).wait_recv()
+
+    def own_copy(self, item):
+        local, _, first, rows, _ = self.pieces[item]
+        mine = self.slot(self.y, self.x, self.z, self.core)
+        return pltpu.make_async_copy(
+            local.at[pl.ds(first, rows)], self.span(item, mine), self.own_sem.at[item]
+        )
+
+    def begin(self, item):
+        mine = self.slot(self.y, self.x, self.z, self.core)
+        self.own_copy(item).start()
+        for to in (self.x_side, self.y_side):
+            self.send(item, mine, to, own=True)
+        for step in range(1, self.depth):
+            to = device(self.y, self.x, self.line[step], self.core)
+            self.send(item, mine, to, own=True)
+        self.send(item, mine, self.sibling, own=True)
+
+    def along(self, item, step):
+        slot = self.slot(self.y, self.x, self.line[step], self.core)
+        self.arrive(item, slot)
+        for to in (self.x_side, self.y_side, self.sibling):
+            self.send(item, slot, to)
+
+    def near(self, item, step):
+        if self.pieces[item][4]:
+            slot = self.slot(self.y, 1 - self.x, self.line[step], self.core)
+            to = self.y_side
+        else:
+            slot = self.slot(1 - self.y, self.x, self.line[step], self.core)
+            to = self.x_side
+        self.arrive(item, slot)
+        self.send(item, slot, to)
+        self.send(item, slot, self.sibling)
+
+    def far(self, item, step, other):
+        y, x = 1 - self.y, 1 - self.x
+        if self.pieces[item][4]:
+            x = x if other else self.x
+        else:
+            y = y if other else self.y
+        slot = self.slot(y, x, self.line[step], self.core)
+        self.arrive(item, slot)
+        self.send(item, slot, self.sibling)
+
+    def settle(self, item):
+        self.own_copy(item).wait()
+        for step in range(self.depth):
+            for y in (self.y, 1 - self.y):
+                for x in (self.x, 1 - self.x):
+                    self.arrive(item, self.slot(y, x, self.line[step], 1 - self.core))
+
+    def turns(self, items):
+        order = [("near", 0)]
+        for step in range(1, self.depth):
+            order.append(("along", step))
+            order.append(("near", step))
+            if step >= 2:
+                order.append(("far", step - 2, 1))
+            order.append(("far", step - 1, 0))
+        for step in range(max(self.depth - 2, 0), self.depth):
+            if step == self.depth - 1:
+                order.append(("far", step, 0))
+            order.append(("far", step, 1))
+        actions = []
+        for name, *rest in order:
+            for item in items:
+                actions.append(functools.partial(getattr(self, name), item, *rest))
+        return actions
+
+    def finish(self):
+        for copy in self.sent:
+            copy.wait_send()
+
+
+def chain(count, me, ctx, own_sum, sum_s, own_end, end_s, sems):
+    sum_send, sum_recv, end_send, end_recv = sems
+
+    def sums(j, slot):
         return pltpu.make_async_remote_copy(
             own_sum,
-            sum_s.at[me],
+            sum_s.at[slot],
             sum_send.at[j],
-            sum_recv.at[me],
-            device_id=(ctx, j),
-            device_id_type=MESH,
-        )
-
-    def sums_from(j):
-        return pltpu.make_async_remote_copy(
-            own_sum,
-            sum_s.at[j],
-            sum_send.at[j],
-            sum_recv.at[j],
+            sum_recv.at[slot],
             device_id=(ctx, j),
             device_id_type=MESH,
         )
@@ -242,104 +336,331 @@
             device_id_type=MESH,
         )
 
-    def each(first, last, act):
-        def body(j, _):
-            act(j)
-            return 0
-
-        lax.fori_loop(first, last, body, 0)
-
-    each(me + 1, count, lambda j: sums(j).start())
+    return sums, ends
+
+
+def each(first, last, act):
+    def body(j, _):
+        act(j)
+        return 0
+
+    lax.fori_loop(first, last, body, 0)
+
+
+def forward_kernel(cfg, mode, names, *refs):
+    r = types.SimpleNamespace(**dict(zip(names, refs)))
+    rows, inner, states, taps, rank, count, channels = cfg
+    at = Names(states, taps, rank)
+    ctx, me = lax.axis_index("ctx"), lax.axis_index("seq")
+    groups, steps, tiles = inner // GROUP, rows // CHUNK, inner // GROUP
+    depth = count // 2
+    width = r.stream.shape[1]
+    barrier = pltpu.get_barrier_semaphore()
+
+    def greet(to):
+        pl.semaphore_signal(barrier, inc=1, device_id=to, device_id_type=MESH)
+
+    queue = collections.deque()
+
+    def weave(times):
+        for _ in range(min(times, len(queue))):
+            queue.popleft()()
+
+    if mode == "given":
+        each(0, me, lambda j: greet((ctx, j)))
+    else:
+        each(0, me, lambda j: greet((ctx, j)))
+        each(me + 1, count, lambda j: greet((ctx, j)))
+        y, x, z, core = places()
+        greet(device(y, 1 - x, z, core))
+        greet(device(1 - y, x, z, core))
+
+    if mode != "first":
+        half = r.win_hbm.shape[0] // 2
+        halves = [
+            pltpu.make_async_copy(
+                r.win_hbm.at[pl.ds(k * half, half)],
+                r.win_s.at[pl.ds(k * half, half)],
+                r.load_sem.at[k],
+            )
+            for k in range(2)
+        ]
+        if mode == "later":
+            small_copy = pltpu.make_async_copy(r.gsm_hbm, r.gsm_s, r.load_sem.at[2])
+            small_copy.start()
+        for copy in halves:
+            copy.start()
+    if mode == "given":
+        out_copy = pltpu.make_async_copy(r.wout_hbm, r.wout_s, r.load_sem.at[2])
+        out_copy.start()
+
+    stream = r.stream[...]
+    scale = lax.rsqrt(jnp.mean(stream * stream, axis=1, keepdims=True) + EPS)
+    stores = []
+
+    if mode == "given":
+
+        @pl.when(me < count - 1)
+        def _():
+            pl.semaphore_wait(barrier, count - 1 - me)
+
+    else:
+        pl.semaphore_wait(barrier, count + 1)
+        pieces = []
+
+        def add_piece(local, whole, cuts):
+            start = len(pieces)
+            total = local.shape[0]
+            for k, last_y in enumerate(cuts):
+                piece = total // len(cuts)
+                pieces.append((local, whole, k * piece, piece, last_y))
+            return list(range(start, len(pieces)))
+
+        first_items, next_items = [], []
+        if mode == "first":
+            first_items = add_piece(r.own_in, r.win_s, (1, 0))
+            first_items += add_piece(r.own_small, r.gsm_s, (1,))
+        out_items = add_piece(r.own_out, r.wout_s, (1, 0))
+        if mode == "first":
+            next_items = add_piece(r.next_in, r.win2_all, (1, 0))
+            next_items += add_piece(r.next_small, r.gsm2_all, (0,))
+        gather = Gather(depth, pieces, r.own_sem, r.send_sem, r.recv_sem)
+
+        def begin(items):
+            for item in items:
+                gather.begin(item)
+
+        def settle(items):
+            for item in items:
+                gather.settle(item)
+
+        def keep(source, target, slot):
+            copy = pltpu.make_async_copy(source, target, r.store_sem.at[slot])
+            copy.start()
+            stores.append(copy)
+
+        if mode == "first":
+            begin(first_items)
+            turns = gather.turns(first_items)
+            for k, turn in enumerate(turns):
+                if k == len(turns) // 2:
+                    begin(out_items + next_items)
+                turn()
+            settle(first_items)
+            keep(r.win_s, r.win_all, 1)
+            turns = gather.turns(out_items)
+            queue.extend(gather.turns(out_items + next_items))
+        else:
+            begin(out_items)
+            queue.extend(gather.turns(out_items))
+        queue.append(lambda: settle(out_items))
+        queue.append(lambda: keep(r.wout_s, r.wout_all, 0))
+        if mode == "first":
+            queue.append(lambda: settle(next_items))
+        if mode == "later":
+            small_copy.wait()
+        merge_small(channels, r.gsm_s, r.sw)
+    pace = -(-len(queue) // 21)
+
+    load_small(at, r.sw, r.vec_s, r.dtw_s)
+    r.normed_s[...] = (stream * scale * gain_row(at, channels, r.vec_s)).astype(BF16)
+    per_tile = GROUP // r.win_s.shape[1]
+
+    def win_tile(i):
+        return r.win_s[pl.ds(i * per_tile, per_tile)].reshape(GROUP, width)
+
+    if mode != "first":
+        halves[0].wait()
+
+    @pl.loop(0, tiles)
+    def _(i):
+        low = dot(r.normed_s[...], win_tile(i), NT).astype(BF16)
+        r.pad[pl.ds(HALO, rows), lanes(i, GROUP)] = low
+        r.padf_s[pl.ds(HALO, rows), lanes(i, GROUP)] = low.astype(F32)
+
+    def edge():
+        return pltpu.make_async_remote_copy(
+            r.pad.at[pl.ds(rows, HALO)],
+            r.halo_s,
+            r.halo_sem.at[0],
+            r.halo_sem.at[1],
+            device_id=(ctx, jnp.minimum(me + 1, count - 1)),
+            device_id_type=MESH,
+        )
+
+    @pl.when(me < count - 1)
+    def _():
+        edge().start()
+
+    weave(pace)
+    if mode != "first":
+        halves[1].wait()
+
+    @pl.loop(0, tiles)
+    def _(i):
+        r.gate[:, lanes(i, GROUP)] = dot(r.normed_s[...], win_tile(i + tiles), NT)
+
+    weave(pace)
+
+    @pl.when(me > 0)
+    def _():
+        edge().wait_recv()
+
+    @pl.when(me == 0)
+    def _():
+        r.halo_s[...] = jnp.zeros_like(r.halo_s)
+
+    r.pad[pl.ds(0, HALO), :] = r.halo_s[...]
+    r.padf_s[pl.ds(0, HALO), :] = r.halo_s[...].astype(F32)
+
+    @pl.loop(0, tiles)
+    def _(i):
+        here = lanes(i, GROUP)
+        total = r.vec_s[pl.ds(at.conv_b, 1), here]
+        for k in range(taps):
+            total = (
+                total
+                + r.vec_s[pl.ds(at.conv + k, 1), here]
+                * r.padf_s[pl.ds(HALO - taps + 1 + k, rows), here]
+            )
+        r.act[:, here] = (total * sigmoid(total)).astype(BF16)
+
+    weave(pace)
+    small = dot(r.act[...], r.sw[pl.ds(0, at.small), :], NT)
+    r.sp[...] = small
+    small_low = small.astype(BF16)
+
+    @pl.loop(0, tiles)
+    def _(i):
+        here = lanes(i, GROUP)
+        before = dot(small_low, r.dtw_s[:, here]) + r.vec_s[pl.ds(at.dt_b, 1), here]
+        step = softplus(before)
+        r.pre[:, here] = before
+        r.dt_s[:, here] = step
+        r.dx_s[:, here] = step * r.act[:, here].astype(F32)
+        keep_sum(r.own_sum, i, step)
+
+    sums, ends = chain(
+        count, me, ctx, r.own_sum, r.sum_s, r.own_end, r.end_s,
+        (r.sum_send, r.sum_recv, r.end_send, r.end_recv),
+    )
+    each(me + 1, count, lambda j: sums(j, me).start())
+    weave(pace)
     for n in range(states):
-        bb_s[:, n, :] = jnp.broadcast_to(
+        r.bb_s[:, n, :] = jnp.broadcast_to(
             small[:, rank + n : rank + n + 1], (rows, 128)
         )
-    cd_s[...] = spread(small_low, rank + states, states)
+    r.cd_s[...] = spread(small_low, rank + states, states)
 
     def advance(t, state, rate2, here):
         return (
-            jnp.exp2(dt_s[pl.ds(t, 1), here] * rate2) * state
-            + dx_s[pl.ds(t, 1), here] * widen(bb_s[t], GROUP)
+            jnp.exp2(r.dt_s[pl.ds(t, 1), here] * rate2) * state
+            + r.dx_s[pl.ds(t, 1), here] * widen(r.bb_s[t], GROUP)
         )
 
     for g in range(groups):
         here = pl.ds(g * GROUP, GROUP)
-        rate2 = vec_ref[pl.ds(0, states), here] * LOG2E
+        rate2 = r.vec_s[pl.ds(0, states), here] * LOG2E
 
         def first_pass(step, state):
             for i in range(CHUNK):
                 state = advance(step * CHUNK + i, state, rate2, here)
             return state
 
-        own_end[:, here] = lax.fori_loop(
+        r.own_end[:, here] = lax.fori_loop(
             0, steps, first_pass, jnp.zeros((states, GROUP), F32)
         ).astype(BF16)
         each(me + 1, count, lambda j: ends(g, j, me).start())
+        weave(pace)
+
+    def h_copy(g):
+        here = pl.ds(g * GROUP, GROUP)
+        return pltpu.make_async_copy(
+            r.hs.at[:, here], r.h_hbm.at[:, here], r.h_sem.at[g]
+        )
 
     for g in range(groups):
         here = pl.ds(g * GROUP, GROUP)
-        rate2 = vec_ref[pl.ds(0, states), here] * LOG2E
+        rate2 = r.vec_s[pl.ds(0, states), here] * LOG2E
 
         def carry(j, state):
             if g == 0:
-                sums_from(j).wait_recv()
+                sums(j, j).wait_recv()
             ends(g, j, j).wait_recv()
             return (
-                jnp.exp2(rate2 * sum_of(sum_s, j, g)) * state
-                + end_s[j, :, here].astype(F32)
-            )
-
-        start = lax.fori_loop(0, me, carry, jnp.zeros((states, GROUP), F32))
-        hs[pl.ds(0, states), here] = start.astype(BF16)
+                jnp.exp2(rate2 * sum_of(r.sum_s, j, g)) * state
+                + r.end_s[j, :, here].astype(F32)
+            )
+
+        state = lax.fori_loop(0, me, carry, jnp.zeros((states, GROUP), F32))
+        r.hs[pl.ds(0, states), here] = state.astype(BF16)
 
         def second_pass(step, state):
             base = pl.multiple_of(step * CHUNK * states + states, states)
             for i in range(CHUNK):
                 state = advance(step * CHUNK + i, state, rate2, here)
-                hs[pl.ds(base + i * states, states), here] = state.astype(BF16)
+                r.hs[pl.ds(base + i * states, states), here] = state.astype(BF16)
             tokens = pl.ds(pl.multiple_of(step * CHUNK, CHUNK), CHUNK)
-            y_ref[tokens, here] = dot(
-                cd_s[tokens, :], hs[pl.ds(base, CHUNK * states), here]
+            r.y[tokens, here] = dot(
+                r.cd_s[tokens, :], r.hs[pl.ds(base, CHUNK * states), here]
             )
             return state
 
-        lax.fori_loop(0, steps, second_pass, start)
-        pltpu.make_async_copy(hs.at[:, here], h_hbm.at[:, here], h_sem.at[g]).start()
+        thirds = 1 if mode == "given" else 3
+        for part in range(thirds):
+            state = lax.fori_loop(
+                steps * part // thirds,
+                steps * (part + 1) // thirds,
+                second_pass,
+                state,
+            )
+            weave(pace)
+        h_copy(g).start()
         y_value = (
-            y_ref[:, here]
-            + vec_ref[pl.ds(at.skip, 1), here] * act_ref[:, here].astype(F32)
-        )
-        gate = gate_ref[:, here]
-        y_ref[:, here] = y_value
-        mixed_ref[:, here] = (y_value * gate * sigmoid(gate)).astype(BF16)
-
-    width = stream_ref.shape[1]
+            r.y[:, here]
+            + r.vec_s[pl.ds(at.skip, 1), here] * r.act[:, here].astype(F32)
+        )
+        gate = r.gate[:, here]
+        r.y[:, here] = y_value
+        r.mixed[:, here] = (y_value * gate * sigmoid(gate)).astype(BF16)
+
+    if mode == "given":
+        out_copy.wait()
+    else:
+        while queue and not stores_hold_out(mode, stores):
+            weave(1)
+    out_tile = 256 // r.wout_s.shape[1]
     for i in range(width // 256):
         here = pl.ds(i * 256, 256)
-        new_ref[:, here] = stream_ref[:, here] + dot(
-            mixed_ref[...], wout_ref[here, :], NT
-        )
+        wout = r.wout_s[pl.ds(i * out_tile, out_tile)].reshape(256, inner)
+        r.new[:, here] = r.stream[:, here] + dot(r.mixed[...], wout, NT)
+
+    weave(len(queue))
+    if mode != "given":
+        gather.finish()
 
     @pl.when(me < count - 1)
     def _():
         edge().wait_send()
 
-    each(me + 1, count, lambda j: sums(j).wait_send())
+    each(me + 1, count, lambda j: sums(j, me).wait_send())
     for g in range(groups):
-        here = pl.ds(g * GROUP, GROUP)
         each(me + 1, count, lambda j: ends(g, j, me).wait_send())
-        pltpu.make_async_copy(hs.at[:, here], h_hbm.at[:, here], h_sem.at[g]).wait()
+        h_copy(g).wait()
+    for copy in stores:
+        copy.wait()
+
+
+def stores_hold_out(mode, stores):
+    return len(stores) == (2 if mode == "first" else 1)
 
 
 def backward_kernel(
     cfg,
     sgrad_ref,
     stream_ref,
-    gain_ref,
+    sw_ref,
     win_ref,
-    xw_ref,
-    dtw_ref,
-    vec_ref,
     wout_ref,
     pad_ref,
     gate_ref,
@@ -352,10 +673,10 @@
     nsg_ref,
     gin_hbm,
     gout_hbm,
-    gx_ref,
-    gdt_ref,
-    gvec_ref,
-    ggain_ref,
+    gsmall_ref,
+    full_s,
+    vec_ref,
+    dtw_ref,
     hb,
     normed_s,
     low_s,
@@ -387,19 +708,13 @@
     in_sem,
     out_sem,
 ):
-    rows, inner, states, taps, rank, count = cfg
-    at = Names(states, taps)
+    rows, inner, states, taps, rank, count, channels = cfg
+    at = Names(states, taps, rank)
     ctx, me = lax.axis_index("ctx"), lax.axis_index("seq")
     groups, steps = inner // GROUP, rows // CHUNK
     width = stream_ref.shape[1]
     barrier = pltpu.get_barrier_semaphore()
-
-    def each(first, last, act):
-        def body(j, _):
-            act(j)
-            return 0
-
-        lax.fori_loop(first, last, body, 0)
+    gvec_ref = full_s.at[pl.ds(at.vec, at.rows - at.vec)]
 
     each(
         me + 1,
@@ -415,10 +730,12 @@
         )
 
     states_in(0).start()
+    load_small(at, sw_ref, vec_ref, dtw_ref)
+    gain = gain_row(at, channels, vec_ref)
     low_s[...] = sgrad_ref[...].astype(BF16)
     stream = stream_ref[...]
     scale = lax.rsqrt(jnp.mean(stream * stream, axis=1, keepdims=True) + EPS)
-    normed_s[...] = (stream * scale * gain_ref[...]).astype(BF16)
+    normed_s[...] = (stream * scale * gain).astype(BF16)
     small_low = sp_ref[...].astype(BF16)
 
     @pl.loop(0, inner // GROUP)
@@ -441,25 +758,10 @@
         dx_s[pl.ds(0, rows), here] = step * act
         keep_sum(own_sum, i, step)
 
-    def sums(j, slot):
-        return pltpu.make_async_remote_copy(
-            own_sum,
-            sum_s.at[slot],
-            sum_send.at[j],
-            sum_recv.at[slot],
-            device_id=(ctx, j),
-            device_id_type=MESH,
-        )
-
-    def ends(g, j, slot):
-        return pltpu.make_async_remote_copy(
-            own_end.at[:, pl.ds(g * GROUP, GROUP)],
-            end_s.at[slot, :, pl.ds(g * GROUP, GROUP)],
-            end_send.at[g, j],
-            end_recv.at[g, slot],
-            device_id=(ctx, j),
-            device_id_type=MESH,
-        )
+    sums, ends = chain(
+        count, me, ctx, own_sum, sum_s, own_end, end_s,
+        (sum_send, sum_recv, end_send, end_recv),
+    )
 
     @pl.when(me > 0)
     def _():
@@ -575,9 +877,13 @@
     @pl.loop(0, inner // GROUP)
     def _(i):
         here = lanes(i, GROUP)
-        gdt_ref[:, here] = dot(small_low, prelow_s[:, here], TN)
-        gx_ref[:, here] = dot(small_grad, act_ref[:, here], TN)
-        act_grad = sg_s[:, here] + dot(small_grad, xw_ref[:, here])
+        full_s[pl.ds(at.dt, rank), here] = dot(
+            small_low, prelow_s[:, here], TN
+        )[:rank]
+        full_s[pl.ds(0, at.small), here] = dot(small_grad, act_ref[:, here], TN)
+        act_grad = sg_s[:, here] + dot(
+            small_grad, sw_ref[pl.ds(0, at.small), here]
+        )
         total = vec_ref[pl.ds(at.conv_b, 1), here]
         for k in range(taps):
             total = (
@@ -689,10 +995,19 @@
     stream = stream_ref[...]
     scale = lax.rsqrt(jnp.mean(stream * stream, axis=1, keepdims=True) + EPS)
     normed_grad = nsg_ref[...]
-    ggain_ref[...] = jnp.broadcast_to(
-        jnp.sum(normed_grad * stream * scale, axis=0, keepdims=True), (8, width)
-    )
-    scaled = normed_grad * gain_ref[...]
+    gain_grad = jnp.sum(normed_grad * stream * scale, axis=0, keepdims=True)
+    gain_grad = jnp.broadcast_to(gain_grad, (8, width)).astype(BF16)
+    pick = gain_pick(channels)
+    for i in range(inner // 256):
+        wide = dot(gain_grad[:, 128 * i : 128 * i + 128], pick, NT)
+        gvec_ref[pl.ds(at.gain, 1), pl.ds(256 * i, 256)] = wide[:1]
+    for k in range(at.count, at.rows):
+        full_s[pl.ds(k, 1), :] = jnp.zeros((1, inner), F32)
+    if len(gsmall_ref.shape) == 3:
+        split_small(channels, full_s, gsmall_ref)
+    else:
+        gsmall_ref[...] = full_s[...]
+    scaled = normed_grad * gain
     inner_sum = jnp.mean(scaled * stream, axis=1, keepdims=True)
     nsg_ref[...] = (
         sgrad_ref[...] + scale * scaled - stream * (scale * scale * scale) * inner_sum
@@ -717,56 +1032,96 @@
     return [pl.BlockSpec(memory_space=pl.ANY)] * count
 
 
-def forward_call(cfg, stream, gain, win, xw, dtw, vec, wout):
-    rows, inner, states, taps, rank, count = cfg
-    small = rank + 2 * states
+def forward_call(cfg, mode, stream, operands):
+    rows, inner, states, taps, rank, count, channels = cfg
+    at = Names(states, taps, rank)
+    width = stream.shape[1]
     groups = inner // GROUP
+    devices = inner // channels
     shape = jax.ShapeDtypeStruct
     dma = pltpu.SemaphoreType.DMA
-    return pl.pallas_call(
-        functools.partial(forward_kernel, cfg),
-        out_shape=(
-            shape(stream.shape, F32),
-            shape((rows + HALO, inner), BF16),
-            shape((rows, inner), F32),
-            shape((rows, inner), BF16),
-            shape((rows, small), F32),
-            shape((rows, inner), F32),
-            shape(((rows + 1) * states, inner), BF16),
-            shape((rows, inner), F32),
-            shape((rows, inner), BF16),
+    vmem, any_space = in_vmem(1)[0], in_any(1)[0]
+    inputs = [("stream", stream, vmem)]
+    for name, array in operands:
+        inputs.append((name, array, vmem if name == "sw" else any_space))
+    outputs = [
+        ("new", shape(stream.shape, F32), vmem),
+        ("pad", shape((rows + HALO, inner), BF16), vmem),
+        ("gate", shape((rows, inner), F32), vmem),
+        ("act", shape((rows, inner), BF16), vmem),
+        ("sp", shape((rows, at.small), F32), vmem),
+        ("pre", shape((rows, inner), F32), vmem),
+        ("h_hbm", shape(((rows + 1) * states, inner), BF16), any_space),
+        ("y", shape((rows, inner), F32), vmem),
+        ("mixed", shape((rows, inner), BF16), vmem),
+    ]
+    if mode == "given":
+        given = dict(operands)
+        in_shape, out_shape = given["win_hbm"].shape, given["wout_hbm"].shape
+    else:
+        in_shape = (devices, 2 * inner // devices, width)
+        out_shape = (devices, width // devices, inner)
+        small_shape = (devices, at.rows * channels // 128, 128)
+        outputs.append(("sw", shape((at.rows, inner), BF16), vmem))
+        outputs.append(("wout_all", shape(out_shape, BF16), any_space))
+    if mode == "first":
+        outputs.append(("win_all", shape(in_shape, BF16), any_space))
+        outputs.append(("win2_all", shape(in_shape, BF16), any_space))
+        outputs.append(("gsm2_all", shape(small_shape, BF16), any_space))
+    scratch = [
+        ("win_s", pltpu.VMEM(in_shape, BF16)),
+        ("wout_s", pltpu.VMEM(out_shape, BF16)),
+        ("vec_s", pltpu.VMEM((at.rows - at.vec, inner), F32)),
+        ("dtw_s", pltpu.VMEM((at.small, inner), BF16)),
+        ("normed_s", pltpu.VMEM(stream.shape, BF16)),
+        ("padf_s", pltpu.VMEM((rows + HALO, inner), F32)),
+        ("halo_s", pltpu.VMEM((HALO, inner), BF16)),
+        ("dt_s", pltpu.VMEM((rows, inner), F32)),
+        ("dx_s", pltpu.VMEM((rows, inner), F32)),
+        ("bb_s", pltpu.VMEM((rows, states, 128), F32)),
+        ("cd_s", pltpu.VMEM((rows, CHUNK * states), BF16)),
+        ("hs", pltpu.VMEM(((rows + 1) * states, inner), BF16)),
+        ("own_sum", pltpu.VMEM((8, inner // 8), F32)),
+        ("sum_s", pltpu.VMEM((count, 8, inner // 8), F32)),
+        ("own_end", pltpu.VMEM((states, inner), BF16)),
+        ("end_s", pltpu.VMEM((count, states, inner), BF16)),
+        ("halo_sem", dma((2,))),
+        ("sum_send", dma((count,))),
+        ("sum_recv", dma((count,))),
+        ("end_send", dma((groups, count))),
+        ("end_recv", dma((groups, count))),
+        ("h_sem", dma((groups,))),
+        ("load_sem", dma((3,))),
+    ]
+    if mode != "given":
+        pieces = 8 if mode == "first" else 2
+        scratch += [
+            ("gsm_s", pltpu.VMEM(small_shape, BF16)),
+            ("own_sem", dma((pieces,))),
+            ("send_sem", dma((pieces, Gather.sends(count // 2)))),
+            ("recv_sem", dma((pieces, devices))),
+            ("store_sem", dma((2,))),
+        ]
+    names = [entry[0] for entry in inputs + outputs + scratch]
+    results = pl.pallas_call(
+        functools.partial(forward_kernel, cfg, mode, names),
+        out_shape=tuple(entry[1] for entry in outputs),
+        in_specs=[entry[2] for entry in inputs],
+        out_specs=tuple(entry[2] for entry in outputs),
+        scratch_shapes=[entry[1] for entry in scratch],
+        compiler_params=pltpu.CompilerParams(
+            collective_id={"given": 0, "first": 4, "later": 5}[mode],
+            has_side_effects=True,
+            vmem_limit_bytes=VMEM_BYTES,
         ),
-        in_specs=in_vmem(7),
-        out_specs=tuple(in_vmem(6) + in_any(1) + in_vmem(2)),
-        scratch_shapes=[
-            pltpu.VMEM(stream.shape, BF16),
-            pltpu.VMEM((rows + HALO, inner), F32),
-            pltpu.VMEM((HALO, inner), BF16),
-            pltpu.VMEM((rows, inner), F32),
-            pltpu.VMEM((rows, inner), F32),
-            pltpu.VMEM((rows, states, 128), F32),
-            pltpu.VMEM((rows, CHUNK * states), BF16),
-            pltpu.VMEM(((rows + 1) * states, inner), BF16),
-            pltpu.VMEM((8, inner // 8), F32),
-            pltpu.VMEM((count, 8, inner // 8), F32),
-            pltpu.VMEM((states, inner), BF16),
-            pltpu.VMEM((count, states, inner), BF16),
-            dma((2,)),
-            dma((count,)),
-            dma((count,)),
-            dma((groups, count)),
-            dma((groups, count)),
-            dma((groups,)),
-        ],
-        compiler_params=pltpu.CompilerParams(
-            collective_id=0, has_side_effects=True, vmem_limit_bytes=VMEM_BYTES
-        ),
-        name="forward_layer",
-    )(stream, gain, win, xw, dtw, vec, wout)
-
-
-def backward_call(cfg, sgrad, stream, gain, win, xw, dtw, vec, wout, saved):
-    rows, inner, states, taps, rank, count = cfg
+        name="forward_" + mode,
+    )(*[entry[1] for entry in inputs])
+    return {entry[0]: result for entry, result in zip(outputs, results)}
+
+
+def backward_call(cfg, in_blocks, sgrad, stream, sw, win, wout, saved):
+    rows, inner, states, taps, rank, count, channels = cfg
+    at = Names(states, taps, rank)
     width = stream.shape[1]
     small = rank + 2 * states
     groups = inner // GROUP
@@ -779,14 +1134,16 @@
             shape((rows, width), F32),
             shape((2 * inner, width), BF16),
             shape((width, inner), BF16),
-            shape((small, inner), F32),
-            shape((small, inner), F32),
-            shape((Names(states, taps).padded, inner), F32),
-            shape((8, width), F32),
+            shape((inner // channels, at.rows * channels // 128, 128), BF16)
+            if in_blocks
+            else shape((at.rows, inner), F32),
         ),
-        in_specs=in_vmem(13) + in_any(1) + in_vmem(2),
-        out_specs=tuple(in_vmem(1) + in_any(2) + in_vmem(4)),
+        in_specs=in_vmem(10) + in_any(1) + in_vmem(2),
+        out_specs=tuple(in_vmem(1) + in_any(2) + in_vmem(1)),
         scratch_shapes=[
+            pltpu.VMEM((at.rows, inner), F32),
+            pltpu.VMEM((at.rows - at.vec, inner), F32),
+            pltpu.VMEM((small, inner), BF16),
             pltpu.VMEM((2, (rows + 1) * states, GROUP), BF16),
             pltpu.VMEM((rows, width), BF16),
             pltpu.VMEM((rows, width), BF16),
@@ -803,7 +1160,7 @@
             pltpu.VMEM((rows, wide), F32),
             pltpu.VMEM((rows, inner), BF16),
             pltpu.VMEM((2, GROUP, width), BF16),
-            pltpu.VMEM((2, width // 4, inner), BF16),
+            pltpu.VMEM((2, width // 8, inner), BF16),
             pltpu.VMEM((8, inner), F32),
             pltpu.VMEM((8, inner // 8), F32),
             pltpu.VMEM((count, 8, inner // 8), F32),
@@ -822,7 +1179,7 @@
             collective_id=1, has_side_effects=True, vmem_limit_bytes=VMEM_BYTES
         ),
         name="backward_layer",
-    )(sgrad, stream, gain, win, xw, dtw, vec, wout, *saved)
+    )(sgrad, stream, sw, win, wout, *saved)
 
 
 def parts_of(in_rows, out_rows, small_rows):
@@ -833,168 +1190,6 @@
         (0, cut, in_rows - cut, 0),
         (1, 0, out_rows, 0),
     )
-
-
-def places():
-    ctx, seq = lax.axis_index("ctx"), lax.axis_index("seq")
-    return lax.div(ctx, 2), lax.rem(ctx, 2), lax.div(seq, 2), lax.rem(seq, 2)
-
-
-def device(y, x, z, core):
-    return (2 * y + x, 2 * z + core)
-
-
-def greet_square(depth):
-    y, x, z, core = places()
-    barrier = pltpu.get_barrier_semaphore()
-    partners = [device(y, x, z, 1 - core), device(y, 1 - x, z, core)]
-    partners.append(device(1 - y, x, z, core))
-    for step in range(1, depth):
-        partners.append(device(y, x, lax.rem(z + step, depth), core))
-    for partner in partners:
-        pl.semaphore_signal(barrier, inc=1, device_id=partner, device_id_type=MESH)
-    pl.semaphore_wait(barrier, len(partners))
-
-
-def gather_kernel(layers, depth, parts, *refs):
-    local, whole = refs[: 3 * layers], refs[3 * layers : 6 * layers]
-    own_sem, send_sem, recv_sem = refs[6 * layers :]
-    y, x, z, core = places()
-    greet_square(depth)
-    own_copies = []
-    for layer in range(layers):
-        for array in range(3):
-            copy = pltpu.make_async_copy(
-                local[3 * layer + array],
-                whole[3 * layer + array].at[y, x, z, core],
-                own_sem.at[layer, array],
-            )
-            copy.start()
-            own_copies.append(copy)
-    sent = []
-    used = [0] * layers
-
-    def span(layer, part, block):
-        array, first, rows, _ = parts[part]
-        return whole[3 * layer + array].at[(*block, pl.ds(first, rows))]
-
-    def send(layer, part, block, to, own=False):
-        array, first, rows, _ = parts[part]
-        source = (
-            local[3 * layer + array].at[pl.ds(first, rows)]
-            if own
-            else span(layer, part, block)
-        )
-        copy = pltpu.make_async_remote_copy(
-            source,
-            span(layer, part, block),
-            send_sem.at[layer, used[layer]],
-            recv_sem.at[(layer, *block[:2], block[2], block[3], part)],
-            device_id=to,
-            device_id_type=MESH,
-        )
-        used[layer] += 1
-        copy.start()
-        sent.append(copy)
-
-    def arrive(layer, part, block):
-        pltpu.make_async_remote_copy(
-            span(layer, part, block),
-            span(layer, part, block),
-            send_sem.at[layer, 0],
-            recv_sem.at[(layer, *block[:2], block[2], block[3], part)],
-            device_id=device(y, x, z, 1 - core),
-            device_id_type=MESH,
-        ).wait_recv()
-
-    x_side, y_side = device(y, 1 - x, z, core), device(1 - y, x, z, core)
-    sibling = device(y, x, z, 1 - core)
-    everything = range(len(parts))
-    line = [lax.rem(z + step, depth) for step in range(depth)]
-
-    def begin(layer):
-        block = (y, x, z, core)
-        for part in everything:
-            for to in (x_side, y_side):
-                send(layer, part, block, to, own=True)
-            for step in range(1, depth):
-                to = device(y, x, line[step], core)
-                send(layer, part, block, to, own=True)
-            send(layer, part, block, sibling, own=True)
-
-    def along(layer):
-        for step in range(depth):
-            for part in everything:
-                block = (y, x, line[step], core)
-                if step > 0:
-                    arrive(layer, part, block)
-                    for to in (x_side, y_side, sibling):
-                        send(layer, part, block, to)
-                if parts[part][3] == 1:
-                    block, to = (y, 1 - x, line[step], core), y_side
-                else:
-                    block, to = (1 - y, x, line[step], core), x_side
-                arrive(layer, part, block)
-                send(layer, part, block, to)
-                send(layer, part, block, sibling)
-
-    def rest(layer):
-        for step in range(depth):
-            for part in everything:
-                for other in (0, 1):
-                    if parts[part][3] == 1:
-                        block = (1 - y, x if other == 0 else 1 - x, line[step], core)
-                    else:
-                        block = (y if other == 0 else 1 - y, 1 - x, line[step], core)
-                    arrive(layer, part, block)
-                    send(layer, part, block, sibling)
-
-    def finish(layer):
-        for step in range(depth):
-            for part in everything:
-                for far_y in (y, 1 - y):
-                    for far_x in (x, 1 - x):
-                        arrive(layer, part, (far_y, far_x, line[step], 1 - core))
-
-    for layer in range(layers):
-        begin(layer)
-        along(layer)
-        rest(layer)
-    for layer in range(layers):
-        finish(layer)
-    for copy in own_copies:
-        copy.wait()
-    for copy in sent:
-        copy.wait_send()
-
-
-def gather_call(depth, local):
-    layers = len(local)
-    flat = [array for layer in local for array in layer]
-    parts = parts_of(*(array.shape[0] for array in local[0]))
-    outs = [
-        jax.ShapeDtypeStruct((2, 2, depth, 2) + array.shape, array.dtype)
-        for array in flat
-    ]
-    sends = len(parts) * (2 + depth + 3 * (depth - 1) + 2 * depth + 2 * depth)
-    dma = pltpu.SemaphoreType.DMA
-    gathered = pl.pallas_call(
-        functools.partial(gather_kernel, layers, depth, parts),
-        out_shape=tuple(outs),
-        in_specs=in_any(len(flat)),
-        out_specs=tuple(in_any(len(flat))),
-        scratch_shapes=[
-            dma((layers, 3)),
-            dma((layers, sends)),
-            dma((layers, 2, 2, depth, 2, len(parts))),
-        ],
-        compiler_params=pltpu.CompilerParams(collective_id=2, has_side_effects=True),
-        name="gather_weights",
-    )(*flat)
-    joined = [
-        array.reshape((-1,) + piece.shape[1:]) for array, piece in zip(gathered, flat)
-    ]
-    return [joined[3 * layer : 3 * layer + 3] for layer in range(layers)]
 
 
 def reduce_kernel(depth, parts, *refs):
@@ -1171,10 +1366,6 @@
     )(*shaped)
 
 
-def round_up(value, step):
-    return -(-value // step) * step
-
-
 def on_device(
     mesh,
     hidden_in,
@@ -1195,21 +1386,20 @@
     taps, channels = conv_weight.shape[1:]
     states = a_log.shape[2]
     rank = dt_weight.shape[1]
-    small = rank + 2 * states
     devices, count = mesh.shape["ctx"] * mesh.shape["seq"], mesh.shape["seq"]
     inner = channels * devices
     gains = norm_gain.shape[1]
-    at = Names(states, taps)
-    cfg = (rows, inner, states, taps, rank, count)
-    per_channel = small + rank + at.count
-    packed = per_channel * channels + gains
-    small_rows = round_up(packed, 16 * 1024) // 1024
+    at = Names(states, taps, rank)
+    cfg = (rows, inner, states, taps, rank, count, channels)
     depth = count // 2
     by_kernel = (
         mesh.shape["ctx"] == 4
-        and count % 2 == 0
-        and in_weight.shape[2] % 64 == 0
-        and out_weight.shape[2] % 16 == 0
+        and depth % 2 == 0
+        and layers == 2
+        and in_weight.shape[2] % 32 == 0
+        and out_weight.shape[2] % 32 == 0
+        and 128 % channels == 0
+        and at.rows * channels // 128 % 16 == 0
     )
 
     def pack(layer):
@@ -1222,82 +1412,98 @@
                 conv_bias[layer][None],
                 dt_bias[layer][None],
                 skip_gain[layer][None],
+                jnp.pad(norm_gain[layer], (0, channels - gains))[None],
             ],
             0,
         )
-        flat = jnp.concatenate([by_row.reshape(-1), norm_gain[layer]])
-        flat = jnp.pad(flat, (0, small_rows * 1024 - packed))
-        return flat.reshape(small_rows, 1024)
+        by_row = jnp.pad(by_row, ((0, at.rows - at.count), (0, 0)))
+        if by_kernel:
+            folds = by_row.reshape(128 // channels, -1, channels)
+            by_row = jnp.concatenate(list(folds), 1)
+        return by_row
 
     local = [
         (in_weight[layer].T, out_weight[layer].T, pack(layer))
         for layer in range(layers)
     ]
+    kept = ("pad", "gate", "act", "sp", "pre", "h_hbm", "y", "mixed")
+    stream = hidden_in.astype(F32)
+    streams, runs, weights = [], [], []
     if by_kernel:
-        gathered = gather_call(depth, local)
+        (in0, out0, small0), (in1, out1, small1) = local
+        operands = [
+            ("own_in", in0),
+            ("own_small", small0),
+            ("own_out", out0),
+            ("next_in", in1),
+            ("next_small", small1),
+        ]
+        first = forward_call(cfg, "first", stream, operands)
+        operands = [
+            ("win_hbm", first["win2_all"]),
+            ("gsm_hbm", first["gsm2_all"]),
+            ("own_out", out1),
+        ]
+        second = forward_call(cfg, "later", first["new"], operands)
+        runs = [first, second]
+        wins = [first["win_all"], first["win2_all"]]
+        weights = [
+            (
+                run["sw"],
+                win.reshape(2 * inner, width),
+                run["wout_all"].reshape(width, inner),
+            )
+            for run, win in zip(runs, wins)
+        ]
+        streams = [stream, first["new"]]
+        stream = second["new"]
     else:
-        gathered = [
-            [lax.all_gather(array, ("ctx", "seq"), axis=0, tiled=True) for array in layer]
-            for layer in local
-        ]
-
-    weights = []
-    for win, wout, pack_all in gathered:
-        flat = pack_all.reshape(devices, small_rows * 1024)
-        by_row = flat[:, : per_channel * channels].reshape(
-            devices, per_channel, channels
-        )
-        by_row = by_row.transpose(1, 0, 2).reshape(per_channel, inner)
-        gain = flat[:, per_channel * channels : packed].reshape(1, width).astype(F32)
-        xw = by_row[:small]
-        dtw = jnp.pad(by_row[small : small + rank], ((0, small - rank), (0, 0)))
-        vec = by_row[small + rank :].astype(F32)
-        vec = jnp.concatenate([-jnp.exp(vec[:states]), vec[states:]], 0)
-        vec = jnp.pad(vec, ((0, at.padded - at.count), (0, 0)))
-        weights.append((gain, win, xw, dtw, vec, wout))
-
-    stream = hidden_in.astype(F32)
-    streams, saved = [], []
-    for layer in range(layers):
-        streams.append(stream)
-        stream, *kept = forward_call(cfg, stream, *weights[layer])
-        saved.append(kept)
+        for w_in, w_out, w_small in local:
+            w_in = lax.all_gather(w_in, ("ctx", "seq"), axis=0, tiled=True)
+            w_out = lax.all_gather(w_out, ("ctx", "seq"), axis=0, tiled=True)
+            sw = lax.all_gather(w_small, ("ctx", "seq"), axis=1, tiled=True)
+            operands = [
+                ("win_hbm", w_in.reshape(-1, 128, width)),
+                ("sw", sw),
+                ("wout_hbm", w_out.reshape(-1, 32, inner)),
+            ]
+            run = forward_call(cfg, "given", stream, operands)
+            runs.append(run)
+            weights.append((sw, w_in, w_out))
+            streams.append(stream)
+            stream = run["new"]
     stream_grad = cotangent.astype(F32)
     grads = [None] * layers
     for layer in reversed(range(layers)):
-        stream_grad, g_in, g_out, g_x, g_dt, g_vec, g_gain = backward_call(
-            cfg, stream_grad, streams[layer], *weights[layer], saved[layer]
-        )
-        by_row = jnp.concatenate([g_x, g_dt[:rank], g_vec[: at.count]], 0)
-        by_row = by_row.reshape(per_channel, devices, channels).transpose(1, 0, 2)
-        flat = jnp.concatenate(
-            [
-                by_row.reshape(devices, per_channel * channels),
-                g_gain[0].reshape(devices, gains),
-            ],
-            1,
-        )
-        flat = jnp.pad(flat, ((0, 0), (0, small_rows * 1024 - packed)))
-        g_small = flat.astype(BF16).reshape(devices * small_rows, 1024)
+        stream_grad, g_in, g_out, g_small = backward_call(
+            cfg,
+            by_kernel,
+            stream_grad,
+            streams[layer],
+            *weights[layer],
+            [runs[layer][name] for name in kept],
+        )
         if by_kernel:
-            summed = reduce_call(depth, (g_in, g_out, g_small))
+            s_in, s_out, s_small = reduce_call(
+                depth, (g_in, g_out, g_small.reshape(-1, 128))
+            )
+            s_small = s_small.reshape(-1, 128 // channels, channels)
+            s_small = s_small.transpose(1, 0, 2).reshape(at.rows, channels)
         else:
-            summed = [
+            s_in, s_out, s_small = [
                 lax.psum_scatter(
-                    array.astype(F32), ("ctx", "seq"), scatter_dimension=0, tiled=True
+                    array.astype(F32),
+                    ("ctx", "seq"),
+                    scatter_dimension=dim,
+                    tiled=True,
                 )
-                for array in (g_in, g_out, g_small)
+                for array, dim in ((g_in, 0), (g_out, 0), (g_small, 1))
             ]
-        s_in, s_out, s_small = summed
-        flat = s_small.reshape(-1)
-        by_row = flat[: per_channel * channels].reshape(per_channel, channels)
-        s_x, s_dt, s_vec = (
-            by_row[:small],
-            by_row[small : small + rank],
-            by_row[small + rank :],
-        )
+        s_x = s_small[: at.small, :channels]
+        s_dt = s_small[at.dt : at.dt + rank, :channels]
+        s_vec = s_small[at.vec : at.count, :channels]
         grads[layer] = (
-            flat[per_channel * channels : packed],
+            s_vec[at.gain, :gains],
             s_in.T,
             s_vec[at.conv : at.conv + taps],
             s_vec[at.conv_b],

time: 630 us -> 536 us (0.85)
  Pallas kernels: 567 us -> 498 us
  local copies, waits for them, and re-layouts: 38.9 us -> 15.1 us
    pallas_call x3 -> x2, Pallas kernels: 273 us -> 197 us  [forward_call(): pl.pallas_call(functools.partial(forward_kernel, cfg, mode, names), out_s...]
    slice x44 -> x9, local copies, waits for them, and re-layouts: 10.2 us -> 1.32 us  [the longest x1 0.74 us: pack(): x_weight[layer]]
    unnamed x51 -> x21, local copies, waits for them, and re-layouts: 13.4 us -> 4.93 us
    pallas_call x2, Pallas kernels: 147 us -> 156 us  [backward_call(): pl.pallas_call(functools.partial(backward_kernel, cfg), out_shape=(shape(...]
where the time goes in v2:
time: 536 us; the launch traced here: 528 us
  Pallas kernels  498 us (93%)
  local copies, waits for them, and re-layouts  15.1 us (3%)
  other arithmetic  13 us (2%)
    pallas_call x2, Pallas kernels, forward_call(): pl.pallas_call(functools.partial(forward_kernel, cfg, mode, names), out_s...  197 us
    pallas_call x2, Pallas kernels, backward_call(): pl.pallas_call(functools.partial(backward_kernel, cfg), out_shape=(shape(...  156 us
    pallas_call x2, Pallas kernels, reduce_call(): pl.pallas_call(functools.partial(reduce_kernel, depth, parts), out_shape=...  145 us

profile of v2, /device:TPU:0, one launch (start us, length us, event | category | flops | bytes accessed | tf_op | source)
XLA Modules:
  0.0 527.6 jit_solution(10355732012767255669)
XLA Ops:
  0.7 0.7 slice_bitcast_fusion.16
  1.4 0.7 fusion.6
  2.1 0.7 fusion.4
  3.6 0.7 slice_bitcast_fusion.12
  4.3 0.7 fusion.3
  5.2 0.7 slice_bitcast_fusion.10
  7.5 1.7 slice_bitcast_fusion
  9.2 1.1 fusion
  10.3 0.9 copy.80
  11.2 0.8 copy.78
  12.0 2.1 convert_element_type.15.refs_0_.stream_ref
  14.1 1.1 convert_element_type.17.sgrad_ref
  15.2 134.5 %forward_first.1 = (f32[256,1024]{1,0:T(8,128)}, bf16[272,2048]{1,0:T(8,128)(2,1)}, f32[256,2048]{1,0:T(8,128)}, bf16[256,2048]{1,0:T(8,128)(2,1)}, f32[256,96]{...) custom-call(f32[256,1024]{1,0:T(8,128)} %convert_element_type.15.ref, ...), custom_call_target="tpu_custom_call" | custom-call | tf_op jit(solution)/shard_map/forward_first/pallas_call | solution.py:1106
  149.7 62.5 %forward_later.1 = (f32[256,1024]{1,0:T(8,128)}, bf16[272,2048]{1,0:T(8,128)(2,1)}, f32[256,2048]{1,0:T(8,128)}, bf16[256,2048]{1,0:T(8,128)(2,1)}, f32[256,96]{...) custom-call(f32[256,1024]{1,0:T(8,128)} %get-tuple-element.51.refs_0, ...), custom_call_target="tpu_custom_call" | custom-call | tf_op jit(solution)/shard_map/forward_later/pallas_call | solution.py:1106
  212.3 2.1 convert_element_type.16
  214.3 79.1 %backward_layer.2 = (f32[256,1024]{1,0:T(8,128)}, bf16[4096,1024]{1,0:T(8,128)(2,1)}, bf16[1024,2048]{1,0:T(8,128)(2,1)}, bf16[32,96,128]{2,1,0:T(8,128)(2,1)}) custom-call(f32[256,1024]{1,0:T(8,128)} %convert_element_type.17.sgrad_ref, f32[256,1024]{1,0:T(8,128)} %get-tuple-element.51.refs_0_.stream_ref, bf16[192,2048]{1,0:T(8,128)(2,1)} %get-tuple-element.55.sw_ref, ...), custom_call_target="tpu_custom_call" | custom-call | tf_op jit(solution)/shard_map/backward_layer/pallas_call | solution.py:1131
  293.4 76.7 %backward_layer.3 = (f32[256,1024]{1,0:T(8,128)}, bf16[4096,1024]{1,0:T(8,128)(2,1)}, bf16[1024,2048]{1,0:T(8,128)(2,1)}, bf16[32,96,128]{2,1,0:T(8,128)(2,1)}) custom-call(f32[256,1024]{1,0:T(8,128)} %get-tuple-element.65.sgrad_ref, f32[256,1024]{1,0:T(8,128)} %convert_element_type.15.refs_0_.stream_ref, bf16[192,2048]{1,0:T(8,128)(2,1)} %get-tuple-element.66.sw_ref, ...), custom_call_target="tpu_custom_call" | custom-call | tf_op jit(solution)/shard_map/backward_layer/pallas_call | solution.py:1131
  370.2 71.5 %reduce_gradients.2 = (f32[128,1024]{1,0:T(8,128)}, f32[32,2048]{1,0:T(8,128)}, f32[96,128]{1,0:T(8,128)}) custom-call(bf16[2,2,4,2,128,1024]{5,4,3,2,1,0:T(8,128)(2,1)} %bitcast.107, bf16[2,2,4,2,32,2048]{5,4,3,2,1,0:T(8,128)(2,1)} %bitcast.111, bf16[2,2,4,2,96,128]{5,4,3,2,1,0:T(8,128)(2,1)} %bitcast.115), custom_call_target="tpu_custom_call" | custom-call | tf_op jit(solution)/shard_map/reduce_gradients/pallas_call | solution.py:1345
  441.7 73.7 %reduce_gradients.3 = (f32[128,1024]{1,0:T(8,128)}, f32[32,2048]{1,0:T(8,128)}, f32[96,128]{1,0:T(8,128)}) custom-call(bf16[2,2,4,2,128,1024]{5,4,3,2,1,0:T(8,128)(2,1)} %bitcast.106, bf16[2,2,4,2,32,2048]{5,4,3,2,1,0:T(8,128)(2,1)} %bitcast.109, bf16[2,2,4,2,96,128]{5,4,3,2,1,0:T(8,128)(2,1)} %bitcast.114), custom_call_target="tpu_custom_call" | custom-call | tf_op jit(solution)/shard_map/reduce_gradients/pallas_call | solution.py:1345
  515.5 1.2 pad_maximum_fusion
  516.8 1.3 copy.76
  520.6 0.7 copy.77
  525.3 0.8 pad_maximum_fusion.1
  526.1 1.0 copy.83
  (62 shorter events, 8.9 us)
Async XLA Ops:
  0.6 13.5 %copy-start.1 = (bf16[256,1024]{1,0:T(8,128)(2,1)S(1)}, bf16[256,1024]{1,0:T(8,128)(2,1)}, u32[]{:S(2)}) copy-start(bf16[256,1024]{1,0:T(8,128)(2,1)} %param.13) | copy-start | bytes 1572868
  441.7 73.8 %copy-start.2 = (f32[128,1024]{1,0:T(8,128)S(1)}, f32[128,1024]{1,0:T(8,128)}, u32[]{:S(2)}) copy-start(f32[128,1024]{1,0:T(8,128)} %get-tuple-element.86) | copy-start | bytes 1572868
  515.5 2.6 copy-start.6
  515.5 2.7 copy-start.5
  515.5 9.8 %copy-start.3 = (f32[32,2048]{1,0:T(8,128)S(1)}, f32[32,2048]{1,0:T(8,128)}, u32[]{:S(2)}) copy-start(f32[32,2048]{1,0:T(8,128)} %get-tuple-element.88) | copy-start | bytes 786436
  515.5 9.8 %copy-start.4 = (f32[32,2048]{1,0:T(8,128)S(1)}, f32[32,2048]{1,0:T(8,128)}, u32[]{:S(2)}) copy-start(f32[32,2048]{1,0:T(8,128)} %get-tuple-element.89) | copy-start | bytes 786436
  515.5 10.6 %copy-start = (f32[256,1024]{1,0:T(8,128)S(1)}, f32[256,1024]{1,0:T(8,128)}, u32[]{:S(2)}) copy-start(f32[256,1024]{1,0:T(8,128)} %get-tuple-element.181) | copy-start | bytes 3145732

commit v3 on v2

--- a/solution.py
+++ b/solution.py
@@ -142,6 +142,24 @@
                 moved = pltpu.roll(held[part], shift, 1) if shift else held[part]
                 tile = moved if tile is None else jnp.where(owner == part, moved, tile)
             sw_ref[pl.ds(fold * rows, rows), lanes(j, 128)] = tile.astype(BF16)
+
+
+def split(number, by):
+    if isinstance(number, int):
+        return divmod(number, by)
+    return lax.div(number, by), lax.rem(number, by)
+
+
+class Folded:
+    def __init__(self, ref):
+        self.ref, self.shape = ref, ref.shape[3:]
+
+    def __setitem__(self, block, value):
+        _, x, z, core = self.ref.shape[:4]
+        row = lax.div(block, z * core)
+        self.ref[
+            lax.div(row, x), lax.rem(row, x), lax.rem(lax.div(block, core), z), lax.rem(block, core)
+        ] = value
 
 
 def split_small(channels, full_ref, blocks):
@@ -311,6 +329,139 @@
     def finish(self):
         for copy in self.sent:
             copy.wait_send()
+
+
+class Reduce:
+    def __init__(self, depth, pieces, buffers, own_sem, send_sem, recv_sem):
+        self.depth, self.pieces, self.buffers = depth, pieces, buffers
+        self.own_sem, self.send_sem, self.recv_sem = own_sem, send_sem, recv_sem
+        y, x, z, core = places()
+        self.y, self.x, self.core = y, x, core
+        self.line = [lax.rem(z + step + 1, depth) for step in range(depth)]
+        self.x_side, self.y_side = device(y, 1 - x, z, core), device(1 - y, x, z, core)
+        self.sibling = device(y, x, z, 1 - core)
+        self.along = [device(y, x, there, core) for there in self.line]
+        self.sent = []
+
+    @staticmethod
+    def buffers_of(depth, rows, width):
+        return [
+            pltpu.VMEM(lead + (rows, width), BF16)
+            for lead in ((2, 2, 2), (depth, 2, 2), (depth, 2), (depth,), (depth - 1,))
+        ]
+
+    def part_of(self, item, step, side):
+        whole, _, first, rows, _ = self.pieces[item]
+        return whole.at[:, :, self.line[step], side, pl.ds(first, rows)]
+
+    def local(self, item, step):
+        return pltpu.make_async_copy(
+            self.part_of(item, step, self.core),
+            self.buffers[item][0].at[step % 2],
+            self.own_sem.at[item, step % 2],
+        )
+
+    def hop(self, stage, item, step):
+        _, core_in, first_in, second_in, line_in = self.buffers[item]
+        crosses_y = self.pieces[item][4]
+        y, x = self.y, self.x
+        if stage == 0:
+            source = self.part_of(item, step, 1 - self.core)
+            target, to = core_in.at[step], self.sibling
+        elif stage == 1:
+            source = core_in.at[step, 1 - y] if crosses_y else core_in.at[step, :, 1 - x]
+            target, to = first_in.at[step], self.y_side if crosses_y else self.x_side
+        elif stage == 2:
+            source = first_in.at[step, 1 - x if crosses_y else 1 - y]
+            target, to = second_in.at[step], self.x_side if crosses_y else self.y_side
+        else:
+            source, target, to = second_in.at[step], line_in.at[step], self.along[step]
+        return pltpu.make_async_remote_copy(
+            source,
+            target,
+            self.send_sem.at[item, stage, step],
+            self.recv_sem.at[item, stage, step],
+            device_id=to,
+            device_id_type=MESH,
+        )
+
+    def send(self, stage, item, step):
+        copy = self.hop(stage, item, step)
+        copy.start()
+        self.sent.append(copy)
+
+    @staticmethod
+    def add(target, other, rows):
+        @pl.loop(0, rows // 16)
+        def _(k):
+            here = pl.ds(pl.multiple_of(k * 16, 16), 16)
+            target[here] = (
+                target[here].astype(F32) + other[here].astype(F32)
+            ).astype(BF16)
+
+    def begin(self, item):
+        for step in range(self.depth):
+            self.send(0, item, step)
+            if step < 2:
+                self.local(item, step).start()
+
+    def settle(self, stage, item, step):
+        own, core_in, first_in, second_in, _ = self.buffers[item]
+        rows, crosses_y = self.pieces[item][3:]
+        self.hop(stage, item, step).wait_recv()
+        if stage == 0:
+            self.local(item, step).wait()
+            for y in (0, 1):
+                for x in (0, 1):
+                    self.add(core_in.at[step, y, x], own.at[step % 2, y, x], rows)
+            if step + 2 < self.depth:
+                self.local(item, step + 2).start()
+        elif stage == 1:
+            for far in (0, 1):
+                kept = (
+                    core_in.at[step, self.y, far]
+                    if crosses_y
+                    else core_in.at[step, far, self.x]
+                )
+                self.add(first_in.at[step, far], kept, rows)
+        else:
+            kept = first_in.at[step, self.x if crosses_y else self.y]
+            self.add(second_in.at[step], kept, rows)
+        if stage < 2 or step < self.depth - 1:
+            self.send(stage + 1, item, step)
+
+    def last(self, item):
+        _, out, first, rows, _ = self.pieces[item]
+        second_in, line_in = self.buffers[item][3:]
+        for step in range(self.depth - 1):
+            self.hop(3, item, step).wait_recv()
+
+        @pl.loop(0, rows // 16)
+        def _(k):
+            here = pl.ds(pl.multiple_of(k * 16, 16), 16)
+            total = second_in[self.depth - 1, here].astype(F32)
+            for step in range(self.depth - 1):
+                total = total + line_in[step, here].astype(F32)
+            out[pl.ds(pl.multiple_of(first + k * 16, 16), 16)] = total
+
+    def turns(self, items):
+        actions = []
+        for turn in range(self.depth + 2):
+            for stage in range(3):
+                step = turn - stage
+                if 0 <= step < self.depth:
+                    for item in items:
+                        actions.append(
+                            functools.partial(self.settle, stage, item, step)
+                        )
+        for item in items:
+            actions.append(functools.partial(self.last, item))
+        return actions
+
+    def finish(self):
+        for copy in self.sent:
+            copy.wait_send()
+        self.sent = []
 
 
 def chain(count, me, ctx, own_sum, sum_s, own_end, end_s, sems):
@@ -655,151 +806,221 @@
     return len(stores) == (2 if mode == "first" else 1)
 
 
-def backward_kernel(
-    cfg,
-    sgrad_ref,
-    stream_ref,
-    sw_ref,
-    win_ref,
-    wout_ref,
-    pad_ref,
-    gate_ref,
-    act_ref,
-    sp_ref,
-    pre_ref,
-    h_hbm,
-    y_ref,
-    mixed_ref,
-    nsg_ref,
-    gin_hbm,
-    gout_hbm,
-    gsmall_ref,
-    full_s,
-    vec_ref,
-    dtw_ref,
-    hb,
-    normed_s,
-    low_s,
-    sg_s,
-    dt_s,
-    dx_s,
-    stepg_s,
-    pb_s,
-    cb_s,
-    bd_s,
-    ab_s,
-    rb_s,
-    pin_s,
-    pout_s,
-    prelow_s,
-    stage_in,
-    stage_out,
-    halo_s,
-    own_sum,
-    sum_s,
-    own_end,
-    end_s,
-    halo_sem,
-    sum_send,
-    sum_recv,
-    end_send,
-    end_recv,
-    h_sem,
-    in_sem,
-    out_sem,
-):
+def backward_kernel(cfg, mode, names, *refs):
+    r = types.SimpleNamespace(**dict(zip(names, refs)))
     rows, inner, states, taps, rank, count, channels = cfg
     at = Names(states, taps, rank)
     ctx, me = lax.axis_index("ctx"), lax.axis_index("seq")
-    groups, steps = inner // GROUP, rows // CHUNK
-    width = stream_ref.shape[1]
+    groups, steps, tiles = inner // GROUP, rows // CHUNK, inner // GROUP
+    depth = count // 2
+    width = r.stream.shape[1]
     barrier = pltpu.get_barrier_semaphore()
-    gvec_ref = full_s.at[pl.ds(at.vec, at.rows - at.vec)]
-
-    each(
-        me + 1,
-        count,
-        lambda j: pl.semaphore_signal(
-            barrier, inc=1, device_id=(ctx, j), device_id_type=MESH
-        ),
-    )
-
-    def states_in(g):
+    gvec = r.full_s.at[pl.ds(at.vec, at.rows - at.vec)]
+
+    def signal(semaphore, to):
+        pl.semaphore_signal(semaphore, inc=1, device_id=to, device_id_type=MESH)
+
+    queue = collections.deque()
+
+    def weave(times):
+        for _ in range(min(times, len(queue))):
+            queue.popleft()()
+
+    each(me + 1, count, lambda j: signal(barrier, (ctx, j)))
+    if mode != "given":
+        each(0, me, lambda j: signal(barrier, (ctx, j)))
+        y, x, z, core = places()
+        signal(barrier, device(y, 1 - x, z, core))
+        signal(barrier, device(1 - y, x, z, core))
+
+    def wout_copy(i):
+        slot = lax.rem(i, 2)
         return pltpu.make_async_copy(
-            h_hbm.at[:, pl.ds(g * GROUP, GROUP)], hb.at[g % 2], h_sem.at[g % 2]
-        )
-
-    states_in(0).start()
-    load_small(at, sw_ref, vec_ref, dtw_ref)
-    gain = gain_row(at, channels, vec_ref)
-    low_s[...] = sgrad_ref[...].astype(BF16)
-    stream = stream_ref[...]
+            r.wout.at[:, :, lanes(i, GROUP)], r.wout_s.at[slot], r.wout_sem.at[slot]
+        )
+
+    def gate_copies(i):
+        slot = lax.rem(i, 2)
+        return [
+            pltpu.make_async_copy(
+                array.at[:, lanes(i, GROUP)], r.gate_s.at[slot, k], r.gate_sem.at[slot, k]
+            )
+            for k, array in enumerate((r.gate, r.y))
+        ]
+
+    win_rows = r.win_s.shape[1]
+
+    def win_copy(i, slot):
+        return pltpu.make_async_copy(
+            r.win.at[pl.ds(i * win_rows, win_rows)], r.win_s.at[slot], r.win_sem.at[slot]
+        )
+
+    span = rows // 2 * states
+
+    def states_in(k):
+        g, half = k // 2, 1 - k % 2
+        return pltpu.make_async_copy(
+            r.h_hbm.at[pl.ds(half * span, span + states), pl.ds(g * GROUP, GROUP)],
+            r.hb.at[k % 2],
+            r.h_sem.at[k % 2],
+        )
+
+    wout_copy(0).start()
+    for copy in gate_copies(0):
+        copy.start()
+    load_small(at, r.sw, r.vec_s, r.dtw_s)
+    gain = gain_row(at, channels, r.vec_s)
+    r.low_s[...] = r.sgrad[...].astype(BF16)
+    stream = r.stream[...]
     scale = lax.rsqrt(jnp.mean(stream * stream, axis=1, keepdims=True) + EPS)
-    normed_s[...] = (stream * scale * gain).astype(BF16)
-    small_low = sp_ref[...].astype(BF16)
-
-    @pl.loop(0, inner // GROUP)
+    r.normed_s[...] = (stream * scale * gain).astype(BF16)
+    small_low = r.sp[...].astype(BF16)
+
+    in_items, out_items, own_items = [], [], []
+    if mode == "given":
+
+        @pl.when(me > 0)
+        def _():
+            pl.semaphore_wait(barrier, me)
+
+    else:
+        pl.semaphore_wait(barrier, count + 1)
+        pieces, buffers = [], []
+
+        def add_piece(whole, out, cuts, held):
+            start = len(pieces)
+            total = whole.shape[4]
+            for k, first_y in enumerate(cuts):
+                piece = total // len(cuts)
+                pieces.append((whole, out, k * piece, piece, first_y))
+                buffers.append(held[k])
+            return list(range(start, len(pieces)))
+
+        def held_by(name):
+            found = []
+            while hasattr(r, f"{name}{len(found)}_0"):
+                k = len(found)
+                found.append([getattr(r, f"{name}{k}_{part}") for part in range(5)])
+            return found
+
+        held_in, held_small, held_out = (
+            held_by("rin"),
+            held_by("rsmall"),
+            held_by("rout"),
+        )
+        out_items = add_piece(r.gout, r.sum_out, (1, 0), held_out)
+        if mode == "first":
+            in_items = add_piece(r.next_gin, r.sum_next_in, (1, 0), held_in)
+            in_items += add_piece(r.next_gsmall, r.sum_next_small, (1,), held_small)
+            own_items = add_piece(r.gin, r.sum_in, (1, 0), held_in)
+            own_items += add_piece(r.gsmall_hbm, r.sum_small, (0,), held_small)
+        reduce = Reduce(depth, pieces, buffers, r.own_sem, r.send_sem, r.recv_sem)
+        for item in in_items:
+            reduce.begin(item)
+
+    out_shape = r.stage_out.shape[1:]
+    out_rows = out_shape[0] * out_shape[1] * out_shape[2]
+    line = r.gout.shape[2]
+
+    def block_of(whole, i):
+        row, z = split(2 * i, line)
+        y, x = split(row, 2)
+        return whole.at[y, x, pl.ds(z, 2)]
+
+    for k in range(width // out_rows):
+        slot = k % 2
+        copy = pltpu.make_async_copy(
+            r.stage_out.at[slot], block_of(r.gout, k), r.out_sem.at[slot]
+        )
+        if k >= 2:
+            copy.wait()
+
+        @pl.loop(0, tiles)
+        def _(i):
+            here = lanes(i, GROUP)
+            r.stage_out[slot, :, :, :, here] = (
+                dot(r.low_s[:, pl.ds(k * out_rows, out_rows)], r.mixed[:, here], TN)
+                .astype(BF16)
+                .reshape(out_shape[:-1] + (GROUP,))
+            )
+
+        copy.start()
+    for slot in range(2):
+        pltpu.make_async_copy(
+            r.stage_out.at[slot], block_of(r.gout, 0), r.out_sem.at[slot]
+        ).wait()
+    if mode != "given":
+        for item in out_items:
+            reduce.begin(item)
+        queue.extend(reduce.turns(in_items + out_items))
+    pace = -(-len(queue) // (24 if mode == "first" else 16))
+    weave(pace)
+
+    @pl.loop(0, tiles)
     def _(i):
         here = lanes(i, GROUP)
-        mixed_grad = dot(low_s[...], wout_ref[:, here])
-        gate = gate_ref[:, here]
+        slot = lax.rem(i, 2)
+
+        @pl.when(i + 1 < tiles)
+        def _():
+            wout_copy(i + 1).start()
+            for copy in gate_copies(i + 1):
+                copy.start()
+
+        wout_copy(i).wait()
+        for copy in gate_copies(i):
+            copy.wait()
+        mixed_grad = dot(r.low_s[...], r.wout_s[slot].reshape(width, GROUP))
+        gate = r.gate_s[slot, 0]
         sig = sigmoid(gate)
-        act = act_ref[:, here].astype(F32)
+        act = r.act[:, here].astype(F32)
         scan_grad = mixed_grad * gate * sig
-        sg_s[:, here] = scan_grad
-        pb_s[:, lanes(i + inner // GROUP, GROUP)] = (
-            mixed_grad * y_ref[:, here] * sig * (1.0 + gate * (1.0 - sig))
+        r.sg_s[:, here] = scan_grad
+        r.pb_s[:, lanes(i + tiles, GROUP)] = (
+            mixed_grad * r.gate_s[slot, 1] * sig * (1.0 + gate * (1.0 - sig))
         ).astype(BF16)
-        gvec_ref[pl.ds(at.skip, 1), here] = jnp.sum(
-            scan_grad * act, axis=0, keepdims=True
-        )
-        step = softplus(pre_ref[:, here])
-        dt_s[:, here] = step
-        dx_s[pl.ds(0, rows), here] = step * act
-        keep_sum(own_sum, i, step)
+        gvec[pl.ds(at.skip, 1), here] = jnp.sum(scan_grad * act, axis=0, keepdims=True)
+        step = softplus(r.pre[:, here])
+        r.dt_s[:, here] = step
+        r.dx_s[pl.ds(0, rows), here] = step * act
+        keep_sum(r.own_sum, i, step)
 
     sums, ends = chain(
-        count, me, ctx, own_sum, sum_s, own_end, end_s,
-        (sum_send, sum_recv, end_send, end_recv),
+        count, me, ctx, r.own_sum, r.sum_s, r.own_end, r.end_s,
+        (r.sum_send, r.sum_recv, r.end_send, r.end_recv),
     )
-
-    @pl.when(me > 0)
-    def _():
-        pl.semaphore_wait(barrier, me)
-
     each(0, me, lambda j: sums(j, me).start())
+    weave(pace)
     for n in range(states):
         first = rank + states + n
-        cb_s[:, n, :] = jnp.broadcast_to(
-            sp_ref[:, first : first + 1], (rows, 128)
-        )
-    bd_s[...] = spread(small_low, rank, states)
+        r.cb_s[:, n, :] = jnp.broadcast_to(r.sp[:, first : first + 1], (rows, 128))
+    r.bd_s[...] = spread(small_low, rank, states)
     ones = jnp.where(chunk_mask(CHUNK, states), 1.0, 0.0).astype(BF16)
+    states_in(0).start()
 
     for g in range(groups):
         here = pl.ds(g * GROUP, GROUP)
-        rate2 = vec_ref[pl.ds(0, states), here] * LOG2E
+        rate2 = r.vec_s[pl.ds(0, states), here] * LOG2E
 
         def first_pass(k, state):
             step = steps - 1 - k
             for i in reversed(range(CHUNK)):
                 t = step * CHUNK + i
-                state = jnp.exp2(dt_s[pl.ds(t, 1), here] * rate2) * (
-                    state + sg_s[pl.ds(t, 1), here] * widen(cb_s[t], GROUP)
+                state = jnp.exp2(r.dt_s[pl.ds(t, 1), here] * rate2) * (
+                    state + r.sg_s[pl.ds(t, 1), here] * widen(r.cb_s[t], GROUP)
                 )
             return state
 
-        own_end[:, here] = lax.fori_loop(
+        r.own_end[:, here] = lax.fori_loop(
             0, steps, first_pass, jnp.zeros((states, GROUP), F32)
         ).astype(BF16)
         each(0, me, lambda j: ends(g, j, me).start())
+        weave(pace)
 
     for g in range(groups):
         here = pl.ds(g * GROUP, GROUP)
-        rate = vec_ref[pl.ds(0, states), here]
+        rate = r.vec_s[pl.ds(0, states), here]
         rate2 = rate * LOG2E
-        if g + 1 < groups:
-            states_in(g + 1).start()
 
         def carry(k, state):
             j = count - 1 - k
@@ -807,107 +1028,118 @@
                 sums(j, j).wait_recv()
             ends(g, j, j).wait_recv()
             return (
-                jnp.exp2(rate2 * sum_of(sum_s, j, g)) * state
-                + end_s[j, :, here].astype(F32)
+                jnp.exp2(rate2 * sum_of(r.sum_s, j, g)) * state
+                + r.end_s[j, :, here].astype(F32)
             )
 
         begin = lax.fori_loop(
             0, count - 1 - me, carry, jnp.zeros((states, GROUP), F32)
         )
-        states_in(g).wait()
-
-        def second_pass(k, both):
-            state, total = both
-            step = steps - 1 - k
-            base = pl.multiple_of(step * CHUNK * states, states)
-            for i in reversed(range(CHUNK)):
-                t = step * CHUNK + i
-                dt = dt_s[pl.ds(t, 1), here]
-                adjoint = state + sg_s[pl.ds(t, 1), here] * widen(cb_s[t], GROUP)
-                state = jnp.exp2(dt * rate2) * adjoint
-                held = hb[g % 2, pl.ds(base + i * states, states), :].astype(F32)
-                rated = state * held * rate
-                total = total + dt * rated
-                ab_s[pl.ds(i * states, states), :] = adjoint.astype(BF16)
-                rb_s[pl.ds(i * states, states), :] = rated.astype(BF16)
-            tokens = pl.ds(pl.multiple_of(step * CHUNK, CHUNK), CHUNK)
-            from_in = dot(bd_s[tokens, :], ab_s[...])
-            from_rate = dot(ones, rb_s[...])
-            scan_grad = sg_s[tokens, here]
-            into_in = dot(dx_s[tokens, here].astype(BF16), ab_s[...], NT)
-            into_out = dot(
-                scan_grad.astype(BF16),
-                hb[g % 2, pl.ds(base + states, CHUNK * states), :],
-                NT,
-            )
-            if g == 0:
-                pin_s[tokens, :] = into_in
-                pout_s[tokens, :] = into_out
-            else:
-                pin_s[tokens, :] += into_in
-                pout_s[tokens, :] += into_out
-            stepg_s[tokens, here] = (
-                act_ref[tokens, here].astype(F32) * from_in + from_rate
-            )
-            sg_s[tokens, here] = (
-                dt_s[tokens, here] * from_in
-                + vec_ref[pl.ds(at.skip, 1), here] * scan_grad
-            )
-            return state, total
-
-        _, total = lax.fori_loop(
-            0, steps, second_pass, (begin, jnp.zeros((states, GROUP), F32))
-        )
-        gvec_ref[pl.ds(0, states), here] = total
-
-    @pl.loop(0, inner // GROUP)
+        both = (begin, jnp.zeros((states, GROUP), F32))
+        for part in range(2):
+            k = 2 * g + part
+            half = 1 - part
+            held_states = r.hb.at[k % 2]
+            if k + 1 < 2 * groups:
+                states_in(k + 1).start()
+            states_in(k).wait()
+
+            def second_pass(turn, both):
+                state, total = both
+                step = steps - 1 - turn
+                base = pl.multiple_of(step * CHUNK * states - half * span, states)
+                for i in reversed(range(CHUNK)):
+                    t = step * CHUNK + i
+                    dt = r.dt_s[pl.ds(t, 1), here]
+                    adjoint = state + r.sg_s[pl.ds(t, 1), here] * widen(
+                        r.cb_s[t], GROUP
+                    )
+                    state = jnp.exp2(dt * rate2) * adjoint
+                    held = held_states[pl.ds(base + i * states, states), :]
+                    rated = state * held.astype(F32) * rate
+                    total = total + dt * rated
+                    r.ab_s[pl.ds(i * states, states), :] = adjoint.astype(BF16)
+                    r.rb_s[pl.ds(i * states, states), :] = rated.astype(BF16)
+                tokens = pl.ds(pl.multiple_of(step * CHUNK, CHUNK), CHUNK)
+                from_in = dot(r.bd_s[tokens, :], r.ab_s[...])
+                from_rate = dot(ones, r.rb_s[...])
+                scan_grad = r.sg_s[tokens, here]
+                into_in = dot(r.dx_s[tokens, here].astype(BF16), r.ab_s[...], NT)
+                into_out = dot(
+                    scan_grad.astype(BF16),
+                    held_states[pl.ds(base + states, CHUNK * states), :],
+                    NT,
+                )
+                if g == 0:
+                    r.pin_s[tokens, :] = into_in
+                    r.pout_s[tokens, :] = into_out
+                else:
+                    r.pin_s[tokens, :] += into_in
+                    r.pout_s[tokens, :] += into_out
+                r.stepg_s[tokens, here] = (
+                    r.act[tokens, here].astype(F32) * from_in + from_rate
+                )
+                r.sg_s[tokens, here] = (
+                    r.dt_s[tokens, here] * from_in
+                    + r.vec_s[pl.ds(at.skip, 1), here] * scan_grad
+                )
+                return state, total
+
+            for quarter in range(2):
+                low = (2 * part + quarter) * steps // 4
+                high = (2 * part + quarter + 1) * steps // 4
+                both = lax.fori_loop(low, high, second_pass, both)
+                weave(pace)
+        gvec[pl.ds(0, states), here] = both[1]
+
+    win_copy(tiles, 0).start()
+
+    @pl.loop(0, tiles)
     def _(i):
         here = lanes(i, GROUP)
-        pre_grad = stepg_s[pl.ds(0, rows), here] * sigmoid(pre_ref[:, here])
-        gvec_ref[pl.ds(at.dt_b, 1), here] = jnp.sum(pre_grad, axis=0, keepdims=True)
-        prelow_s[:, here] = pre_grad.astype(BF16)
-        dx_s[:, here] = pad_ref[:, here].astype(F32)
+        pre_grad = r.stepg_s[pl.ds(0, rows), here] * sigmoid(r.pre[:, here])
+        gvec[pl.ds(at.dt_b, 1), here] = jnp.sum(pre_grad, axis=0, keepdims=True)
+        r.prelow_s[:, here] = pre_grad.astype(BF16)
+        r.dx_s[:, here] = r.pad[:, here].astype(F32)
 
     small_grad = (
-        dot(prelow_s[...], dtw_ref[...], NT)
-        + gather_back(pin_s[...], rank, states, sp_ref.shape[1])
-        + gather_back(pout_s[...], rank + states, states, sp_ref.shape[1])
+        dot(r.prelow_s[...], r.dtw_s[...], NT)
+        + gather_back(r.pin_s[...], rank, states, at.small)
+        + gather_back(r.pout_s[...], rank + states, states, at.small)
     ).astype(BF16)
 
-    @pl.loop(0, inner // GROUP)
+    @pl.loop(0, tiles)
     def _(i):
         here = lanes(i, GROUP)
-        full_s[pl.ds(at.dt, rank), here] = dot(
-            small_low, prelow_s[:, here], TN
+        r.full_s[pl.ds(at.dt, rank), here] = dot(
+            small_low, r.prelow_s[:, here], TN
         )[:rank]
-        full_s[pl.ds(0, at.small), here] = dot(small_grad, act_ref[:, here], TN)
-        act_grad = sg_s[:, here] + dot(
-            small_grad, sw_ref[pl.ds(0, at.small), here]
-        )
-        total = vec_ref[pl.ds(at.conv_b, 1), here]
+        r.full_s[pl.ds(0, at.small), here] = dot(small_grad, r.act[:, here], TN)
+        act_grad = r.sg_s[:, here] + dot(small_grad, r.sw[pl.ds(0, at.small), here])
+        total = r.vec_s[pl.ds(at.conv_b, 1), here]
         for k in range(taps):
             total = (
                 total
-                + vec_ref[pl.ds(at.conv + k, 1), here]
-                * dx_s[pl.ds(HALO - taps + 1 + k, rows), here]
+                + r.vec_s[pl.ds(at.conv + k, 1), here]
+                * r.dx_s[pl.ds(HALO - taps + 1 + k, rows), here]
             )
         sig = sigmoid(total)
         conv_grad = act_grad * sig * (1.0 + total * (1.0 - sig))
-        stepg_s[pl.ds(0, rows), here] = conv_grad
-        gvec_ref[pl.ds(at.conv_b, 1), here] = jnp.sum(conv_grad, axis=0, keepdims=True)
+        r.stepg_s[pl.ds(0, rows), here] = conv_grad
+        gvec[pl.ds(at.conv_b, 1), here] = jnp.sum(conv_grad, axis=0, keepdims=True)
         for k in range(taps):
-            gvec_ref[pl.ds(at.conv + k, 1), here] = jnp.sum(
-                conv_grad * dx_s[pl.ds(HALO - taps + 1 + k, rows), here],
+            gvec[pl.ds(at.conv + k, 1), here] = jnp.sum(
+                conv_grad * r.dx_s[pl.ds(HALO - taps + 1 + k, rows), here],
                 axis=0,
                 keepdims=True,
             )
 
     def edge():
         return pltpu.make_async_remote_copy(
-            stepg_s.at[pl.ds(0, 8)],
-            halo_s,
-            halo_sem.at[0],
-            halo_sem.at[1],
+            r.stepg_s.at[pl.ds(0, 8)],
+            r.halo_s,
+            r.halo_sem.at[0],
+            r.halo_sem.at[1],
             device_id=(ctx, jnp.maximum(me - 1, 0)),
             device_id_type=MESH,
         )
@@ -916,54 +1148,45 @@
     def _():
         edge().start()
 
-    tiles = inner // GROUP
-
-    def project(i, first):
+    weave(pace)
+    in_shape = r.stage_in.shape[1:]
+
+    def project(i, turn):
         here = lanes(i, GROUP)
-        slot = lax.rem(i, 2)
+        slot = lax.rem(turn, 2)
         copy = pltpu.make_async_copy(
-            stage_in.at[slot], gin_hbm.at[here], in_sem.at[slot]
-        )
-
-        @pl.when(first >= 2)
+            r.stage_in.at[slot], block_of(r.gin, i), r.in_sem.at[slot]
+        )
+        following = lax.rem(i + 1, 2 * tiles)
+
+        @pl.when(turn + 1 < 2 * tiles)
+        def _():
+            win_copy(following, 1 - slot).start()
+
+        @pl.when(turn >= 2)
         def _():
             copy.wait()
 
-        stage_in[slot] = dot(pb_s[:, here], normed_s[...], TN).astype(BF16)
+        r.stage_in[slot] = (
+            dot(r.pb_s[:, here], r.normed_s[...], TN).astype(BF16).reshape(in_shape)
+        )
         copy.start()
-        part = dot(pb_s[:, here], win_ref[here, :])
-
-        @pl.when(first == 0)
+        win_copy(i, slot).wait()
+        part = dot(r.pb_s[:, here], r.win_s[slot].reshape(GROUP, width))
+
+        @pl.when(turn == 0)
         def _():
-            nsg_ref[...] = part
-
-        @pl.when(first > 0)
+            r.nsg[...] = part
+
+        @pl.when(turn > 0)
         def _():
-            nsg_ref[...] += part
+            r.nsg[...] += part
 
     @pl.loop(0, tiles)
     def _(i):
         project(i + tiles, i)
 
-    out_rows = stage_out.shape[1]
-    for r in range(width // out_rows):
-        slot = r % 2
-        copy = pltpu.make_async_copy(
-            stage_out.at[slot],
-            gout_hbm.at[pl.ds(r * out_rows, out_rows)],
-            out_sem.at[slot],
-        )
-        if r >= 2:
-            copy.wait()
-
-        @pl.loop(0, tiles)
-        def _(i):
-            here = lanes(i, GROUP)
-            stage_out[slot, :, here] = dot(
-                low_s[:, pl.ds(r * out_rows, out_rows)], mixed_ref[:, here], TN
-            ).astype(BF16)
-
-        copy.start()
+    weave(pace)
 
     @pl.when(me < count - 1)
     def _():
@@ -971,13 +1194,13 @@
 
     @pl.when(me == count - 1)
     def _():
-        halo_s[...] = jnp.zeros_like(halo_s)
+        r.halo_s[...] = jnp.zeros_like(r.halo_s)
 
     @pl.when(me > 0)
     def _():
         edge().wait_send()
 
-    stepg_s[pl.ds(rows, 8), :] = halo_s[...]
+    r.stepg_s[pl.ds(rows, 8), :] = r.halo_s[...]
 
     @pl.loop(0, tiles)
     def _(i):
@@ -986,39 +1209,53 @@
         for k in range(taps):
             total = (
                 total
-                + vec_ref[pl.ds(at.conv + k, 1), here]
-                * stepg_s[pl.ds(taps - 1 - k, rows), here]
+                + r.vec_s[pl.ds(at.conv + k, 1), here]
+                * r.stepg_s[pl.ds(taps - 1 - k, rows), here]
             )
-        pb_s[:, here] = total.astype(BF16)
+        r.pb_s[:, here] = total.astype(BF16)
         project(i, i + tiles)
 
-    stream = stream_ref[...]
+    stream = r.stream[...]
     scale = lax.rsqrt(jnp.mean(stream * stream, axis=1, keepdims=True) + EPS)
-    normed_grad = nsg_ref[...]
+    normed_grad = r.nsg[...]
     gain_grad = jnp.sum(normed_grad * stream * scale, axis=0, keepdims=True)
     gain_grad = jnp.broadcast_to(gain_grad, (8, width)).astype(BF16)
     pick = gain_pick(channels)
     for i in range(inner // 256):
         wide = dot(gain_grad[:, 128 * i : 128 * i + 128], pick, NT)
-        gvec_ref[pl.ds(at.gain, 1), pl.ds(256 * i, 256)] = wide[:1]
+        gvec[pl.ds(at.gain, 1), pl.ds(256 * i, 256)] = wide[:1]
     for k in range(at.count, at.rows):
-        full_s[pl.ds(k, 1), :] = jnp.zeros((1, inner), F32)
-    if len(gsmall_ref.shape) == 3:
-        split_small(channels, full_s, gsmall_ref)
+        r.full_s[pl.ds(k, 1), :] = jnp.zeros((1, inner), F32)
+    if mode == "given":
+        r.gsmall[...] = r.full_s[...]
+    elif mode == "last":
+        split_small(channels, r.full_s, r.gsmall)
     else:
-        gsmall_ref[...] = full_s[...]
+        split_small(channels, r.full_s, Folded(r.gsmall_s))
+        small_copy = pltpu.make_async_copy(r.gsmall_s, r.gsmall_hbm, r.small_sem.at[0])
+        small_copy.start()
     scaled = normed_grad * gain
     inner_sum = jnp.mean(scaled * stream, axis=1, keepdims=True)
-    nsg_ref[...] = (
-        sgrad_ref[...] + scale * scaled - stream * (scale * scale * scale) * inner_sum
+    r.nsg[...] = (
+        r.sgrad[...] + scale * scaled - stream * (scale * scale * scale) * inner_sum
     )
     for slot in range(2):
         pltpu.make_async_copy(
-            stage_in.at[slot], gin_hbm.at[pl.ds(0, GROUP)], in_sem.at[slot]
+            r.stage_in.at[slot], block_of(r.gin, 0), r.in_sem.at[slot]
         ).wait()
-        pltpu.make_async_copy(
-            stage_out.at[slot], gout_hbm.at[pl.ds(0, out_rows)], out_sem.at[slot]
-        ).wait()
+    weave(len(queue))
+    if mode == "first":
+        small_copy.wait()
+        reduce.finish()
+        for partner in square_partners(depth):
+            signal(r.ready_sem, partner)
+        pl.semaphore_wait(r.ready_sem, len(square_partners(depth)))
+        for item in own_items:
+            reduce.begin(item)
+        for turn in reduce.turns(own_items):
+            turn()
+    if mode != "given":
+        reduce.finish()
     each(0, me, lambda j: sums(j, me).wait_send())
     for g in range(groups):
         each(0, me, lambda j: ends(g, j, me).wait_send())
@@ -1119,251 +1356,125 @@
     return {entry[0]: result for entry, result in zip(outputs, results)}
 
 
-def backward_call(cfg, in_blocks, sgrad, stream, sw, win, wout, saved):
+def backward_call(cfg, mode, sgrad, stream, weights, saved, later):
     rows, inner, states, taps, rank, count, channels = cfg
     at = Names(states, taps, rank)
     width = stream.shape[1]
-    small = rank + 2 * states
     groups = inner // GROUP
     wide = CHUNK * states
+    depth = count // 2
+    sw, win, wout = weights
     shape = jax.ShapeDtypeStruct
     dma = pltpu.SemaphoreType.DMA
-    return pl.pallas_call(
-        functools.partial(backward_kernel, cfg),
-        out_shape=(
-            shape((rows, width), F32),
-            shape((2 * inner, width), BF16),
-            shape((width, inner), BF16),
-            shape((inner // channels, at.rows * channels // 128, 128), BF16)
-            if in_blocks
-            else shape((at.rows, inner), F32),
+    vmem, any_space = in_vmem(1)[0], in_any(1)[0]
+    in_rows, out_rows = win.shape[1], wout.shape[1]
+    lead = (1, 1, win.shape[0] // 2, 2) if mode == "given" else (2, 2, depth, 2)
+    small_rows = at.rows * channels // 128
+    inputs = [
+        ("sgrad", sgrad, vmem),
+        ("stream", stream, vmem),
+        ("sw", sw, vmem),
+        ("win", win, any_space),
+        ("wout", wout, any_space),
+    ]
+    for name in ("pad", "act", "sp", "pre", "mixed"):
+        inputs.append((name, saved[name], vmem))
+    for name in ("gate", "y", "h_hbm"):
+        inputs.append((name, saved[name], any_space))
+    outputs = [
+        ("nsg", shape((rows, width), F32), vmem),
+        ("gin", shape(lead + (in_rows, width), BF16), any_space),
+        ("gout", shape(lead + (out_rows, inner), BF16), any_space),
+    ]
+    scratch = [
+        ("full_s", pltpu.VMEM((at.rows, inner), F32)),
+        ("vec_s", pltpu.VMEM((at.rows - at.vec, inner), F32)),
+        ("dtw_s", pltpu.VMEM((at.small, inner), BF16)),
+        ("hb", pltpu.VMEM((2, (rows // 2 + 1) * states, GROUP), BF16)),
+        ("normed_s", pltpu.VMEM((rows, width), BF16)),
+        ("low_s", pltpu.VMEM((rows, width), BF16)),
+        ("sg_s", pltpu.VMEM((rows, inner), F32)),
+        ("dt_s", pltpu.VMEM((rows, inner), F32)),
+        ("dx_s", pltpu.VMEM((rows + HALO, inner), F32)),
+        ("stepg_s", pltpu.VMEM((rows + 8, inner), F32)),
+        ("pb_s", pltpu.VMEM((rows, 2 * inner), BF16)),
+        ("cb_s", pltpu.VMEM((rows, states, 128), F32)),
+        ("bd_s", pltpu.VMEM((rows, wide), BF16)),
+        ("ab_s", pltpu.VMEM((wide, GROUP), BF16)),
+        ("rb_s", pltpu.VMEM((wide, GROUP), BF16)),
+        ("pin_s", pltpu.VMEM((rows, wide), F32)),
+        ("pout_s", pltpu.VMEM((rows, wide), F32)),
+        ("prelow_s", pltpu.VMEM((rows, inner), BF16)),
+        ("stage_in", pltpu.VMEM((2, 2, 2, in_rows, width), BF16)),
+        ("stage_out", pltpu.VMEM((2, 2, 2, out_rows, inner), BF16)),
+        ("win_s", pltpu.VMEM((2, GROUP // in_rows, in_rows, width), BF16)),
+        ("wout_s", pltpu.VMEM((2,) + wout.shape[:2] + (GROUP,), BF16)),
+        ("gate_s", pltpu.VMEM((2, 2, rows, GROUP), F32)),
+        ("halo_s", pltpu.VMEM((8, inner), F32)),
+        ("own_sum", pltpu.VMEM((8, inner // 8), F32)),
+        ("sum_s", pltpu.VMEM((count, 8, inner // 8), F32)),
+        ("own_end", pltpu.VMEM((states, inner), BF16)),
+        ("end_s", pltpu.VMEM((count, states, inner), BF16)),
+        ("halo_sem", dma((2,))),
+        ("sum_send", dma((count,))),
+        ("sum_recv", dma((count,))),
+        ("end_send", dma((groups, count))),
+        ("end_recv", dma((groups, count))),
+        ("h_sem", dma((2,))),
+        ("in_sem", dma((2,))),
+        ("out_sem", dma((2,))),
+        ("win_sem", dma((2,))),
+        ("wout_sem", dma((2,))),
+        ("gate_sem", dma((2, 2))),
+    ]
+    if mode == "given":
+        outputs.append(("gsmall", shape((at.rows, inner), F32), vmem))
+    else:
+        outputs.append(("sum_out", shape((out_rows, inner), F32), vmem))
+        held = [("rout", out_rows // 2, inner, 2)]
+        pieces = 2
+        if mode == "last":
+            small_shape = (inner // channels, small_rows, 128)
+            outputs.append(("gsmall", shape(small_shape, BF16), vmem))
+        else:
+            inputs.append(("next_gin", later["gin"], any_space))
+            small = later["gsmall"].reshape(lead + (small_rows, 128))
+            inputs.append(("next_gsmall", small, any_space))
+            outputs.append(("gsmall_hbm", shape(small.shape, BF16), any_space))
+            scratch.append(("gsmall_s", pltpu.VMEM(small.shape, BF16)))
+            for name in ("sum_in", "sum_next_in"):
+                outputs.append((name, shape((in_rows, width), F32), vmem))
+            for name in ("sum_small", "sum_next_small"):
+                outputs.append((name, shape((small_rows, 128), F32), vmem))
+            held.append(("rin", in_rows // 2, width, 2))
+            held.append(("rsmall", small_rows, 128, 1))
+            scratch.append(("small_sem", dma((1,))))
+            scratch.append(("ready_sem", pltpu.SemaphoreType.REGULAR))
+            pieces = 8
+        for name, piece, wide_by, cuts in held:
+            for k in range(cuts):
+                for part, buffer in enumerate(Reduce.buffers_of(depth, piece, wide_by)):
+                    scratch.append((f"{name}{k}_{part}", buffer))
+        scratch += [
+            ("own_sem", dma((pieces, 2))),
+            ("send_sem", dma((pieces, 4, depth))),
+            ("recv_sem", dma((pieces, 4, depth))),
+        ]
+    names = [entry[0] for entry in inputs + outputs + scratch]
+    results = pl.pallas_call(
+        functools.partial(backward_kernel, cfg, mode, names),
+        out_shape=tuple(entry[1] for entry in outputs),
+        in_specs=[entry[2] for entry in inputs],
+        out_specs=tuple(entry[2] for entry in outputs),
+        scratch_shapes=[entry[1] for entry in scratch],
+        compiler_params=pltpu.CompilerParams(
+            collective_id={"given": 1, "last": 6, "first": 7}[mode],
+            has_side_effects=True,
+            vmem_limit_bytes=VMEM_BYTES,
         ),
-        in_specs=in_vmem(10) + in_any(1) + in_vmem(2),
-        out_specs=tuple(in_vmem(1) + in_any(2) + in_vmem(1)),
-        scratch_shapes=[
-            pltpu.VMEM((at.rows, inner), F32),
-            pltpu.VMEM((at.rows - at.vec, inner), F32),
-            pltpu.VMEM((small, inner), BF16),
-            pltpu.VMEM((2, (rows + 1) * states, GROUP), BF16),
-            pltpu.VMEM((rows, width), BF16),
-            pltpu.VMEM((rows, width), BF16),
-            pltpu.VMEM((rows, inner), F32),
-            pltpu.VMEM((rows, inner), F32),
-            pltpu.VMEM((rows + HALO, inner), F32),
-            pltpu.VMEM((rows + 8, inner), F32),
-            pltpu.VMEM((rows, 2 * inner), BF16),
-            pltpu.VMEM((rows, states, 128), F32),
-            pltpu.VMEM((rows, wide), BF16),
-            pltpu.VMEM((wide, GROUP), BF16),
-            pltpu.VMEM((wide, GROUP), BF16),
-            pltpu.VMEM((rows, wide), F32),
-            pltpu.VMEM((rows, wide), F32),
-            pltpu.VMEM((rows, inner), BF16),
-            pltpu.VMEM((2, GROUP, width), BF16),
-            pltpu.VMEM((2, width // 8, inner), BF16),
-            pltpu.VMEM((8, inner), F32),
-            pltpu.VMEM((8, inner // 8), F32),
-            pltpu.VMEM((count, 8, inner // 8), F32),
-            pltpu.VMEM((states, inner), BF16),
-            pltpu.VMEM((count, states, inner), BF16),
-            dma((2,)),
-            dma((count,)),
-            dma((count,)),
-            dma((groups, count)),
-            dma((groups, count)),
-            dma((2,)),
-            dma((2,)),
-            dma((2,)),
-        ],
-        compiler_params=pltpu.CompilerParams(
-            collective_id=1, has_side_effects=True, vmem_limit_bytes=VMEM_BYTES
-        ),
-        name="backward_layer",
-    )(sgrad, stream, sw, win, wout, *saved)
-
-
-def parts_of(in_rows, out_rows, small_rows):
-    cut = in_rows * 3 // 4 // 16 * 16
-    return (
-        (0, 0, cut, 1),
-        (2, 0, small_rows, 1),
-        (0, cut, in_rows - cut, 0),
-        (1, 0, out_rows, 0),
-    )
-
-
-def reduce_kernel(depth, parts, *refs):
-    whole, outs = refs[:3], refs[3:6]
-    pieces = len(parts)
-    own = refs[6 : 6 + pieces]
-    core_in = refs[6 + pieces : 6 + 2 * pieces]
-    first_in = refs[6 + 2 * pieces : 6 + 3 * pieces]
-    second_in = refs[6 + 3 * pieces : 6 + 4 * pieces]
-    line_in = refs[6 + 4 * pieces : 6 + 5 * pieces]
-    own_sem, send_sem, recv_sem = refs[6 + 5 * pieces :]
-    y, x, z, core = places()
-    greet_square(depth)
-    line = [lax.rem(z + step + 1, depth) for step in range(depth)]
-    x_side, y_side = device(y, 1 - x, z, core), device(1 - y, x, z, core)
-    sibling = device(y, x, z, 1 - core)
-
-    def part_of(part, step, side):
-        array, first, rows, _ = parts[part]
-        return whole[array].at[:, :, line[step], side, pl.ds(first, rows)]
-
-    def local(part, step):
-        return pltpu.make_async_copy(
-            part_of(part, step, core), own[part].at[step], own_sem.at[step, part]
-        )
-
-    def remote(stage, part, step, source, target, to):
-        return pltpu.make_async_remote_copy(
-            source,
-            target,
-            send_sem.at[stage, step, part],
-            recv_sem.at[stage, step, part],
-            device_id=to,
-            device_id_type=MESH,
-        )
-
-    def hop(stage, part, step):
-        crosses_y = parts[part][3] == 1
-        if stage == 0:
-            return remote(
-                0,
-                part,
-                step,
-                part_of(part, step, 1 - core),
-                core_in[part].at[step],
-                sibling,
-            )
-        if stage == 1:
-            source = (
-                core_in[part].at[step, 1 - y]
-                if crosses_y
-                else core_in[part].at[step, :, 1 - x]
-            )
-            to = y_side if crosses_y else x_side
-            return remote(1, part, step, source, first_in[part].at[step], to)
-        if stage == 2:
-            source = first_in[part].at[step, 1 - x if crosses_y else 1 - y]
-            to = x_side if crosses_y else y_side
-            return remote(2, part, step, source, second_in[part].at[step], to)
-        to = device(y, x, line[step], core)
-        return remote(
-            3, part, step, second_in[part].at[step], line_in[part].at[step], to
-        )
-
-    def add(target, other, rows):
-        @pl.loop(0, rows // 16)
-        def _(r):
-            here = pl.ds(pl.multiple_of(r * 16, 16), 16)
-            target[here] = (
-                target[here].astype(F32) + other[here].astype(F32)
-            ).astype(BF16)
-
-    def settle(stage, part, step):
-        rows = parts[part][2]
-        crosses_y = parts[part][3] == 1
-        hop(stage, part, step).wait_recv()
-        if stage == 0:
-            local(part, step).wait()
-            for far_y in (0, 1):
-                for far_x in (0, 1):
-                    add(
-                        core_in[part].at[step, far_y, far_x],
-                        own[part].at[step, far_y, far_x],
-                        rows,
-                    )
-        elif stage == 1:
-            for far in (0, 1):
-                kept = (
-                    core_in[part].at[step, y, far]
-                    if crosses_y
-                    else core_in[part].at[step, far, x]
-                )
-                add(first_in[part].at[step, far], kept, rows)
-        elif stage == 2:
-            add(
-                second_in[part].at[step],
-                first_in[part].at[step, x if crosses_y else y],
-                rows,
-            )
-
-    everything = range(pieces)
-    for step in range(depth):
-        for part in everything:
-            hop(0, part, step).start()
-            local(part, step).start()
-    for turn in range(depth + 2):
-        for stage in range(3):
-            step = turn - stage
-            if 0 <= step < depth:
-                for part in everything:
-                    settle(stage, part, step)
-                    if stage < 2 or step < depth - 1:
-                        hop(stage + 1, part, step).start()
-    for step in range(depth - 1):
-        for part in everything:
-            hop(3, part, step).wait_recv()
-    for part in everything:
-        array, first, rows, _ = parts[part]
-
-        @pl.loop(0, rows // 16)
-        def _(r):
-            here = pl.ds(pl.multiple_of(r * 16, 16), 16)
-            total = second_in[part][depth - 1, here].astype(F32)
-            for step in range(depth - 1):
-                total = total + line_in[part][step, here].astype(F32)
-            there = pl.ds(pl.multiple_of(first + r * 16, 16), 16)
-            outs[array][there] = total
-
-    for step in range(depth):
-        for part in everything:
-            for stage in range(4):
-                if stage < 3 or step < depth - 1:
-                    hop(stage, part, step).wait_send()
-
-
-def reduce_call(depth, whole):
-    count = 8 * depth
-    sizes = [array.shape[0] // count for array in whole]
-    widths = [array.shape[1] for array in whole]
-    parts = parts_of(*sizes)
-    shaped = [
-        array.reshape(2, 2, depth, 2, size, wide)
-        for array, size, wide in zip(whole, sizes, widths)
-    ]
-
-    def buffers(lead):
-        return [
-            pltpu.VMEM(lead + (rows, widths[array]), BF16)
-            for array, _, rows, _ in parts
-        ]
-
-    dma = pltpu.SemaphoreType.DMA
-    return pl.pallas_call(
-        functools.partial(reduce_kernel, depth, parts),
-        out_shape=tuple(
-            jax.ShapeDtypeStruct((size, wide), F32) for size, wide in zip(sizes, widths)
-        ),
-        in_specs=in_any(3),
-        out_specs=tuple(in_vmem(3)),
-        scratch_shapes=buffers((depth, 2, 2))
-        + buffers((depth, 2, 2))
-        + buffers((depth, 2))
-        + buffers((depth,))
-        + buffers((depth,))
-        + [
-            dma((depth, len(parts))),
-            dma((4, depth, len(parts))),
-            dma((4, depth, len(parts))),
-        ],
-        compiler_params=pltpu.CompilerParams(
-            collective_id=3, has_side_effects=True, vmem_limit_bytes=VMEM_BYTES
-        ),
-        name="reduce_gradients",
-    )(*shaped)
+        name="backward_" + mode,
+    )(*[entry[1] for entry in inputs])
+    return {entry[0]: result for entry, result in zip(outputs, results)}
 
 
 def on_device(
@@ -1426,7 +1537,6 @@
         (in_weight[layer].T, out_weight[layer].T, pack(layer))
         for layer in range(layers)
     ]
-    kept = ("pad", "gate", "act", "sp", "pre", "h_hbm", "y", "mixed")
     stream = hidden_in.astype(F32)
     streams, runs, weights = [], [], []
     if by_kernel:
@@ -1448,12 +1558,7 @@
         runs = [first, second]
         wins = [first["win_all"], first["win2_all"]]
         weights = [
-            (
-                run["sw"],
-                win.reshape(2 * inner, width),
-                run["wout_all"].reshape(width, inner),
-            )
-            for run, win in zip(runs, wins)
+            (run["sw"], win, run["wout_all"]) for run, win in zip(runs, wins)
         ]
         streams = [stream, first["new"]]
         stream = second["new"]
@@ -1462,43 +1567,61 @@
             w_in = lax.all_gather(w_in, ("ctx", "seq"), axis=0, tiled=True)
             w_out = lax.all_gather(w_out, ("ctx", "seq"), axis=0, tiled=True)
             sw = lax.all_gather(w_small, ("ctx", "seq"), axis=1, tiled=True)
-            operands = [
-                ("win_hbm", w_in.reshape(-1, 128, width)),
-                ("sw", sw),
-                ("wout_hbm", w_out.reshape(-1, 32, inner)),
-            ]
+            w_in = w_in.reshape(-1, 128, width)
+            w_out = w_out.reshape(-1, 32, inner)
+            operands = [("win_hbm", w_in), ("sw", sw), ("wout_hbm", w_out)]
             run = forward_call(cfg, "given", stream, operands)
             runs.append(run)
             weights.append((sw, w_in, w_out))
             streams.append(stream)
             stream = run["new"]
     stream_grad = cotangent.astype(F32)
-    grads = [None] * layers
-    for layer in reversed(range(layers)):
-        stream_grad, g_in, g_out, g_small = backward_call(
-            cfg,
-            by_kernel,
-            stream_grad,
-            streams[layer],
-            *weights[layer],
-            [runs[layer][name] for name in kept],
-        )
-        if by_kernel:
-            s_in, s_out, s_small = reduce_call(
-                depth, (g_in, g_out, g_small.reshape(-1, 128))
+    summed = [None] * layers
+    if by_kernel:
+        last = backward_call(
+            cfg, "last", stream_grad, streams[1], weights[1], runs[1], None
+        )
+        head = backward_call(
+            cfg, "first", last["nsg"], streams[0], weights[0], runs[0], last
+        )
+        stream_grad = head["nsg"]
+
+        def unfold(small):
+            small = small.reshape(-1, 128 // channels, channels)
+            return small.transpose(1, 0, 2).reshape(at.rows, channels)
+
+        summed = [
+            (head["sum_in"], head["sum_out"], unfold(head["sum_small"])),
+            (head["sum_next_in"], last["sum_out"], unfold(head["sum_next_small"])),
+        ]
+    else:
+        for layer in reversed(range(layers)):
+            run = backward_call(
+                cfg,
+                "given",
+                stream_grad,
+                streams[layer],
+                weights[layer],
+                runs[layer],
+                None,
             )
-            s_small = s_small.reshape(-1, 128 // channels, channels)
-            s_small = s_small.transpose(1, 0, 2).reshape(at.rows, channels)
-        else:
-            s_in, s_out, s_small = [
+            stream_grad = run["nsg"]
+            summed[layer] = [
                 lax.psum_scatter(
                     array.astype(F32),
                     ("ctx", "seq"),
                     scatter_dimension=dim,
                     tiled=True,
                 )
-                for array, dim in ((g_in, 0), (g_out, 0), (g_small, 1))
+                for array, dim in (
+                    (run["gin"].reshape(-1, width), 0),
+                    (run["gout"].reshape(-1, inner), 0),
+                    (run["gsmall"], 1),
+                )
             ]
+    grads = [None] * layers
+    for layer in range(layers):
+        s_in, s_out, s_small = summed[layer]
         s_x = s_small[: at.small, :channels]
         s_dt = s_small[at.dt : at.dt + rank, :channels]
         s_vec = s_small[at.vec : at.count, :channels]

time: 536 us -> 484 us (0.903)
  Pallas kernels: 498 us -> 443 us
    pallas_call x4 -> x2, Pallas kernels: 301 us -> 246 us  [backward_call(): pl.pallas_call(functools.partial(backward_kernel, cfg, mode, names), out_...]
where the time goes in v3:
time: 484 us; the launch traced here: 475 us
  Pallas kernels  443 us (92%)
  local copies, waits for them, and re-layouts  16.8 us (3%)
  other arithmetic  14 us (3%)
    pallas_call x2, Pallas kernels, backward_call(): pl.pallas_call(functools.partial(backward_kernel, cfg, mode, names), out_...  246 us
    pallas_call x2, Pallas kernels, forward_call(): pl.pallas_call(functools.partial(forward_kernel, cfg, mode, names), out_s...  197 us

profile of v3, /device:TPU:0, one launch (start us, length us, event | category | flops | bytes accessed | tf_op | source)
XLA Modules:
  0.0 475.3 jit_solution(13103377916471112193)
XLA Ops:
  0.7 0.7 slice_bitcast_fusion.16
  1.4 0.7 fusion.6
  2.1 0.7 fusion.4
  3.6 0.7 slice_bitcast_fusion.12
  4.3 0.7 fusion.3
  5.2 0.7 slice_bitcast_fusion.10
  7.5 1.7 slice_bitcast_fusion
  9.2 1.1 fusion
  10.3 0.9 copy.80
  11.2 0.8 copy.78
  12.0 2.1 convert_element_type.15.refs_0_.refs_1_
  14.1 1.1 convert_element_type.17.refs_0_
  15.2 134.5 %forward_first.1 = (f32[256,1024]{1,0:T(8,128)}, bf16[272,2048]{1,0:T(8,128)(2,1)}, f32[256,2048]{1,0:T(8,128)}, bf16[256,2048]{1,0:T(8,128)(2,1)}, f32[256,96]{...) custom-call(f32[256,1024]{1,0:T(8,128)} %convert_element_type.15.ref, ...), custom_call_target="tpu_custom_call" | custom-call | tf_op jit(solution)/shard_map/forward_first/pallas_call | solution.py:1343
  149.7 62.5 %forward_later.1 = (f32[256,1024]{1,0:T(8,128)}, bf16[272,2048]{1,0:T(8,128)(2,1)}, f32[256,2048]{1,0:T(8,128)}, bf16[256,2048]{1,0:T(8,128)(2,1)}, f32[256,96]{...) custom-call(f32[256,1024]{1,0:T(8,128)} %get-tuple-element.47.refs_0, ...), custom_call_target="tpu_custom_call" | custom-call | tf_op jit(solution)/shard_map/forward_later/pallas_call | solution.py:1343
  212.2 2.1 convert_element_type.16
  214.3 88.4 %backward_last.1 = (f32[256,1024]{1,0:T(8,128)}, bf16[2,2,4,2,128,1024]{5,4,3,2,1,0:T(8,128)(2,1)}, bf16[2,2,4,2,32,2048]{5,4,3,2,1,0:T(8,128)(2,1)}, f32[32,2048]{1,0:T(8,128)}, bf16[32,96,128]{2,1,0:T(8,128)(2,1)}) custom-call(f32[256,1024]{1,0:T(8,128)} %convert_element_type.17.refs_0_, f32[256,1024]{1,0:T(8,128)} %get-tuple-element.47.refs_0_.refs_1_, ...), custom_call_target="tpu_custom_call" | custom-call | tf_op jit(solution)/shard_map/backward_last/pallas_call | solution.py:1464
  302.8 157.9 %backward_first.1 = (f32[256,1024]{1,0:T(8,128)}, bf16[2,2,4,2,128,1024]{5,4,3,2,1,0:T(8,128)(2,1)}, bf16[2,2,4,2,32,2048]{5,4,3,2,1,0:T(8,128)(2,1)}, f32[32,20...) custom-call(f32[256,1024]{1,0:T(8,128)} %get-tuple-element.61.refs_0, ...), custom_call_target="tpu_custom_call" | custom-call | tf_op jit(solution)/shard_map/backward_first/pallas_call | solution.py:1464
  460.7 1.0 copy.60
  462.7 0.9 copy.62
  465.2 0.7 copy.77
  469.5 1.8 pad_maximum_fusion.1
  471.3 1.3 pad_maximum_fusion
  472.6 1.3 copy.76
  473.9 1.0 copy.83
  (52 shorter events, 8.6 us)
Async XLA Ops:
  0.6 13.5 %copy-start.1 = (bf16[256,1024]{1,0:T(8,128)(2,1)S(1)}, bf16[256,1024]{1,0:T(8,128)(2,1)}, u32[]{:S(2)}) copy-start(bf16[256,1024]{1,0:T(8,128)(2,1)} %param.13) | copy-start | bytes 1572868
  302.8 166.8 %copy-start.2 = (f32[32,2048]{1,0:T(8,128)S(1)}, f32[32,2048]{1,0:T(8,128)}, u32[]{:S(2)}) copy-start(f32[32,2048]{1,0:T(8,128)} %get-tuple-element.81) | copy-start | bytes 786436
  460.7 13.2 %copy-start = (f32[256,1024]{1,0:T(8,128)S(1)}, f32[256,1024]{1,0:T(8,128)}, u32[]{:S(2)}) copy-start(f32[256,1024]{1,0:T(8,128)} %get-tuple-element.173) | copy-start | bytes 3145732

commit v4 on v3

--- a/solution.py
+++ b/solution.py
@@ -344,15 +344,15 @@
         self.sent = []
 
     @staticmethod
-    def buffers_of(depth, rows, width):
-        return [
-            pltpu.VMEM(lead + (rows, width), BF16)
-            for lead in ((2, 2, 2), (depth, 2, 2), (depth, 2), (depth,), (depth - 1,))
-        ]
-
-    def part_of(self, item, step, side):
-        whole, _, first, rows, _ = self.pieces[item]
-        return whole.at[:, :, self.line[step], side, pl.ds(first, rows)]
+    def buffers_of(depth, rows, width, sided=False):
+        square, row = ((2,), ()) if sided else ((2, 2), (2,))
+        leads = ((2,) + square, (depth,) + square, (depth,) + row, (depth,), (depth - 1,))
+        return [pltpu.VMEM(lead + (rows, width), BF16) for lead in leads]
+
+    def part_of(self, item, step, core):
+        whole, _, first, rows, _, side = self.pieces[item]
+        y = slice(None) if side is None else side
+        return whole.at[y, :, self.line[step], core, pl.ds(first, rows)]
 
     def local(self, item, step):
         return pltpu.make_async_copy(
@@ -363,16 +363,24 @@
 
     def hop(self, stage, item, step):
         _, core_in, first_in, second_in, line_in = self.buffers[item]
-        crosses_y = self.pieces[item][4]
+        crosses_y, side = self.pieces[item][4:]
         y, x = self.y, self.x
         if stage == 0:
             source = self.part_of(item, step, 1 - self.core)
             target, to = core_in.at[step], self.sibling
         elif stage == 1:
-            source = core_in.at[step, 1 - y] if crosses_y else core_in.at[step, :, 1 - x]
+            if side is not None:
+                source = core_in.at[step, 1 - x]
+            elif crosses_y:
+                source = core_in.at[step, 1 - y]
+            else:
+                source = core_in.at[step, :, 1 - x]
             target, to = first_in.at[step], self.y_side if crosses_y else self.x_side
         elif stage == 2:
-            source = first_in.at[step, 1 - x if crosses_y else 1 - y]
+            if side is not None:
+                source = first_in.at[step]
+            else:
+                source = first_in.at[step, 1 - x if crosses_y else 1 - y]
             target, to = second_in.at[step], self.x_side if crosses_y else self.y_side
         else:
             source, target, to = second_in.at[step], line_in.at[step], self.along[step]
@@ -385,10 +393,19 @@
             device_id_type=MESH,
         )
 
+    def when(self, stage, item, receives, act):
+        side = self.pieces[item][5]
+        if side is None or stage < 2:
+            act()
+        elif stage == 2 and not receives:
+            pl.when(self.y != side)(act)
+        else:
+            pl.when(self.y == side)(act)
+
     def send(self, stage, item, step):
         copy = self.hop(stage, item, step)
-        copy.start()
-        self.sent.append(copy)
+        self.when(stage, item, False, copy.start)
+        self.sent.append((stage, item, copy))
 
     @staticmethod
     def add(target, other, rows):
@@ -406,17 +423,30 @@
                 self.local(item, step).start()
 
     def settle(self, stage, item, step):
+        self.when(
+            stage, item, True, functools.partial(self.receive, stage, item, step)
+        )
+        if stage < 2 or step < self.depth - 1:
+            self.send(stage + 1, item, step)
+
+    def receive(self, stage, item, step):
         own, core_in, first_in, second_in, _ = self.buffers[item]
-        rows, crosses_y = self.pieces[item][3:]
+        rows, crosses_y, side = self.pieces[item][3:]
         self.hop(stage, item, step).wait_recv()
         if stage == 0:
             self.local(item, step).wait()
-            for y in (0, 1):
-                for x in (0, 1):
+            for x in (0, 1):
+                if side is not None:
+                    self.add(core_in.at[step, x], own.at[step % 2, x], rows)
+                    continue
+                for y in (0, 1):
                     self.add(core_in.at[step, y, x], own.at[step % 2, y, x], rows)
             if step + 2 < self.depth:
                 self.local(item, step + 2).start()
         elif stage == 1:
+            if side is not None:
+                self.add(first_in.at[step], core_in.at[step, self.x], rows)
+                return
             for far in (0, 1):
                 kept = (
                     core_in.at[step, self.y, far]
@@ -424,14 +454,17 @@
                     else core_in.at[step, far, self.x]
                 )
                 self.add(first_in.at[step, far], kept, rows)
+        elif side is not None:
+            self.add(second_in.at[step], first_in.at[step], rows)
         else:
             kept = first_in.at[step, self.x if crosses_y else self.y]
             self.add(second_in.at[step], kept, rows)
-        if stage < 2 or step < self.depth - 1:
-            self.send(stage + 1, item, step)
 
     def last(self, item):
-        _, out, first, rows, _ = self.pieces[item]
+        self.when(3, item, True, functools.partial(self.total, item))
+
+    def total(self, item):
+        _, out, first, rows, _, _ = self.pieces[item]
         second_in, line_in = self.buffers[item][3:]
         for step in range(self.depth - 1):
             self.hop(3, item, step).wait_recv()
@@ -459,8 +492,8 @@
         return actions
 
     def finish(self):
-        for copy in self.sent:
-            copy.wait_send()
+        for stage, item, copy in self.sent:
+            self.when(stage, item, False, copy.wait_send)
         self.sent = []
 
 
@@ -545,7 +578,7 @@
         out_copy = pltpu.make_async_copy(r.wout_hbm, r.wout_s, r.load_sem.at[2])
         out_copy.start()
 
-    stream = r.stream[...]
+    stream = r.stream[...].astype(F32)
     scale = lax.rsqrt(jnp.mean(stream * stream, axis=1, keepdims=True) + EPS)
     stores = []
 
@@ -569,12 +602,14 @@
 
         first_items, next_items = [], []
         if mode == "first":
-            first_items = add_piece(r.own_in, r.win_s, (1, 0))
-            first_items += add_piece(r.own_small, r.gsm_s, (1,))
-        out_items = add_piece(r.own_out, r.wout_s, (1, 0))
+            first_items = add_piece(r.all_in.at[0], r.win_s, (1, 0))
+            first_items += add_piece(r.all_small.at[0], r.gsm_s, (1,))
+        out_items = add_piece(
+            r.all_out.at[0 if mode == "first" else 1], r.wout_s, (1, 0)
+        )
         if mode == "first":
-            next_items = add_piece(r.next_in, r.win2_all, (1, 0))
-            next_items += add_piece(r.next_small, r.gsm2_all, (0,))
+            next_items = add_piece(r.all_in.at[1], r.win2_all, (1, 0))
+            next_items += add_piece(r.all_small.at[1], r.gsm2_all, (0,))
         gather = Gather(depth, pieces, r.own_sem, r.send_sem, r.recv_sem)
 
         def begin(items):
@@ -611,7 +646,7 @@
         if mode == "later":
             small_copy.wait()
         merge_small(channels, r.gsm_s, r.sw)
-    pace = -(-len(queue) // 21)
+    pace = -(-len(queue) // 33)
 
     load_small(at, r.sw, r.vec_s, r.dtw_s)
     r.normed_s[...] = (stream * scale * gain_row(at, channels, r.vec_s)).astype(BF16)
@@ -718,11 +753,14 @@
                 state = advance(step * CHUNK + i, state, rate2, here)
             return state
 
-        r.own_end[:, here] = lax.fori_loop(
-            0, steps, first_pass, jnp.zeros((states, GROUP), F32)
-        ).astype(BF16)
+        state = jnp.zeros((states, GROUP), F32)
+        for part in range(2):
+            state = lax.fori_loop(
+                steps * part // 2, steps * (part + 1) // 2, first_pass, state
+            )
+            weave(pace)
+        r.own_end[:, here] = state.astype(BF16)
         each(me + 1, count, lambda j: ends(g, j, me).start())
-        weave(pace)
 
     def h_copy(g):
         here = pl.ds(g * GROUP, GROUP)
@@ -757,7 +795,7 @@
             )
             return state
 
-        thirds = 1 if mode == "given" else 3
+        thirds = 1 if mode == "given" else 5
         for part in range(thirds):
             state = lax.fori_loop(
                 steps * part // thirds,
@@ -784,7 +822,9 @@
     for i in range(width // 256):
         here = pl.ds(i * 256, 256)
         wout = r.wout_s[pl.ds(i * out_tile, out_tile)].reshape(256, inner)
-        r.new[:, here] = r.stream[:, here] + dot(r.mixed[...], wout, NT)
+        r.new[:, here] = (
+            r.stream[:, here].astype(F32) + dot(r.mixed[...], wout, NT)
+        ).astype(r.new.dtype)
 
     weave(len(queue))
     if mode != "given":
@@ -866,12 +906,13 @@
         )
 
     wout_copy(0).start()
+    win_copy(tiles, 0).start()
     for copy in gate_copies(0):
         copy.start()
     load_small(at, r.sw, r.vec_s, r.dtw_s)
     gain = gain_row(at, channels, r.vec_s)
     r.low_s[...] = r.sgrad[...].astype(BF16)
-    stream = r.stream[...]
+    stream = r.stream[...].astype(F32)
     scale = lax.rsqrt(jnp.mean(stream * stream, axis=1, keepdims=True) + EPS)
     r.normed_s[...] = (stream * scale * gain).astype(BF16)
     small_low = r.sp[...].astype(BF16)
@@ -887,12 +928,12 @@
         pl.semaphore_wait(barrier, count + 1)
         pieces, buffers = [], []
 
-        def add_piece(whole, out, cuts, held):
+        def add_piece(whole, out, cuts, held, side=None):
             start = len(pieces)
             total = whole.shape[4]
             for k, first_y in enumerate(cuts):
                 piece = total // len(cuts)
-                pieces.append((whole, out, k * piece, piece, first_y))
+                pieces.append((whole, out, k * piece, piece, first_y, side))
                 buffers.append(held[k])
             return list(range(start, len(pieces)))
 
@@ -910,14 +951,15 @@
         )
         out_items = add_piece(r.gout, r.sum_out, (1, 0), held_out)
         if mode == "first":
-            in_items = add_piece(r.next_gin, r.sum_next_in, (1, 0), held_in)
+            in_items = add_piece(r.next_gin, r.sum_next_in, (1, 0, 1, 0), held_in)
             in_items += add_piece(r.next_gsmall, r.sum_next_small, (1,), held_small)
-            own_items = add_piece(r.gin, r.sum_in, (1, 0), held_in)
-            own_items += add_piece(r.gsmall_hbm, r.sum_small, (0,), held_small)
+            own_items = add_piece(r.gin, r.sum_in, (1, 0, 1, 0), held_in)
+            own_items += add_piece(r.gsmall_hbm, r.sum_small, (1,), held_small)
         reduce = Reduce(depth, pieces, buffers, r.own_sem, r.send_sem, r.recv_sem)
         for item in in_items:
             reduce.begin(item)
 
+    r.lowt_s[...] = r.sgrad[...].astype(F32).T.astype(BF16)
     out_shape = r.stage_out.shape[1:]
     out_rows = out_shape[0] * out_shape[1] * out_shape[2]
     line = r.gout.shape[2]
@@ -939,7 +981,7 @@
         def _(i):
             here = lanes(i, GROUP)
             r.stage_out[slot, :, :, :, here] = (
-                dot(r.low_s[:, pl.ds(k * out_rows, out_rows)], r.mixed[:, here], TN)
+                dot(r.lowt_s[pl.ds(k * out_rows, out_rows), :], r.mixed[:, here])
                 .astype(BF16)
                 .reshape(out_shape[:-1] + (GROUP,))
             )
@@ -953,8 +995,7 @@
         for item in out_items:
             reduce.begin(item)
         queue.extend(reduce.turns(in_items + out_items))
-    pace = -(-len(queue) // (24 if mode == "first" else 16))
-    weave(pace)
+    pace = -(-len(queue) // (24 if mode == "first" else 26))
 
     @pl.loop(0, tiles)
     def _(i):
@@ -990,6 +1031,47 @@
         (r.sum_send, r.sum_recv, r.end_send, r.end_recv),
     )
     each(0, me, lambda j: sums(j, me).start())
+    weave(pace)
+    in_shape = r.stage_in.shape[1:]
+
+    def in_copy(i, slot):
+        return pltpu.make_async_copy(
+            r.stage_in.at[slot], block_of(r.gin, i), r.in_sem.at[slot]
+        )
+
+    def project(i, turn):
+        here = lanes(i, GROUP)
+        slot = lax.rem(turn, 2)
+        copy = in_copy(i, slot)
+        following = lax.rem(i + 1, 2 * tiles)
+
+        @pl.when(turn + 1 < 2 * tiles)
+        def _():
+            win_copy(following, 1 - slot).start()
+
+        @pl.when(turn >= 2)
+        def _():
+            copy.wait()
+
+        r.stage_in[slot] = (
+            dot(r.pb_s[:, here], r.normed_s[...], TN).astype(BF16).reshape(in_shape)
+        )
+        copy.start()
+        win_copy(i, slot).wait()
+        part = dot(r.pb_s[:, here], r.win_s[slot].reshape(GROUP, width))
+
+        @pl.when(turn == 0)
+        def _():
+            r.nsg[...] = part
+
+        @pl.when(turn > 0)
+        def _():
+            r.nsg[...] += part
+
+    @pl.loop(0, tiles)
+    def _(i):
+        project(i + tiles, i)
+
     weave(pace)
     for n in range(states):
         first = rank + states + n
@@ -1092,8 +1174,6 @@
                 weave(pace)
         gvec[pl.ds(0, states), here] = both[1]
 
-    win_copy(tiles, 0).start()
-
     @pl.loop(0, tiles)
     def _(i):
         here = lanes(i, GROUP)
@@ -1149,45 +1229,6 @@
         edge().start()
 
     weave(pace)
-    in_shape = r.stage_in.shape[1:]
-
-    def project(i, turn):
-        here = lanes(i, GROUP)
-        slot = lax.rem(turn, 2)
-        copy = pltpu.make_async_copy(
-            r.stage_in.at[slot], block_of(r.gin, i), r.in_sem.at[slot]
-        )
-        following = lax.rem(i + 1, 2 * tiles)
-
-        @pl.when(turn + 1 < 2 * tiles)
-        def _():
-            win_copy(following, 1 - slot).start()
-
-        @pl.when(turn >= 2)
-        def _():
-            copy.wait()
-
-        r.stage_in[slot] = (
-            dot(r.pb_s[:, here], r.normed_s[...], TN).astype(BF16).reshape(in_shape)
-        )
-        copy.start()
-        win_copy(i, slot).wait()
-        part = dot(r.pb_s[:, here], r.win_s[slot].reshape(GROUP, width))
-
-        @pl.when(turn == 0)
-        def _():
-            r.nsg[...] = part
-
-        @pl.when(turn > 0)
-        def _():
-            r.nsg[...] += part
-
-    @pl.loop(0, tiles)
-    def _(i):
-        project(i + tiles, i)
-
-    weave(pace)
-
     @pl.when(me < count - 1)
     def _():
         edge().wait_recv()
@@ -1215,7 +1256,7 @@
         r.pb_s[:, here] = total.astype(BF16)
         project(i, i + tiles)
 
-    stream = r.stream[...]
+    stream = r.stream[...].astype(F32)
     scale = lax.rsqrt(jnp.mean(stream * stream, axis=1, keepdims=True) + EPS)
     normed_grad = r.nsg[...]
     gain_grad = jnp.sum(normed_grad * stream * scale, axis=0, keepdims=True)
@@ -1237,12 +1278,10 @@
     scaled = normed_grad * gain
     inner_sum = jnp.mean(scaled * stream, axis=1, keepdims=True)
     r.nsg[...] = (
-        r.sgrad[...] + scale * scaled - stream * (scale * scale * scale) * inner_sum
+        r.sgrad[...].astype(F32) + scale * scaled - stream * (scale * scale * scale) * inner_sum
     )
     for slot in range(2):
-        pltpu.make_async_copy(
-            r.stage_in.at[slot], block_of(r.gin, 0), r.in_sem.at[slot]
-        ).wait()
+        in_copy(0, slot).wait()
     weave(len(queue))
     if mode == "first":
         small_copy.wait()
@@ -1282,7 +1321,7 @@
     for name, array in operands:
         inputs.append((name, array, vmem if name == "sw" else any_space))
     outputs = [
-        ("new", shape(stream.shape, F32), vmem),
+        ("new", shape(stream.shape, BF16 if mode == "later" else F32), vmem),
         ("pad", shape((rows + HALO, inner), BF16), vmem),
         ("gate", shape((rows, inner), F32), vmem),
         ("act", shape((rows, inner), BF16), vmem),
@@ -1393,6 +1432,7 @@
         ("hb", pltpu.VMEM((2, (rows // 2 + 1) * states, GROUP), BF16)),
         ("normed_s", pltpu.VMEM((rows, width), BF16)),
         ("low_s", pltpu.VMEM((rows, width), BF16)),
+        ("lowt_s", pltpu.VMEM((width, rows), BF16)),
         ("sg_s", pltpu.VMEM((rows, inner), F32)),
         ("dt_s", pltpu.VMEM((rows, inner), F32)),
         ("dx_s", pltpu.VMEM((rows + HALO, inner), F32)),
@@ -1431,7 +1471,7 @@
         outputs.append(("gsmall", shape((at.rows, inner), F32), vmem))
     else:
         outputs.append(("sum_out", shape((out_rows, inner), F32), vmem))
-        held = [("rout", out_rows // 2, inner, 2)]
+        held = [("rout", out_rows // 2, inner, 2, False)]
         pieces = 2
         if mode == "last":
             small_shape = (inner // channels, small_rows, 128)
@@ -1446,14 +1486,15 @@
                 outputs.append((name, shape((in_rows, width), F32), vmem))
             for name in ("sum_small", "sum_next_small"):
                 outputs.append((name, shape((small_rows, 128), F32), vmem))
-            held.append(("rin", in_rows // 2, width, 2))
-            held.append(("rsmall", small_rows, 128, 1))
+            held.append(("rin", in_rows // 4, width, 4, False))
+            held.append(("rsmall", small_rows, 128, 1, False))
             scratch.append(("small_sem", dma((1,))))
             scratch.append(("ready_sem", pltpu.SemaphoreType.REGULAR))
-            pieces = 8
-        for name, piece, wide_by, cuts in held:
+            pieces = 12
+        for name, piece, wide_by, cuts, sided in held:
             for k in range(cuts):
-                for part, buffer in enumerate(Reduce.buffers_of(depth, piece, wide_by)):
+                found = Reduce.buffers_of(depth, piece, wide_by, sided)
+                for part, buffer in enumerate(found):
                     scratch.append((f"{name}{k}_{part}", buffer))
         scratch += [
             ("own_sem", dma((pieces, 2))),
@@ -1513,46 +1554,34 @@
         and at.rows * channels // 128 % 16 == 0
     )
 
-    def pack(layer):
-        by_row = jnp.concatenate(
-            [
-                x_weight[layer].T,
-                dt_weight[layer],
-                a_log[layer].T,
-                conv_weight[layer],
-                conv_bias[layer][None],
-                dt_bias[layer][None],
-                skip_gain[layer][None],
-                jnp.pad(norm_gain[layer], (0, channels - gains))[None],
-            ],
-            0,
-        )
-        by_row = jnp.pad(by_row, ((0, at.rows - at.count), (0, 0)))
-        if by_kernel:
-            folds = by_row.reshape(128 // channels, -1, channels)
-            by_row = jnp.concatenate(list(folds), 1)
-        return by_row
-
-    local = [
-        (in_weight[layer].T, out_weight[layer].T, pack(layer))
-        for layer in range(layers)
-    ]
-    stream = hidden_in.astype(F32)
+    gain_rows = jnp.pad(norm_gain, ((0, 0), (0, channels - gains)))
+    packed = jnp.concatenate(
+        [
+            x_weight.transpose(0, 2, 1),
+            dt_weight,
+            a_log.transpose(0, 2, 1),
+            conv_weight,
+            jnp.stack([conv_bias, dt_bias, skip_gain, gain_rows], 1),
+            jnp.zeros((layers, at.rows - at.count, channels), BF16),
+        ],
+        1,
+    )
+    all_in, all_out = in_weight.transpose(0, 2, 1), out_weight.transpose(0, 2, 1)
+    stream = hidden_in if by_kernel else hidden_in.astype(F32)
     streams, runs, weights = [], [], []
     if by_kernel:
-        (in0, out0, small0), (in1, out1, small1) = local
+        folds = packed.reshape(layers, 128 // channels, -1, channels)
+        all_small = jnp.concatenate([folds[:, k] for k in range(folds.shape[1])], 2)
         operands = [
-            ("own_in", in0),
-            ("own_small", small0),
-            ("own_out", out0),
-            ("next_in", in1),
-            ("next_small", small1),
+            ("all_in", all_in),
+            ("all_small", all_small),
+            ("all_out", all_out),
         ]
         first = forward_call(cfg, "first", stream, operands)
         operands = [
             ("win_hbm", first["win2_all"]),
             ("gsm_hbm", first["gsm2_all"]),
-            ("own_out", out1),
+            ("all_out", all_out),
         ]
         second = forward_call(cfg, "later", first["new"], operands)
         runs = [first, second]
@@ -1563,7 +1592,7 @@
         streams = [stream, first["new"]]
         stream = second["new"]
     else:
-        for w_in, w_out, w_small in local:
+        for w_in, w_out, w_small in zip(all_in, all_out, packed):
             w_in = lax.all_gather(w_in, ("ctx", "seq"), axis=0, tiled=True)
             w_out = lax.all_gather(w_out, ("ctx", "seq"), axis=0, tiled=True)
             sw = lax.all_gather(w_small, ("ctx", "seq"), axis=1, tiled=True)
@@ -1575,7 +1604,7 @@
             weights.append((sw, w_in, w_out))
             streams.append(stream)
             stream = run["new"]
-    stream_grad = cotangent.astype(F32)
+    stream_grad = cotangent
     summed = [None] * layers
     if by_kernel:
         last = backward_call(

time: 484 us -> 466 us (0.963)
  Pallas kernels: 443 us -> 432 us
  other arithmetic: 14 us -> 7.41 us
    pallas_call x2, Pallas kernels: 246 us -> 239 us  [backward_call(): pl.pallas_call(functools.partial(backward_kernel, cfg, mode, names), out_...]
    convert_element_type x3 -> x0, other arithmetic: 5.31 us -> none  [the longest x1 2.13 us: on_device(): stream = hidden_in.astype(F32)]
where the time goes in v4:
time: 466 us; the launch traced here: 458 us
  Pallas kernels  432 us (93%)
  local copies, waits for them, and re-layouts  16.5 us (4%)
  other arithmetic  7.41 us (2%)
    pallas_call x2, Pallas kernels, backward_call(): pl.pallas_call(functools.partial(backward_kernel, cfg, mode, names), out_...  239 us
    pallas_call x2, Pallas kernels, forward_call(): pl.pallas_call(functools.partial(forward_kernel, cfg, mode, names), out_s...  193 us

profile of v4, /device:TPU:0, one launch (start us, length us, event | category | flops | bytes accessed | tf_op | source)
XLA Modules:
  0.0 457.5 jit_solution(717085733512249951)
XLA Ops:
  0.6 0.7 pad_bitcast_fusion
  1.4 0.8 copy.75
  2.2 0.8 copy.76
  3.0 0.8 copy.73
  3.8 0.8 copy.77
  4.6 0.8 copy.74
  5.4 0.8 copy.78
  6.2 0.9 concatenate.6
  7.5 0.7 pad_maximum_fusion.4.refs_2_
  8.3 2.0 copy.72
  10.3 133.7 %forward_first.1 = (f32[256,1024]{1,0:T(8,128)}, bf16[272,2048]{1,0:T(8,128)(2,1)}, f32[256,2048]{1,0:T(8,128)}, bf16[256,2048]{1,0:T(8,128)(2,1)}, f32[256,96]{...) custom-call(bf16[256,1024]{1,0:T(8,128)(2,1)} %refs_1_.1, ...), custom_call_target="tpu_custom_call" | custom-call | tf_op jit(solution)/shard_map/forward_first/pallas_call | solution.py:1382
  144.0 59.5 %forward_later.1 = (bf16[256,1024]{1,0:T(8,128)(2,1)}, bf16[272,2048]{1,0:T(8,128)(2,1)}, f32[256,2048]{1,0:T(8,128)}, bf16[256,2048]{1,0:T(8,128)(2,1)}, f32[25...) custom-call(f32[256,1024]{1,0:T(8,128)} %get-tuple-element.47.refs_0, ...), custom_call_target="tpu_custom_call" | custom-call | tf_op jit(solution)/shard_map/forward_later/pallas_call | solution.py:1382
  203.6 85.8 %backward_last.1 = (f32[256,1024]{1,0:T(8,128)}, bf16[2,2,4,2,128,1024]{5,4,3,2,1,0:T(8,128)(2,1)}, bf16[2,2,4,2,32,2048]{5,4,3,2,1,0:T(8,128)(2,1)}, f32[32,2048]{1,0:T(8,128)}, bf16[32,96,128]{2,1,0:T(8,128)(2,1)}) custom-call(bf16[256,1024]{1,0:T(8,128)(2,1)} %refs_0_.3, f32[256,1024]{1,0:T(8,128)} %get-tuple-element.47.refs_0_.refs_1_, ...), custom_call_target="tpu_custom_call" | custom-call | tf_op jit(solution)/shard_map/backward_last/pallas_call | solution.py:1505
  289.4 153.3 %backward_first.1 = (f32[256,1024]{1,0:T(8,128)}, bf16[2,2,4,2,128,1024]{5,4,3,2,1,0:T(8,128)(2,1)}, bf16[2,2,4,2,32,2048]{5,4,3,2,1,0:T(8,128)(2,1)}, f32[32,20...) custom-call(f32[256,1024]{1,0:T(8,128)} %get-tuple-element.61.refs_0, ...), custom_call_target="tpu_custom_call" | custom-call | tf_op jit(solution)/shard_map/backward_first/pallas_call | solution.py:1505
  442.7 0.9 copy.82
  444.2 1.0 copy.84
  445.4 0.6 pad_maximum_fusion.2
  446.9 0.6 pad_maximum_fusion.5
  448.4 0.7 copy.99
  450.9 1.8 pad_maximum_fusion.1
  452.7 1.3 pad_maximum_fusion
  454.0 1.3 copy.98
  455.3 0.8 copy.104
  456.1 1.0 copy.105
  (43 shorter events, 4.8 us)
Async XLA Ops:
  289.4 161.6 %copy-start.2 = (f32[32,2048]{1,0:T(8,128)S(1)}, f32[32,2048]{1,0:T(8,128)}, u32[]{:S(2)}) copy-start(f32[32,2048]{1,0:T(8,128)} %get-tuple-element.81) | copy-start | bytes 786436
  442.7 12.6 %copy-start.1 = (bf16[256,1024]{1,0:T(8,128)(2,1)S(1)}, bf16[256,1024]{1,0:T(8,128)(2,1)}, u32[]{:S(2)}) copy-start(bf16[256,1024]{1,0:T(8,128)(2,1)} %get-tuple-element.156) | copy-start | bytes 1572868
  444.0 12.1 %copy-start = (f32[256,1024]{1,0:T(8,128)S(1)}, f32[256,1024]{1,0:T(8,128)}, u32[]{:S(2)}) copy-start(f32[256,1024]{1,0:T(8,128)} %get-tuple-element.157) | copy-start | bytes 3145732

commit v5 on v4

--- a/solution.py
+++ b/solution.py
@@ -125,6 +125,30 @@
     ]
     gain = jnp.concatenate(tiles, 1)
     return gain[at.gain % 8 : at.gain % 8 + 1]
+
+
+def pack_small(at, layer, raw, sum_s, packed_s):
+    x_weight, dt_weight, a_log, conv_weight, vectors, norm_gain = raw
+    channels, states, rank = x_weight.shape[1], at.conv, at.vec - at.dt
+
+    def place(count, first):
+        row = lax.broadcasted_iota(jnp.int32, (count, 128), 0)
+        col = lax.broadcasted_iota(jnp.int32, (count, 128), 1)
+        return (col == row + first).astype(F32).astype(BF16)
+
+    beside = place(channels, channels)
+    sum_s[...] = dot(x_weight[layer], place(channels, 0), TN)
+    sum_s[pl.ds(0, rank), :] += dot(dt_weight[layer], beside)
+    sum_s[pl.ds(rank, states), :] += dot(a_log[layer], beside, TN)
+    taps = conv_weight.shape[1]
+    sum_s[pl.ds(rank + states, taps), :] += dot(conv_weight[layer], beside)
+    row = rank + states + taps
+    for ref in vectors:
+        sum_s[pl.ds(row, 1), :] += dot(ref[...], beside)[layer : layer + 1]
+        row += 1
+    gains = dot(norm_gain[...], place(norm_gain.shape[1], channels))
+    sum_s[pl.ds(row, 1), :] += gains[layer : layer + 1]
+    packed_s[layer] = sum_s[...].astype(BF16)
 
 
 def merge_small(channels, blocks, sw_ref):
@@ -578,6 +602,18 @@
         out_copy = pltpu.make_async_copy(r.wout_hbm, r.wout_s, r.load_sem.at[2])
         out_copy.start()
 
+    if mode == "first":
+        raw = (
+            r.x_weight,
+            r.dt_weight,
+            r.a_log,
+            r.conv_weight,
+            (r.conv_bias, r.dt_bias, r.skip_gain),
+            r.norm_gain,
+        )
+        for layer in range(2):
+            pack_small(at, layer, raw, r.pack_s, r.packed_s)
+
     stream = r.stream[...].astype(F32)
     scale = lax.rsqrt(jnp.mean(stream * stream, axis=1, keepdims=True) + EPS)
     stores = []
@@ -603,13 +639,13 @@
         first_items, next_items = [], []
         if mode == "first":
             first_items = add_piece(r.all_in.at[0], r.win_s, (1, 0))
-            first_items += add_piece(r.all_small.at[0], r.gsm_s, (1,))
+            first_items += add_piece(r.packed_s.at[0], r.gsm_s, (1,))
         out_items = add_piece(
             r.all_out.at[0 if mode == "first" else 1], r.wout_s, (1, 0)
         )
         if mode == "first":
             next_items = add_piece(r.all_in.at[1], r.win2_all, (1, 0))
-            next_items += add_piece(r.all_small.at[1], r.gsm2_all, (0,))
+            next_items += add_piece(r.packed_s.at[1], r.gsm2_all, (0,))
         gather = Gather(depth, pieces, r.own_sem, r.send_sem, r.recv_sem)
 
         def begin(items):
@@ -731,6 +767,19 @@
         (r.sum_send, r.sum_recv, r.end_send, r.end_recv),
     )
     each(me + 1, count, lambda j: sums(j, me).start())
+    saves = []
+
+    def save(name, slot, part=slice(None)):
+        copy = pltpu.make_async_copy(
+            getattr(r, name).at[:, part],
+            getattr(r, name + "_hbm").at[:, part],
+            r.save_sem.at[slot],
+        )
+        copy.start()
+        saves.append(copy)
+
+    for slot, name in enumerate(("pad", "gate", "act", "pre")):
+        save(name, slot)
     weave(pace)
     for n in range(states):
         r.bb_s[:, n, :] = jnp.broadcast_to(
@@ -812,6 +861,8 @@
         gate = r.gate[:, here]
         r.y[:, here] = y_value
         r.mixed[:, here] = (y_value * gate * sigmoid(gate)).astype(BF16)
+        save("y", 4 + 2 * g, here)
+        save("mixed", 5 + 2 * g, here)
 
     if mode == "given":
         out_copy.wait()
@@ -838,7 +889,7 @@
     for g in range(groups):
         each(me + 1, count, lambda j: ends(g, j, me).wait_send())
         h_copy(g).wait()
-    for copy in stores:
+    for copy in stores + saves:
         copy.wait()
 
 
@@ -905,6 +956,14 @@
             r.h_sem.at[k % 2],
         )
 
+    fetches = {
+        name: pltpu.make_async_copy(
+            getattr(r, name + "_hbm"), getattr(r, name), r.fetch_sem.at[k]
+        )
+        for k, name in enumerate(("stream", "pre", "act", "pad"))
+    }
+    for copy in fetches.values():
+        copy.start()
     wout_copy(0).start()
     win_copy(tiles, 0).start()
     for copy in gate_copies(0):
@@ -912,9 +971,6 @@
     load_small(at, r.sw, r.vec_s, r.dtw_s)
     gain = gain_row(at, channels, r.vec_s)
     r.low_s[...] = r.sgrad[...].astype(BF16)
-    stream = r.stream[...].astype(F32)
-    scale = lax.rsqrt(jnp.mean(stream * stream, axis=1, keepdims=True) + EPS)
-    r.normed_s[...] = (stream * scale * gain).astype(BF16)
     small_low = r.sp[...].astype(BF16)
 
     in_items, out_items, own_items = [], [], []
@@ -996,6 +1052,13 @@
             reduce.begin(item)
         queue.extend(reduce.turns(in_items + out_items))
     pace = -(-len(queue) // (24 if mode == "first" else 26))
+
+    fetches["stream"].wait()
+    stream = r.stream[...].astype(F32)
+    scale = lax.rsqrt(jnp.mean(stream * stream, axis=1, keepdims=True) + EPS)
+    r.normed_s[...] = (stream * scale * gain).astype(BF16)
+    fetches["pre"].wait()
+    fetches["act"].wait()
 
     @pl.loop(0, tiles)
     def _(i):
@@ -1173,6 +1236,8 @@
                 both = lax.fori_loop(low, high, second_pass, both)
                 weave(pace)
         gvec[pl.ds(0, states), here] = both[1]
+
+    fetches["pad"].wait()
 
     @pl.loop(0, tiles)
     def _(i):
@@ -1319,18 +1384,23 @@
     vmem, any_space = in_vmem(1)[0], in_any(1)[0]
     inputs = [("stream", stream, vmem)]
     for name, array in operands:
-        inputs.append((name, array, vmem if name == "sw" else any_space))
+        large = name.startswith(("all_", "win_", "wout_", "gsm_"))
+        inputs.append((name, array, any_space if large else vmem))
     outputs = [
         ("new", shape(stream.shape, BF16 if mode == "later" else F32), vmem),
-        ("pad", shape((rows + HALO, inner), BF16), vmem),
-        ("gate", shape((rows, inner), F32), vmem),
-        ("act", shape((rows, inner), BF16), vmem),
         ("sp", shape((rows, at.small), F32), vmem),
-        ("pre", shape((rows, inner), F32), vmem),
         ("h_hbm", shape(((rows + 1) * states, inner), BF16), any_space),
-        ("y", shape((rows, inner), F32), vmem),
-        ("mixed", shape((rows, inner), BF16), vmem),
     ]
+    saved = {
+        "pad": ((rows + HALO, inner), BF16),
+        "gate": ((rows, inner), F32),
+        "act": ((rows, inner), BF16),
+        "pre": ((rows, inner), F32),
+        "y": ((rows, inner), F32),
+        "mixed": ((rows, inner), BF16),
+    }
+    for name, (size, kind) in saved.items():
+        outputs.append((name + "_hbm", shape(size, kind), any_space))
     if mode == "given":
         given = dict(operands)
         in_shape, out_shape = given["win_hbm"].shape, given["wout_hbm"].shape
@@ -1368,11 +1438,16 @@
         ("end_recv", dma((groups, count))),
         ("h_sem", dma((groups,))),
         ("load_sem", dma((3,))),
+        ("save_sem", dma((4 + 2 * groups,))),
     ]
+    for name, (size, kind) in saved.items():
+        scratch.append((name, pltpu.VMEM(size, kind)))
     if mode != "given":
         pieces = 8 if mode == "first" else 2
         scratch += [
             ("gsm_s", pltpu.VMEM(small_shape, BF16)),
+            ("pack_s", pltpu.VMEM(small_shape[1:], F32)),
+            ("packed_s", pltpu.VMEM((2,) + small_shape[1:], BF16)),
             ("own_sem", dma((pieces,))),
             ("send_sem", dma((pieces, Gather.sends(count // 2)))),
             ("recv_sem", dma((pieces, devices))),
@@ -1392,7 +1467,10 @@
         ),
         name="forward_" + mode,
     )(*[entry[1] for entry in inputs])
-    return {entry[0]: result for entry, result in zip(outputs, results)}
+    return {
+        entry[0].removesuffix("_hbm"): result
+        for entry, result in zip(outputs, results)
+    }
 
 
 def backward_call(cfg, mode, sgrad, stream, weights, saved, later):
@@ -1411,15 +1489,19 @@
     small_rows = at.rows * channels // 128
     inputs = [
         ("sgrad", sgrad, vmem),
-        ("stream", stream, vmem),
         ("sw", sw, vmem),
         ("win", win, any_space),
         ("wout", wout, any_space),
     ]
-    for name in ("pad", "act", "sp", "pre", "mixed"):
+    for name in ("sp", "mixed"):
         inputs.append((name, saved[name], vmem))
-    for name in ("gate", "y", "h_hbm"):
+    for name in ("gate", "y"):
         inputs.append((name, saved[name], any_space))
+    inputs.append(("h_hbm", saved["h"], any_space))
+    fetched = {name: saved[name] for name in ("pre", "act", "pad")}
+    fetched["stream"] = stream
+    for name, array in fetched.items():
+        inputs.append((name + "_hbm", array, any_space))
     outputs = [
         ("nsg", shape((rows, width), F32), vmem),
         ("gin", shape(lead + (in_rows, width), BF16), any_space),
@@ -1466,7 +1548,10 @@
         ("win_sem", dma((2,))),
         ("wout_sem", dma((2,))),
         ("gate_sem", dma((2, 2))),
+        ("fetch_sem", dma((len(fetched),))),
     ]
+    for name, array in fetched.items():
+        scratch.append((name, pltpu.VMEM(array.shape, array.dtype)))
     if mode == "given":
         outputs.append(("gsmall", shape((at.rows, inner), F32), vmem))
     else:
@@ -1550,31 +1635,24 @@
         and layers == 2
         and in_weight.shape[2] % 32 == 0
         and out_weight.shape[2] % 32 == 0
-        and 128 % channels == 0
-        and at.rows * channels // 128 % 16 == 0
+        and channels == 64
+        and at.rows == 2 * at.small
     )
 
-    gain_rows = jnp.pad(norm_gain, ((0, 0), (0, channels - gains)))
-    packed = jnp.concatenate(
-        [
-            x_weight.transpose(0, 2, 1),
-            dt_weight,
-            a_log.transpose(0, 2, 1),
-            conv_weight,
-            jnp.stack([conv_bias, dt_bias, skip_gain, gain_rows], 1),
-            jnp.zeros((layers, at.rows - at.count, channels), BF16),
-        ],
-        1,
-    )
     all_in, all_out = in_weight.transpose(0, 2, 1), out_weight.transpose(0, 2, 1)
     stream = hidden_in if by_kernel else hidden_in.astype(F32)
     streams, runs, weights = [], [], []
     if by_kernel:
-        folds = packed.reshape(layers, 128 // channels, -1, channels)
-        all_small = jnp.concatenate([folds[:, k] for k in range(folds.shape[1])], 2)
         operands = [
             ("all_in", all_in),
-            ("all_small", all_small),
+            ("x_weight", x_weight),
+            ("dt_weight", dt_weight),
+            ("a_log", a_log),
+            ("conv_weight", conv_weight),
+            ("conv_bias", conv_bias),
+            ("dt_bias", dt_bias),
+            ("skip_gain", skip_gain),
+            ("norm_gain", norm_gain),
             ("all_out", all_out),
         ]
         first = forward_call(cfg, "first", stream, operands)
@@ -1592,6 +1670,18 @@
         streams = [stream, first["new"]]
         stream = second["new"]
     else:
+        gain_rows = jnp.pad(norm_gain, ((0, 0), (0, channels - gains)))
+        packed = jnp.concatenate(
+            [
+                x_weight.transpose(0, 2, 1),
+                dt_weight,
+                a_log.transpose(0, 2, 1),
+                conv_weight,
+                jnp.stack([conv_bias, dt_bias, skip_gain, gain_rows], 1),
+                jnp.zeros((layers, at.rows - at.count, channels), BF16),
+            ],
+            1,
+        )
         for w_in, w_out, w_small in zip(all_in, all_out, packed):
             w_in = lax.all_gather(w_in, ("ctx", "seq"), axis=0, tiled=True)
             w_out = lax.all_gather(w_out, ("ctx", "seq"), axis=0, tiled=True)

time: 466 us -> 452 us (0.970)
  Pallas kernels: 432 us -> 424 us
  local copies, waits for them, and re-layouts: 16.5 us -> 11.1 us
    pallas_call x2, Pallas kernels: 193 us -> 187 us  [forward_call(): pl.pallas_call(functools.partial(forward_kernel, cfg, mode, names), out_s...]
where the time goes in v5:
time: 452 us; the launch traced here: 443 us
  Pallas kernels  424 us (94%)
  local copies, waits for them, and re-layouts  11.1 us (2%)
  other arithmetic  6.69 us (1%)
    pallas_call x2, Pallas kernels, backward_call(): pl.pallas_call(functools.partial(backward_kernel, cfg, mode, names), out_...  236 us
    pallas_call x2, Pallas kernels, forward_call(): pl.pallas_call(functools.partial(forward_kernel, cfg, mode, names), out_s...  187 us

profile of v5, /device:TPU:0, one launch (start us, length us, event | category | flops | bytes accessed | tf_op | source)
XLA Modules:
  0.0 442.6 jit_solution(16873122128029411899)
XLA Ops:
  0.6 1.4 copy.51.refs_4_
  2.0 2.0 copy.50
  4.1 130.9 %forward_first.1 = (f32[256,1024]{1,0:T(8,128)}, f32[256,96]{1,0:T(8,128)}, bf16[4112,2048]{1,0:T(8,128)(2,1)}, bf16[272,2048]{1,0:T(8,128)(2,1)}, f32[256,2048]...) custom-call(bf16[256,1024]{1,0:T(8,128)(2,1)} %refs_12_.1, ...), custom_call_target="tpu_custom_call" | custom-call | tf_op jit(solution)/shard_map/forward_first/pallas_call | solution.py:1457
  135.0 56.5 %forward_later.1 = (bf16[256,1024]{1,0:T(8,128)(2,1)}, f32[256,96]{1,0:T(8,128)}, bf16[4112,2048]{1,0:T(8,128)(2,1)}, bf16[272,2048]{1,0:T(8,128)(2,1)}, f32[256...) custom-call(f32[256,1024]{1,0:T(8,128)} %get-tuple-element.47.refs_0, ...), custom_call_target="tpu_custom_call" | custom-call | tf_op jit(solution)/shard_map/forward_later/pallas_call | solution.py:1457
  191.4 84.8 %backward_last.1 = (f32[256,1024]{1,0:T(8,128)}, bf16[2,2,4,2,128,1024]{5,4,3,2,1,0:T(8,128)(2,1)}, bf16[2,2,4,2,32,2048]{5,4,3,2,1,0:T(8,128)(2,1)}, f32[32,2048]{1,0:T(8,128)}, bf16[32,96,128]{2,1,0:T(8,128)(2,1)}) custom-call(bf16[256,1024]{1,0:T(8,128)(2,1)} %refs_0_.3, bf16[192,2048]{1,0:T(8,128)(2,1)} %get-tuple-element.51.refs_1_, ...), custom_call_target="tpu_custom_call" | custom-call | tf_op jit(solution)/shard_map/backward_last/pallas_call | solution.py:1590
  276.2 151.5 %backward_first.1 = (f32[256,1024]{1,0:T(8,128)}, bf16[2,2,4,2,128,1024]{5,4,3,2,1,0:T(8,128)(2,1)}, bf16[2,2,4,2,32,2048]{5,4,3,2,1,0:T(8,128)(2,1)}, f32[32,20...) custom-call(f32[256,1024]{1,0:T(8,128)} %get-tuple-element.61.refs_0, ...), custom_call_target="tpu_custom_call" | custom-call | tf_op jit(solution)/shard_map/backward_first/pallas_call | solution.py:1590
  427.8 0.9 copy.52
  428.8 0.1 reshape.43
  429.3 0.1 copy.58
  429.4 1.0 copy.54
  430.4 0.1 reshape.45
  430.5 0.6 pad_maximum_fusion.2
  431.3 0.6 pad_maximum_fusion.6
  432.0 0.6 pad_maximum_fusion.4
  432.8 0.6 pad_maximum_fusion.5
  433.5 0.7 copy.69
  434.5 0.1 fusion.1
  434.7 0.6 pad_maximum_fusion.9
  435.5 0.6 pad_maximum_fusion.7
  436.1 1.8 pad_maximum_fusion.1
  437.8 1.3 pad_maximum_fusion
  439.1 1.3 copy.68
  440.4 0.8 copy.72
  441.2 1.0 copy.73
  (29 shorter events, 1.5 us)
Async XLA Ops:
  276.2 159.8 %copy-start.2 = (f32[32,2048]{1,0:T(8,128)S(1)}, f32[32,2048]{1,0:T(8,128)}, u32[]{:S(2)}) copy-start(f32[32,2048]{1,0:T(8,128)} %get-tuple-element.81) | copy-start | bytes 786436
  427.8 12.6 %copy-start.1 = (bf16[256,1024]{1,0:T(8,128)(2,1)S(1)}, bf16[256,1024]{1,0:T(8,128)(2,1)}, u32[]{:S(2)}) copy-start(bf16[256,1024]{1,0:T(8,128)(2,1)} %get-tuple-element.154) | copy-start | bytes 1572868
  429.1 12.1 %copy-start = (f32[256,1024]{1,0:T(8,128)S(1)}, f32[256,1024]{1,0:T(8,128)}, u32[]{:S(2)}) copy-start(f32[256,1024]{1,0:T(8,128)} %get-tuple-element.155) | copy-start | bytes 3145732

commit v6 on v5

--- a/solution.py
+++ b/solution.py
@@ -18,6 +18,7 @@
 VMEM_BYTES = 63 * 2**20
 CHUNK = 16
 GROUP = 512
+WIDE = 1024
 HALO = 16
 
 
@@ -570,8 +571,12 @@
 
     queue = collections.deque()
 
+    owed = [0.0]
+
     def weave(times):
-        for _ in range(min(times, len(queue))):
+        owed[0] += times
+        while queue and owed[0] >= 1:
+            owed[0] -= 1
             queue.popleft()()
 
     if mode == "given":
@@ -682,7 +687,7 @@
         if mode == "later":
             small_copy.wait()
         merge_small(channels, r.gsm_s, r.sw)
-    pace = -(-len(queue) // 33)
+    pace = len(queue) / (36 if mode == "first" else 33)
 
     load_small(at, r.sw, r.vec_s, r.dtw_s)
     r.normed_s[...] = (stream * scale * gain_row(at, channels, r.vec_s)).astype(BF16)
@@ -790,7 +795,7 @@
     def advance(t, state, rate2, here):
         return (
             jnp.exp2(r.dt_s[pl.ds(t, 1), here] * rate2) * state
-            + r.dx_s[pl.ds(t, 1), here] * widen(r.bb_s[t], GROUP)
+            + r.dx_s[pl.ds(t, 1), here] * widen(r.bb_s[t], state.shape[1])
         )
 
     for g in range(groups):
@@ -812,12 +817,12 @@
         each(me + 1, count, lambda j: ends(g, j, me).start())
 
     def h_copy(g):
-        here = pl.ds(g * GROUP, GROUP)
+        here = pl.ds(g * WIDE, WIDE)
         return pltpu.make_async_copy(
             r.hs.at[:, here], r.h_hbm.at[:, here], r.h_sem.at[g]
         )
 
-    for g in range(groups):
+    def start_of(g):
         here = pl.ds(g * GROUP, GROUP)
         rate2 = r.vec_s[pl.ds(0, states), here] * LOG2E
 
@@ -830,7 +835,15 @@
                 + r.end_s[j, :, here].astype(F32)
             )
 
-        state = lax.fori_loop(0, me, carry, jnp.zeros((states, GROUP), F32))
+        return lax.fori_loop(0, me, carry, jnp.zeros((states, GROUP), F32))
+
+    for g in range(inner // WIDE):
+        here = pl.ds(g * WIDE, WIDE)
+        rate2 = r.vec_s[pl.ds(0, states), here] * LOG2E
+        each_wide = WIDE // GROUP
+        state = jnp.concatenate(
+            [start_of(g * each_wide + part) for part in range(each_wide)], 1
+        )
         r.hs[pl.ds(0, states), here] = state.astype(BF16)
 
         def second_pass(step, state):
@@ -844,7 +857,7 @@
             )
             return state
 
-        thirds = 1 if mode == "given" else 5
+        thirds = 1 if mode == "given" else 8
         for part in range(thirds):
             state = lax.fori_loop(
                 steps * part // thirds,
@@ -888,6 +901,7 @@
     each(me + 1, count, lambda j: sums(j, me).wait_send())
     for g in range(groups):
         each(me + 1, count, lambda j: ends(g, j, me).wait_send())
+    for g in range(inner // WIDE):
         h_copy(g).wait()
     for copy in stores + saves:
         copy.wait()
@@ -913,8 +927,12 @@
 
     queue = collections.deque()
 
+    owed = [0.0]
+
     def weave(times):
-        for _ in range(min(times, len(queue))):
+        owed[0] += times
+        while queue and owed[0] >= 1:
+            owed[0] -= 1
             queue.popleft()()
 
     each(me + 1, count, lambda j: signal(barrier, (ctx, j)))
@@ -946,12 +964,13 @@
             r.win.at[pl.ds(i * win_rows, win_rows)], r.win_s.at[slot], r.win_sem.at[slot]
         )
 
-    span = rows // 2 * states
+    quarters = 4
+    span = rows // quarters * states
 
     def states_in(k):
-        g, half = k // 2, 1 - k % 2
+        g, quarter = k // quarters, quarters - 1 - k % quarters
         return pltpu.make_async_copy(
-            r.h_hbm.at[pl.ds(half * span, span + states), pl.ds(g * GROUP, GROUP)],
+            r.h_hbm.at[pl.ds(quarter * span, span + states), pl.ds(g * WIDE, WIDE)],
             r.hb.at[k % 2],
             r.h_sem.at[k % 2],
         )
@@ -1007,10 +1026,10 @@
         )
         out_items = add_piece(r.gout, r.sum_out, (1, 0), held_out)
         if mode == "first":
-            in_items = add_piece(r.next_gin, r.sum_next_in, (1, 0, 1, 0), held_in)
-            in_items += add_piece(r.next_gsmall, r.sum_next_small, (1,), held_small)
-            own_items = add_piece(r.gin, r.sum_in, (1, 0, 1, 0), held_in)
-            own_items += add_piece(r.gsmall_hbm, r.sum_small, (1,), held_small)
+            in_items = add_piece(r.next_gin, r.sum_in.at[1], (1, 0, 1, 0), held_in)
+            in_items += add_piece(r.next_gsmall, r.sum_small.at[1], (1,), held_small)
+            own_items = add_piece(r.gin, r.sum_in.at[0], (1, 0, 1, 0), held_in)
+            own_items += add_piece(r.gsmall_hbm, r.sum_small.at[0], (1,), held_small)
         reduce = Reduce(depth, pieces, buffers, r.own_sem, r.send_sem, r.recv_sem)
         for item in in_items:
             reduce.begin(item)
@@ -1051,7 +1070,7 @@
         for item in out_items:
             reduce.begin(item)
         queue.extend(reduce.turns(in_items + out_items))
-    pace = -(-len(queue) // (24 if mode == "first" else 26))
+    pace = len(queue) / (24 if mode == "first" else 26)
 
     fetches["stream"].wait()
     stream = r.stream[...].astype(F32)
@@ -1162,10 +1181,9 @@
         each(0, me, lambda j: ends(g, j, me).start())
         weave(pace)
 
-    for g in range(groups):
+    def begin_of(g):
         here = pl.ds(g * GROUP, GROUP)
-        rate = r.vec_s[pl.ds(0, states), here]
-        rate2 = rate * LOG2E
+        rate2 = r.vec_s[pl.ds(0, states), here] * LOG2E
 
         def carry(k, state):
             j = count - 1 - k
@@ -1177,27 +1195,37 @@
                 + r.end_s[j, :, here].astype(F32)
             )
 
-        begin = lax.fori_loop(
+        return lax.fori_loop(
             0, count - 1 - me, carry, jnp.zeros((states, GROUP), F32)
         )
-        both = (begin, jnp.zeros((states, GROUP), F32))
-        for part in range(2):
-            k = 2 * g + part
-            half = 1 - part
+
+    loads = inner // WIDE * quarters
+    for g in range(inner // WIDE):
+        here = pl.ds(g * WIDE, WIDE)
+        rate = r.vec_s[pl.ds(0, states), here]
+        rate2 = rate * LOG2E
+        each_wide = WIDE // GROUP
+        begin = jnp.concatenate(
+            [begin_of(g * each_wide + part) for part in range(each_wide)], 1
+        )
+        both = (begin, jnp.zeros((states, WIDE), F32))
+        for part in range(quarters):
+            k = quarters * g + part
+            quarter = quarters - 1 - part
             held_states = r.hb.at[k % 2]
-            if k + 1 < 2 * groups:
+            if k + 1 < loads:
                 states_in(k + 1).start()
             states_in(k).wait()
 
             def second_pass(turn, both):
                 state, total = both
                 step = steps - 1 - turn
-                base = pl.multiple_of(step * CHUNK * states - half * span, states)
+                base = pl.multiple_of(step * CHUNK * states - quarter * span, states)
                 for i in reversed(range(CHUNK)):
                     t = step * CHUNK + i
                     dt = r.dt_s[pl.ds(t, 1), here]
                     adjoint = state + r.sg_s[pl.ds(t, 1), here] * widen(
-                        r.cb_s[t], GROUP
+                        r.cb_s[t], WIDE
                     )
                     state = jnp.exp2(dt * rate2) * adjoint
                     held = held_states[pl.ds(base + i * states, states), :]
@@ -1230,9 +1258,9 @@
                 )
                 return state, total
 
-            for quarter in range(2):
-                low = (2 * part + quarter) * steps // 4
-                high = (2 * part + quarter + 1) * steps // 4
+            for k in range(2):
+                low = (2 * part + k) * steps // (2 * quarters)
+                high = (2 * part + k + 1) * steps // (2 * quarters)
                 both = lax.fori_loop(low, high, second_pass, both)
                 weave(pace)
         gvec[pl.ds(0, states), here] = both[1]
@@ -1511,7 +1539,7 @@
         ("full_s", pltpu.VMEM((at.rows, inner), F32)),
         ("vec_s", pltpu.VMEM((at.rows - at.vec, inner), F32)),
         ("dtw_s", pltpu.VMEM((at.small, inner), BF16)),
-        ("hb", pltpu.VMEM((2, (rows // 2 + 1) * states, GROUP), BF16)),
+        ("hb", pltpu.VMEM((2, (rows // 4 + 1) * states, WIDE), BF16)),
         ("normed_s", pltpu.VMEM((rows, width), BF16)),
         ("low_s", pltpu.VMEM((rows, width), BF16)),
         ("lowt_s", pltpu.VMEM((width, rows), BF16)),
@@ -1522,8 +1550,8 @@
         ("pb_s", pltpu.VMEM((rows, 2 * inner), BF16)),
         ("cb_s", pltpu.VMEM((rows, states, 128), F32)),
         ("bd_s", pltpu.VMEM((rows, wide), BF16)),
-        ("ab_s", pltpu.VMEM((wide, GROUP), BF16)),
-        ("rb_s", pltpu.VMEM((wide, GROUP), BF16)),
+        ("ab_s", pltpu.VMEM((wide, WIDE), BF16)),
+        ("rb_s", pltpu.VMEM((wide, WIDE), BF16)),
         ("pin_s", pltpu.VMEM((rows, wide), F32)),
         ("pout_s", pltpu.VMEM((rows, wide), F32)),
         ("prelow_s", pltpu.VMEM((rows, inner), BF16)),
@@ -1567,10 +1595,8 @@
             inputs.append(("next_gsmall", small, any_space))
             outputs.append(("gsmall_hbm", shape(small.shape, BF16), any_space))
             scratch.append(("gsmall_s", pltpu.VMEM(small.shape, BF16)))
-            for name in ("sum_in", "sum_next_in"):
-                outputs.append((name, shape((in_rows, width), F32), vmem))
-            for name in ("sum_small", "sum_next_small"):
-                outputs.append((name, shape((small_rows, 128), F32), vmem))
+            outputs.append(("sum_in", shape((2, in_rows, width), F32), vmem))
+            outputs.append(("sum_small", shape((2, small_rows, 128), F32), vmem))
             held.append(("rin", in_rows // 4, width, 4, False))
             held.append(("rsmall", small_rows, 128, 1, False))
             scratch.append(("small_sem", dma((1,))))
@@ -1705,14 +1731,10 @@
         )
         stream_grad = head["nsg"]
 
-        def unfold(small):
-            small = small.reshape(-1, 128 // channels, channels)
-            return small.transpose(1, 0, 2).reshape(at.rows, channels)
-
-        summed = [
-            (head["sum_in"], head["sum_out"], unfold(head["sum_small"])),
-            (head["sum_next_in"], last["sum_out"], unfold(head["sum_next_small"])),
-        ]
+        sum_in = head["sum_in"]
+        sum_out = jnp.stack([head["sum_out"], last["sum_out"]], 0)
+        sum_small = head["sum_small"].reshape(layers, -1, 128 // channels, channels)
+        sum_small = sum_small.transpose(0, 2, 1, 3).reshape(layers, -1, channels)
     else:
         for layer in reversed(range(layers)):
             run = backward_call(
@@ -1738,29 +1760,21 @@
                     (run["gsmall"], 1),
                 )
             ]
-    grads = [None] * layers
-    for layer in range(layers):
-        s_in, s_out, s_small = summed[layer]
-        s_x = s_small[: at.small, :channels]
-        s_dt = s_small[at.dt : at.dt + rank, :channels]
-        s_vec = s_small[at.vec : at.count, :channels]
-        grads[layer] = (
-            s_vec[at.gain, :gains],
-            s_in.T,
-            s_vec[at.conv : at.conv + taps],
-            s_vec[at.conv_b],
-            s_x.T,
-            s_dt,
-            s_vec[at.dt_b],
-            s_vec[:states].T,
-            s_vec[at.skip],
-            s_out.T,
-        )
-    stacked = tuple(
-        jnp.stack([grads[layer][member] for layer in range(layers)], 0)
-        for member in range(10)
+        sum_in, sum_out, sum_small = [jnp.stack(each, 0) for each in zip(*summed)]
+    vectors = sum_small[:, at.vec : at.count]
+    grads = (
+        vectors[:, at.gain, :gains],
+        sum_in.transpose(0, 2, 1),
+        vectors[:, at.conv : at.conv + taps],
+        vectors[:, at.conv_b],
+        sum_small[:, : at.small].transpose(0, 2, 1),
+        sum_small[:, at.dt : at.dt + rank],
+        vectors[:, at.dt_b],
+        vectors[:, :states].transpose(0, 2, 1),
+        vectors[:, at.skip],
+        sum_out.transpose(0, 2, 1),
     )
-    return (stream.astype(BF16), stream_grad) + stacked
+    return (stream.astype(BF16), stream_grad) + grads
 
 
 def solution(mesh):

time: 452 us -> 439 us (0.971)
  Pallas kernels: 424 us -> 416 us
  other arithmetic: 6.69 us -> 1.78 us
    another operation x9 -> x0, other arithmetic: 6.69 us -> none  [on_device(): jnp.stack([grads[layer][member] for layer in range(layers)], 0)]
    pallas_call x2, Pallas kernels: 187 us -> 183 us  [forward_call(): pl.pallas_call(functools.partial(forward_kernel, cfg, mode, names), out_s...]
    unnamed x12 -> x14, local copies, waits for them, and re-layouts: 7.24 us -> 9.83 us
where the time goes in v6:
time: 439 us; the launch traced here: 432 us
  Pallas kernels  416 us (95%)
  local copies, waits for them, and re-layouts  13.5 us (3%)
    pallas_call x2, Pallas kernels, backward_call(): pl.pallas_call(functools.partial(backward_kernel, cfg, mode, names), out_...  233 us
    pallas_call x2, Pallas kernels, forward_call(): pl.pallas_call(functools.partial(forward_kernel, cfg, mode, names), out_s...  183 us
    unnamed x14, local copies, waits for them, and re-layouts  9.83 us

profile of v6, /device:TPU:0, one launch (start us, length us, event | category | flops | bytes accessed | tf_op | source)
XLA Modules:
  0.0 432.0 jit_solution(4001921440909532727)
XLA Ops:
  0.6 1.4 copy.43.refs_4_
  2.0 2.0 copy.42
  4.1 125.6 %forward_first.1 = (f32[256,1024]{1,0:T(8,128)}, f32[256,96]{1,0:T(8,128)}, bf16[4112,2048]{1,0:T(8,128)(2,1)}, bf16[272,2048]{1,0:T(8,128)(2,1)}, f32[256,2048]...) custom-call(bf16[256,1024]{1,0:T(8,128)(2,1)} %refs_12_.1, ...), custom_call_target="tpu_custom_call" | custom-call | tf_op jit(solution)/shard_map/forward_first/pallas_call | solution.py:1485
  129.7 57.0 %forward_later.1 = (bf16[256,1024]{1,0:T(8,128)(2,1)}, f32[256,96]{1,0:T(8,128)}, bf16[4112,2048]{1,0:T(8,128)(2,1)}, bf16[272,2048]{1,0:T(8,128)(2,1)}, f32[256...) custom-call(f32[256,1024]{1,0:T(8,128)} %get-tuple-element.45.refs_0, ...), custom_call_target="tpu_custom_call" | custom-call | tf_op jit(solution)/shard_map/forward_later/pallas_call | solution.py:1485
  186.7 87.3 %backward_last.1 = (f32[256,1024]{1,0:T(8,128)}, bf16[2,2,4,2,128,1024]{5,4,3,2,1,0:T(8,128)(2,1)}, bf16[2,2,4,2,32,2048]{5,4,3,2,1,0:T(8,128)(2,1)}, f32[32,2048]{1,0:T(8,128)}, bf16[32,96,128]{2,1,0:T(8,128)(2,1)}) custom-call(bf16[256,1024]{1,0:T(8,128)(2,1)} %refs_0_.3, bf16[192,2048]{1,0:T(8,128)(2,1)} %get-tuple-element.49.refs_1_, ...), custom_call_target="tpu_custom_call" | custom-call | tf_op jit(solution)/shard_map/backward_last/pallas_call | solution.py:1616
  274.0 0.0 copy-start.2
  274.0 146.0 %backward_first.1 = (f32[256,1024]{1,0:T(8,128)}, bf16[2,2,4,2,128,1024]{5,4,3,2,1,0:T(8,128)(2,1)}, bf16[2,2,4,2,32,2048]{5,4,3,2,1,0:T(8,128)(2,1)}, f32[32,20...) custom-call(f32[256,1024]{1,0:T(8,128)} %get-tuple-element.59.refs_0_, ...), custom_call_target="tpu_custom_call" | custom-call | tf_op jit(solution)/shard_map/backward_first/pallas_call | solution.py:1616
  420.0 1.1 copy.44
  421.1 0.1 copy.45
  421.2 0.1 reshape.35
  421.3 0.7 slice_reduce_fusion.3
  422.0 0.8 slice_reduce_fusion
  422.8 0.1 slice.43
  422.9 0.7 copy.48
  423.6 0.6 slice_bitcast_fusion.1
  424.2 0.1 slice_bitcast_fusion
  424.3 0.1 slice.40
  424.4 0.7 copy.47
  425.1 0.7 copy.49
  425.8 0.0 copy-done.2
  425.8 1.8 maximum_bitcast_fusion
  427.6 2.5 copy.46
  430.1 0.8 copy.52
  430.9 1.0 copy.53
  (4 shorter events, 0.0 us)
Async XLA Ops:
  274.0 151.8 %copy-start.2 = (f32[32,2048]{1,0:T(8,128)S(1)}, f32[32,2048]{1,0:T(8,128)}, u32[]{:S(2)}) copy-start(f32[32,2048]{1,0:T(8,128)} %get-tuple-element.77) | copy-start | bytes 786436
  419.9 10.1 %copy-start.1 = (bf16[256,1024]{1,0:T(8,128)(2,1)S(1)}, bf16[256,1024]{1,0:T(8,128)(2,1)}, u32[]{:S(2)}) copy-start(bf16[256,1024]{1,0:T(8,128)(2,1)} %get-tuple-element.141) | copy-start | bytes 1572868
  420.0 10.9 %copy-start = (f32[256,1024]{1,0:T(8,128)S(1)}, f32[256,1024]{1,0:T(8,128)}, u32[]{:S(2)}) copy-start(f32[256,1024]{1,0:T(8,128)} %get-tuple-element.142) | copy-start | bytes 3145732

commit v7 on v6

--- a/solution.py
+++ b/solution.py
@@ -441,11 +441,12 @@
                 target[here].astype(F32) + other[here].astype(F32)
             ).astype(BF16)
 
-    def begin(self, item):
+    def begin(self, items):
         for step in range(self.depth):
-            self.send(0, item, step)
-            if step < 2:
-                self.local(item, step).start()
+            for item in items:
+                self.send(0, item, step)
+                if step < 2:
+                    self.local(item, step).start()
 
     def settle(self, stage, item, step):
         self.when(
@@ -1031,8 +1032,7 @@
             own_items = add_piece(r.gin, r.sum_in.at[0], (1, 0, 1, 0), held_in)
             own_items += add_piece(r.gsmall_hbm, r.sum_small.at[0], (1,), held_small)
         reduce = Reduce(depth, pieces, buffers, r.own_sem, r.send_sem, r.recv_sem)
-        for item in in_items:
-            reduce.begin(item)
+        reduce.begin(in_items)
 
     r.lowt_s[...] = r.sgrad[...].astype(F32).T.astype(BF16)
     out_shape = r.stage_out.shape[1:]
@@ -1067,8 +1067,7 @@
             r.stage_out.at[slot], block_of(r.gout, 0), r.out_sem.at[slot]
         ).wait()
     if mode != "given":
-        for item in out_items:
-            reduce.begin(item)
+        reduce.begin(out_items)
         queue.extend(reduce.turns(in_items + out_items))
     pace = len(queue) / (24 if mode == "first" else 26)
 
@@ -1382,8 +1381,7 @@
         for partner in square_partners(depth):
             signal(r.ready_sem, partner)
         pl.semaphore_wait(r.ready_sem, len(square_partners(depth)))
-        for item in own_items:
-            reduce.begin(item)
+        reduce.begin(own_items)
         for turn in reduce.turns(own_items):
             turn()
     if mode != "given":

time: 439 us -> 440 us (level)
  no operation moved by 1% of the time
where the time goes in v7:
time: 440 us; the launch traced here: 432 us
  Pallas kernels  416 us (95%)
  local copies, waits for them, and re-layouts  13.5 us (3%)
    pallas_call x2, Pallas kernels, backward_call(): pl.pallas_call(functools.partial(backward_kernel, cfg, mode, names), out_...  234 us
    pallas_call x2, Pallas kernels, forward_call(): pl.pallas_call(functools.partial(forward_kernel, cfg, mode, names), out_s...  183 us
    unnamed x14, local copies, waits for them, and re-layouts  9.83 us

profile of v7, /device:TPU:0, one launch (start us, length us, event | category | flops | bytes accessed | tf_op | source)
XLA Modules:
  0.0 432.4 jit_solution(10900890608418947205)
XLA Ops:
  0.6 1.4 copy.43.refs_4_
  2.0 2.0 copy.42
  4.1 125.6 %forward_first.1 = (f32[256,1024]{1,0:T(8,128)}, f32[256,96]{1,0:T(8,128)}, bf16[4112,2048]{1,0:T(8,128)(2,1)}, bf16[272,2048]{1,0:T(8,128)(2,1)}, f32[256,2048]...) custom-call(bf16[256,1024]{1,0:T(8,128)(2,1)} %refs_12_.1, ...), custom_call_target="tpu_custom_call" | custom-call | tf_op jit(solution)/shard_map/forward_first/pallas_call | solution.py:1483
  129.7 57.0 %forward_later.1 = (bf16[256,1024]{1,0:T(8,128)(2,1)}, f32[256,96]{1,0:T(8,128)}, bf16[4112,2048]{1,0:T(8,128)(2,1)}, bf16[272,2048]{1,0:T(8,128)(2,1)}, f32[256...) custom-call(f32[256,1024]{1,0:T(8,128)} %get-tuple-element.45.refs_0, ...), custom_call_target="tpu_custom_call" | custom-call | tf_op jit(solution)/shard_map/forward_later/pallas_call | solution.py:1483
  186.7 87.3 %backward_last.1 = (f32[256,1024]{1,0:T(8,128)}, bf16[2,2,4,2,128,1024]{5,4,3,2,1,0:T(8,128)(2,1)}, bf16[2,2,4,2,32,2048]{5,4,3,2,1,0:T(8,128)(2,1)}, f32[32,2048]{1,0:T(8,128)}, bf16[32,96,128]{2,1,0:T(8,128)(2,1)}) custom-call(bf16[256,1024]{1,0:T(8,128)(2,1)} %refs_0_.3, bf16[192,2048]{1,0:T(8,128)(2,1)} %get-tuple-element.49.refs_1_, ...), custom_call_target="tpu_custom_call" | custom-call | tf_op jit(solution)/shard_map/backward_last/pallas_call | solution.py:1614
  274.0 0.0 copy-start.2
  274.0 146.3 %backward_first.1 = (f32[256,1024]{1,0:T(8,128)}, bf16[2,2,4,2,128,1024]{5,4,3,2,1,0:T(8,128)(2,1)}, bf16[2,2,4,2,32,2048]{5,4,3,2,1,0:T(8,128)(2,1)}, f32[32,20...) custom-call(f32[256,1024]{1,0:T(8,128)} %get-tuple-element.59.refs_0_, ...), custom_call_target="tpu_custom_call" | custom-call | tf_op jit(solution)/shard_map/backward_first/pallas_call | solution.py:1614
  420.3 1.1 copy.44
  421.4 0.1 copy.45
  421.5 0.1 reshape.35
  421.6 0.7 slice_reduce_fusion.3
  422.4 0.8 slice_reduce_fusion
  423.1 0.1 slice.43
  423.2 0.7 copy.48
  423.9 0.6 slice_bitcast_fusion.1
  424.6 0.1 slice_bitcast_fusion
  424.6 0.1 slice.40
  424.7 0.7 copy.47
  425.4 0.7 copy.49
  426.1 0.0 copy-done.2
  426.1 1.8 maximum_bitcast_fusion
  427.9 2.5 copy.46
  430.4 0.8 copy.52
  431.2 1.0 copy.53
  (4 shorter events, 0.0 us)
Async XLA Ops:
  274.0 152.1 %copy-start.2 = (f32[32,2048]{1,0:T(8,128)S(1)}, f32[32,2048]{1,0:T(8,128)}, u32[]{:S(2)}) copy-start(f32[32,2048]{1,0:T(8,128)} %get-tuple-element.77) | copy-start | bytes 786436
  420.3 10.1 %copy-start.1 = (bf16[256,1024]{1,0:T(8,128)(2,1)S(1)}, bf16[256,1024]{1,0:T(8,128)(2,1)}, u32[]{:S(2)}) copy-start(bf16[256,1024]{1,0:T(8,128)(2,1)} %get-tuple-element.141) | copy-start | bytes 1572868
  420.3 10.9 %copy-start = (f32[256,1024]{1,0:T(8,128)S(1)}, f32[256,1024]{1,0:T(8,128)}, u32[]{:S(2)}) copy-start(f32[256,1024]{1,0:T(8,128)} %get-tuple-element.142) | copy-start | bytes 3145732
